TPU v7x, 32 devices: a whole 2x2x4 slice. The times are simulated.
32 devices in a mesh: user: 16 (over z, x, core), tensor: 2 (over y).
Axes of the slice: x: 2, y: 2, z: 4, core: 2. Of those that a mesh axis runs over, the one named last changes fastest.
Arguments:
- events: bfloat16 [256, 128, 1024], P('user', None, 'tensor'), may hold values from -6 to 6
- cotangent: bfloat16 [256, 128, 1024], P('user', None, 'tensor'), may hold values from -6 to 6
- w_in: bfloat16 [1024, 4096], P('user', 'tensor'), may hold values from -0.1875 to 0.1875
- w_out: bfloat16 [1024, 1024], P('user', 'tensor'), may hold values from -0.1875 to 0.1875
- slot_source: int32 [256], P('user'), may hold values from 0 to 15, as said below
- slot_length: int32 [256], P('user'), may hold values from 1 to 127, as said below
Outputs:
- grad_x: bfloat16 [256, 128, 1024], P('user', None, 'tensor')
- grad_w_in: float32 [1024, 4096], P('user', 'tensor')
- grad_w_out: float32 [1024, 1024], P('user', 'tensor')
Inputs may be any that keep to these rules, and one draw needn't show every extreme that they name: `slot_source`: the 16 slots of one host name distinct user shards, and for each slot j the entries h * 16 + j over all hosts h name every user shard once, so every history is placed exactly once. `slot_length`: the 16 slot lengths of one host sum to 1024.
All inputs are finite; a program needn't handle non-finite values.
Results may differ from a plain program's by a relative error of at most 0.023.
Values may be sent and summed in bfloat16 or wider, within the bound.
No kernel may reach another device: no remote copies, remote signals or barrier semaphores. Data moves between devices by JAX's collectives and lax.ppermute only.
A program may use at most 128 MiB of HBM per device.

v0:
```python
import functools

import jax
import jax.numpy as jnp
from jax import lax
from jax.experimental import pallas as pl
from jax.experimental.pallas import tpu as pltpu
from jax.sharding import PartitionSpec as P

HEAD_DIM = 128
SEQ_LEN = 128
GROUPS = ((0, 2), (2, 1), (3, 1))

eps = 1e-05
f32 = jnp.float32
bf16 = jnp.bfloat16


def dot_nn(a, b):
    return lax.dot_general(a, b, (((1,), (0,)), ((), ())), preferred_element_type=f32)


def dot_nt(a, b):
    return lax.dot_general(a, b, (((1,), (1,)), ((), ())), preferred_element_type=f32)


def dot_tn(a, b):
    return lax.dot_general(a, b, (((0,), (0,)), ((), ())), preferred_element_type=f32)


def row_mean(t):
    return jnp.mean(t, axis=1, keepdims=True)


def gates(t):
    sig = 0.5 * jnp.tanh(0.5 * t) + 0.5
    silu = t * sig
    return silu, sig + silu * (1.0 - sig)


def attention(pairs, causal, g_s, dh_s, slope_s, hb_s, dz_s):
    scale = HEAD_DIM ** (-0.5)
    spans = [pl.ds(n * SEQ_LEN, SEQ_LEN) for _, n in pairs]
    lanes = [[pl.ds((4 * h + e) * HEAD_DIM, HEAD_DIM) for e in range(4)] for h, _ in pairs]
    heads = [pl.ds(h * HEAD_DIM, HEAD_DIM) for h, _ in pairs]
    every = range(len(pairs))
    weight = causal * (1.0 / SEQ_LEN)

    def part(i, e):
        return g_s[spans[i], lanes[i][e]]

    s = [(dot_nt(part(i, 2), part(i, 3)) * scale).astype(bf16) for i in every]
    pair = [gates(t) for t in s]
    attn = [silu * weight for silu, _ in pair]
    slope = [t * weight for _, t in pair]
    y = [dot_nn(attn[i], part(i, 1)) for i in every]
    cen = [t - row_mean(t) for t in y]
    rstd = [lax.rsqrt(row_mean(t * t) + eps) for t in cen]
    yn = [cen[i] * rstd[i] for i in every]
    uf = [part(i, 0).astype(f32) for i in every]
    dh = [dh_s[spans[i], heads[i]] for i in every]
    dyn = [dh[i] * uf[i] for i in every]
    one = [row_mean(t) for t in dyn]
    two = [row_mean(dyn[i] * yn[i]) for i in every]
    dy = [((dyn[i] - one[i] - yn[i] * two[i]) * rstd[i]).astype(bf16) for i in every]
    grad_a = [dot_nt(dy[i], part(i, 1)) for i in every]
    ds = [(grad_a[i] * scale).astype(bf16) * slope[i] for i in every]

    def store(i, e, grad):
        dz_s[spans[i], lanes[i][e]] = grad.astype(bf16) * slope_s[spans[i], lanes[i][e]]

    for i in every:
        hb_s[spans[i], heads[i]] = (yn[i] * uf[i]).astype(bf16)
        store(i, 0, dh[i] * yn[i])
    for i in every:
        store(i, 1, dot_tn(attn[i], dy[i]))
    for i in every:
        store(i, 2, dot_nn(ds[i], part(i, 3)))
    for i in every:
        store(i, 3, dot_tn(ds[i], part(i, 2)))


def split_order(count):
    rest = sorted(range(1, count), key=lambda j: abs(j - count / 2))
    return rest + [0]


def group_kernel(start, steps, first, last, heads, parts, users, *refs):
    refs = list(refs)
    lens_ref, where_ref, xo_ref, do_ref, far_ref, w_hbm = refs[:6]
    refs = refs[6:]
    acc_hbm = None if first else refs.pop(0)
    refs = refs if first else refs[2:]
    gx_ref, bs_ref = refs[:2]
    refs = refs[2:]
    grads_hbm = [refs.pop(0) for _ in range(2 if last else 1)]
    (w_s, acc_s, nb_s, nt_s, dm_s, dt_s, dz_s, hb_s, g_s, slope_s, dh_s, out_s) = refs[:12]
    load_sems, store_sems = refs[12:]
    rows, own = xo_ref.shape
    width = own * parts
    cols_in = heads * 4 * HEAD_DIM
    histories = rows // SEQ_LEN
    me, user = where_ref[0], where_ref[1]
    step = pl.program_id(0)

    def only(index, run):
        if steps == 1:
            run()
        else:
            pl.when(step == index)(run)

    loads = []
    for p in range(parts):
        source = pl.ds(pl.multiple_of(lax.rem(me + p, parts) * own, own), own)
        loads.append(
            pltpu.make_async_copy(w_hbm.at[source], w_s.at[pl.ds(p * own, own)], load_sems.at[p])
        )
    if not first:
        acc_load = pltpu.make_async_copy(acc_hbm, acc_s, load_sems.at[parts])

    def begin():
        for copy in loads:
            copy.start()
        if first:
            acc_s[...] = jnp.zeros_like(acc_s)
        else:
            acc_load.start()

    def loaded():
        for copy in loads:
            copy.wait()

    only(0, begin)

    causal = lax.broadcasted_iota(jnp.int32, (SEQ_LEN, SEQ_LEN), 0) >= lax.broadcasted_iota(
        jnp.int32, (SEQ_LEN, SEQ_LEN), 1
    )
    causal = causal.astype(f32).astype(bf16)
    position = lax.broadcasted_iota(jnp.int32, (SEQ_LEN, 1), 0)
    half = min(2 * SEQ_LEN, rows)
    halves = [slice(lo, lo + half) for lo in range(0, rows, half)]

    rstds = []
    for here in halves:
        xo = xo_ref[here, :].astype(f32)
        xr = far_ref[here, :].astype(f32)
        mean = (jnp.sum(xo, axis=1, keepdims=True) + jnp.sum(xr, axis=1, keepdims=True)) / width
        xo = xo - mean
        xr = xr - mean
        var = (
            jnp.sum(xo * xo, axis=1, keepdims=True) + jnp.sum(xr * xr, axis=1, keepdims=True)
        ) / width
        rstd = lax.rsqrt(var + eps)
        rstds.append(rstd)
        bo = (xo * rstd).astype(bf16)
        br = (xr * rstd).astype(bf16)
        nb_s[here, :own] = bo
        nb_s[here, own:] = br
        nt_s[:own, here] = bo.T
        nt_s[own:, here] = br.T
    only(0, loaded)
    for h in range(heads):
        c = slice(h * 4 * HEAD_DIM, (h + 1) * 4 * HEAD_DIM)
        z = dot_nn(nb_s[...], w_s[:, c]).astype(bf16)
        g_s[:, c], slope_s[:, c] = gates(z)
    for here in halves:
        base = start * histories + step * histories
        valid = jnp.concatenate(
            [
                (position < lens_ref[base + n]).astype(f32)
                for n in range(here.start // SEQ_LEN, here.stop // SEQ_LEN)
            ],
            axis=0,
        ).astype(bf16)
        there = slice(rows + here.start, rows + here.stop)
        do = do_ref[here, :] * valid
        dr = far_ref[there, :] * valid
        dm_s[here, :own] = do
        dm_s[here, own:] = dr
        dt_s[:own, here] = do.T
        dt_s[own:, here] = dr.T
    dh_s[...] = dot_nn(dm_s[...], w_s[:, cols_in:])

    if not first:
        only(0, acc_load.wait)
    target = out_s if last else acc_s
    size = width // users
    far = users // 4
    zi, xi, ci = user // 4, lax.rem(user // 2, 2), lax.rem(user, 2)
    stores = []

    def ship(lo, wide):
        lanes = pl.ds(lo, wide)
        if not last:
            stores.append(
                pltpu.make_async_copy(
                    acc_s.at[:, lanes], grads_hbm[0].at[:, lanes], store_sems.at[len(stores)]
                )
            )
            only(steps - 1, stores[-1].start)
            return
        keep, send = grads_hbm
        for at, j in enumerate(split_order(far)):
            zd = lax.rem(zi + far - j, far)
            for xs in range(2):
                xd = xi if xs == 0 else 1 - xi
                for cs in range(2):
                    cd = ci if cs == 0 else 1 - ci
                    row = ((zd * 2 + xd) * 2 + cd) * size
                    row = lax.rem(row // own - me + parts, parts) * own + lax.rem(row, own)
                    slot = xs * far + at
                    there = keep if cs == 0 else send
                    stores.append(
                        pltpu.make_async_copy(
                            out_s.at[pl.ds(pl.multiple_of(row, size), size), lanes],
                            there.at[pl.ds(slot * size, size), lanes],
                            store_sems.at[len(stores)],
                        )
                    )
                    only(steps - 1, stores[-1].start)

    def add(lhs, rhs, lo, wide):
        chunk = min(512, width)
        for r in range(0, width, chunk):
            term = dot_nn(lhs[r : r + chunk, :], rhs[...]) + acc_s[r : r + chunk, lo : lo + wide]
            target[r : r + chunk, lo : lo + wide] = term.astype(target.dtype)
        ship(lo, wide)

    block = 4 * HEAD_DIM
    stride = max(1, 8 // histories)
    for lo in range(0, heads, stride):
        hi = min(lo + stride, heads)
        pairs = [(h, n) for h in range(lo, hi) for n in range(histories)]
        attention(pairs, causal, g_s, dh_s, slope_s, hb_s, dz_s)
        for h in range(max(0, lo - stride), lo):
            add(nt_s, dz_s.at[:, h * block : (h + 1) * block], h * block, block)
    dn_all = dot_nt(dz_s[...], w_s[:, :cols_in])
    add(dt_s, hb_s, cols_in, heads * HEAD_DIM)
    for here, rstd in zip(halves, rstds):
        dn = dn_all[here, :]
        nf = nb_s[here, :].astype(f32)
        one = jnp.sum(dn, axis=1, keepdims=True) / width
        two = jnp.sum(dn * nf, axis=1, keepdims=True) / width
        branch = (dn - one - nf * two) * rstd
        gx_ref[here, :] = (dm_s[here, :own].astype(f32) + branch[:, :own]).astype(bf16)
        bs_ref[here, :] = branch[:, own:].astype(bf16)
    for h in range((heads - 1) // stride * stride, heads):
        add(nt_s, dz_s.at[:, h * block : (h + 1) * block], h * block, block)

    for copy in stores:
        only(steps - 1, copy.wait)


def group_call(group, blocks, users, lens, where, x, d, far, weights, past):
    start, steps = group
    first, last = start == 0, start + steps == blocks
    rows, own = x.shape[0] // blocks, x.shape[1]
    width, cols = weights.shape
    parts = width // own
    heads = cols // (5 * HEAD_DIM)
    cols_in = heads * 4 * HEAD_DIM
    smem = pl.BlockSpec(memory_space=pltpu.SMEM)
    anywhere = pl.BlockSpec(memory_space=pl.ANY)
    mine = pl.BlockSpec((rows, own), lambda i: (start + i, 0))
    theirs = pl.BlockSpec((2 * rows, width - own), lambda i: (i, 0))
    args = [lens, where, x, d, far, weights] + past
    specs = [smem, smem, mine, mine, theirs] + [anywhere] * (1 + len(past))
    if last:
        grads = [jax.ShapeDtypeStruct((width // 2, cols), bf16)] * 2
    else:
        grads = [jax.ShapeDtypeStruct((width, cols), f32)]
    flops = steps * (4 * rows * width * cols + 2 * rows * width * cols_in)
    return pl.pallas_call(
        functools.partial(group_kernel, start, steps, first, last, heads, parts, users),
        grid=(steps,),
        out_shape=[
            jax.ShapeDtypeStruct((blocks * rows, own), bf16),
            jax.ShapeDtypeStruct((blocks * rows, width - own), bf16),
        ]
        + grads,
        in_specs=specs,
        out_specs=[
            pl.BlockSpec((rows, own), lambda i: (start + i, 0)),
            pl.BlockSpec((rows, width - own), lambda i: (start + i, 0)),
        ]
        + [anywhere] * len(grads),
        input_output_aliases={} if first else {7: 0, 8: 1},
        scratch_shapes=[
            pltpu.VMEM((width, cols), bf16),
            pltpu.VMEM((width, cols), f32),
            pltpu.VMEM((rows, width), bf16),
            pltpu.VMEM((width, rows), bf16),
            pltpu.VMEM((rows, width), bf16),
            pltpu.VMEM((width, rows), bf16),
            pltpu.VMEM((rows, cols_in), bf16),
            pltpu.VMEM((rows, cols - cols_in), bf16),
            pltpu.VMEM((rows, cols_in), bf16),
            pltpu.VMEM((rows, cols_in), bf16),
            pltpu.VMEM((rows, cols - cols_in), f32),
            pltpu.VMEM((width, cols) if last else (16, 128), bf16),
            pltpu.SemaphoreType.DMA((parts + 1,)),
            pltpu.SemaphoreType.DMA(((users if last else 1) * (heads + 1),)),
        ],
        compiler_params=pltpu.CompilerParams(vmem_limit_bytes=56 * 2**20),
        cost_estimate=pl.CostEstimate(
            flops=flops, bytes_accessed=16 * 2**20, transcendentals=steps * rows * cols
        ),
    )(*args)


def scatter_parts(keep, send, users):
    far = users // 4
    order = split_order(far)
    size = keep.shape[0] // (2 * far)

    def swap(block, bit):
        return lax.ppermute(block, "user", [(i, i ^ bit) for i in range(users)])

    got = swap(send, 1)

    def both(lo, hi):
        span = slice(lo * size, hi * size)
        return keep[span].astype(f32) + got[span].astype(f32)

    cuts = [(0, 1), (1, far - 1), (far - 1, far)]
    across = [swap(both(far + lo, far + hi).astype(bf16), 2) for lo, hi in cuts]
    moved = []
    for (lo, hi), other in zip(cuts[:2], across):
        near = (both(lo, hi) + other.astype(f32)).astype(bf16)
        for at in range(lo, hi):
            pairs = [(i, (i - 4 * order[at]) % users) for i in range(users)]
            block = near[(at - lo) * size : (at - lo + 1) * size]
            moved.append(lax.ppermute(block, "user", pairs))
    return got, [across[2]] + moved


def finish_kernel(cols_in, kept_ref, sent_ref, *refs):
    terms = refs[:-3]
    gx_ref, win_ref, wout_ref = refs[-3:]
    gx_ref[...] = (kept_ref[...].astype(f32) + sent_ref[...].astype(f32)).astype(bf16)

    @pl.when(pl.program_id(0) == 0)
    def _():
        total = terms[0][...].astype(f32)
        for term in terms[1:]:
            total = total + term[...].astype(f32)
        win_ref[...] = total[:, :cols_in]
        wout_ref[...] = total[:, cols_in:]


def finish(kept, sent, keep, got, rest, cols_in):
    rows, own = kept.shape
    size, cols = rest[0].shape
    slot = keep.shape[0] // (2 * size) - 1
    steps = 4
    lines = pl.BlockSpec((rows // steps, own), lambda i: (i, 0))
    specs = [lines] * 2
    specs += [pl.BlockSpec((size, cols), lambda i: (slot, 0))] * 2
    specs += [pl.BlockSpec((size, cols), lambda i: (0, 0))] * len(rest)
    return pl.pallas_call(
        functools.partial(finish_kernel, cols_in),
        grid=(steps,),
        out_shape=[
            jax.ShapeDtypeStruct((rows, own), bf16),
            jax.ShapeDtypeStruct((size, cols_in), f32),
            jax.ShapeDtypeStruct((size, cols - cols_in), f32),
        ],
        in_specs=specs,
        out_specs=[
            lines,
            pl.BlockSpec((size, cols_in), lambda i: (0, 0)),
            pl.BlockSpec((size, cols - cols_in), lambda i: (0, 0)),
        ],
        compiler_params=pltpu.CompilerParams(vmem_limit_bytes=32 * 2**20),
        cost_estimate=pl.CostEstimate(
            flops=rows * own, bytes_accessed=12 * 2**20, transcendentals=0
        ),
    )(kept, sent, keep, got, *rest)


def exchange(block, tensor):
    if tensor == 2:
        return lax.ppermute(block, "tensor", [(0, 1), (1, 0)])
    own = block.shape[1]
    every = lax.all_gather(block, "tensor", axis=1, tiled=True)
    return jnp.roll(every, -lax.axis_index("tensor") * own, axis=1)[:, own:]


def give_back(block, own, tensor):
    if tensor == 2:
        return lax.ppermute(block, "tensor", [(0, 1), (1, 0)])
    every = jnp.concatenate([jnp.zeros((block.shape[0], own), block.dtype), block], axis=1)
    every = jnp.roll(every, lax.axis_index("tensor") * own, axis=1)
    return lax.psum_scatter(every, "tensor", scatter_dimension=1, tiled=True)


def local(events, cotangent, w_in, w_out, slot_source, slot_length):
    tensor = lax.axis_size("tensor")
    users = lax.axis_size("user")
    hist, seq_len, own = events.shape
    x = events.reshape(hist * seq_len, own)
    d = cotangent.reshape(hist * seq_len, own)
    blocks = sum(steps for _, steps in GROUPS)
    rows = hist // blocks * seq_len
    far, ahead = [], None
    for start, steps in GROUPS:
        spans = [slice(i * rows, (i + 1) * rows) for i in range(start, start + steps)]
        if ahead is not None:
            x, d, _ = lax.optimization_barrier((x, d, ahead))
        ahead = jnp.concatenate([t[span] for span in spans for t in (x, d)], axis=0)
        far.append(exchange(ahead, tensor))

    weights = lax.all_gather(
        jnp.concatenate([w_in, w_out], axis=1), "user", axis=0, tiled=True
    )
    table = lax.all_gather(slot_source * 256 + slot_length, "user", axis=0, tiled=True)
    table = table.reshape(users, hist)
    user = lax.axis_index("user")
    lens = jnp.sum(jnp.where(table // 256 == user, table % 256, 0), axis=0)
    where = jnp.stack([lax.axis_index("tensor"), user]).astype(jnp.int32)

    past = []
    for group, theirs in zip(GROUPS, far):
        kept, bs, *grads = group_call(
            group, blocks, users, lens, where, x, d, theirs, weights, past
        )
        past = grads + [kept, bs]
    sent = give_back(bs, own, tensor)
    keep, send = grads
    got, rest = scatter_parts(keep, send, users)
    grad_x, grad_in, grad_out = finish(kept, sent, keep, got, rest, w_in.shape[1])
    return (grad_x.reshape(hist, seq_len, own), grad_in, grad_out)


def solution(mesh):
    in_specs = (
        P("user", None, "tensor"),
        P("user", None, "tensor"),
        P("user", "tensor"),
        P("user", "tensor"),
        P("user"),
        P("user"),
    )
    out_specs = (P("user", None, "tensor"), P("user", "tensor"), P("user", "tensor"))
    return jax.shard_map(local, mesh=mesh, in_specs=in_specs, out_specs=out_specs, check_vma=False)
```

profile of v0, /device:TPU:0, one launch (start us, length us, event | category | flops | bytes accessed | tf_op | source)
XLA Modules:
  0.0 193.9 jit_solution(16748256819597686397)
XLA Ops:
  7.2 0.0 copy-start.3
  7.2 0.0 all-gather.2.cloned.1.call-start
  7.2 1.9 pad_maximum_fusion.3
  9.1 0.0 all-gather.2.cloned.1.call-update
  9.1 1.3 fusion.5
  10.4 0.1 fusion.6
  10.5 0.0 copy-start.2
  10.5 0.0 copy-start.4
  10.5 1.5 pad_maximum_fusion
  12.0 3.0 %collective-permute-start.2 = (bf16[2048,512]{1,0:T(8,128)(2,1)}, bf16[2048,512]{1,0:T(8,128)(2,1)}, u32[]{:S(2)}, u32[]{:S(2)}) collective-permute-start(bf16[2048,512]{1,0:T(8,128)(2,1)} %pad_maximum_fusion), channel_id=1, source_target_pairs={{0,1},{1,0},{2,3},{3,2},{4,5},{5,4},{6,7},{7,6},{8,9},{9,8},{10,11... | collective-permute-start | bytes 6291464 | tf_op jit(solution)/shard_map/ppermute | solution.py:383
  15.1 0.1 pad_maximum_fusion.1
  15.1 0.0 copy-start.7
  15.1 0.0 copy-start.5
  15.2 0.0 copy-start.6
  15.2 1.5 collective-permute-start.1
  16.8 0.1 pad_maximum_fusion.2
  16.8 0.6 collective-permute-start
  17.5 0.6 dynamic-slice
  18.8 0.1 add_dynamic-update-slice_fusion
  18.9 12.3 %all-reduce = s32[256]{0:T(256)S(1)} all-reduce(s32[256]{0:T(256)S(1)} %add_dynamic-update-slice_fusion), channel_id=1, replica_groups=mesh['user'=16,'tensor'=2] {'user'}, use_global_device_ids=true, to_apply=%add | all-reduce | flops 256 | bytes 2048
  31.2 0.1 reshape.22
  31.3 0.6 pad_add_fusion.refs_1_
  31.9 0.5 fusion.2.refs_0_
  32.4 29.3 %collective-permute-done.2.refs_4_ = bf16[2048,512]{1,0:T(8,128)(2,1)} collective-permute-done((bf16[2048,512]{1,0:T(8,128)(2,1)}, bf16[2048,512]{1,0:T(8,128)(2,1)}, u32[]{:S(2)}, u32[]{:S(2)}) %collective-permute-start.2) | collective-permute-done | bytes 2097184 | tf_op jit(solution)/shard_map/ppermute | solution.py:383
  61.7 8.0 %all-gather.2.cloned.1.call-done.refs_5_ = bf16[1024,2560]{1,0:T(8,128)(2,1)} async-done(((bf16[64,2560]{1,0:T(8,128)(2,1)}), bf16[1024,2560]{1,0:T(8,128)(2,1)}) %all-gather.2.cloned.1.call-update) | async-done | bytes 5242896 | tf_op jit(solution)/shard_map/all_gather | solution.py:413
  69.8 30.9 %shard_map.85 = (bf16[2048,512]{1,0:T(8,128)(2,1)}, bf16[2048,512]{1,0:T(8,128)(2,1)}, f32[1024,2560]{1,0:T(8,128)}) custom-call(s32[16]{0:T(128)} %fusion.2.refs_0_, s32[2]{0:T(128)} %pad_add_fusion.refs_1_, bf16[2048,512]{1,0:T(8,128)(2,1)} %bitcast.10, bf16[2048,512]{1,0:T(8,128)(2,1)} %bitcast.15, bf16[2048,512]{1,0:T(8,128)(2,1)} %collective-permute-done.2.refs_4_, ...), custom_call_target="tpu_custom_call" | custom-call | flops 15032385536 | bytes 16777216 | tf_op jit(solution)/shard_map/pallas_call | solution.py:273
  100.7 0.0 collective-permute-done.1.refs_4_
  100.7 17.6 %shard_map.86 = (bf16[2048,512]{1,0:T(8,128)(2,1)}, bf16[2048,512]{1,0:T(8,128)(2,1)}, f32[1024,2560]{1,0:T(8,128)}) custom-call(s32[16]{0:T(128)} %fusion.2.refs_0_, s32[2]{0:T(128)} %pad_add_fusion.refs_1_, bf16[2048,512]{1,0:T(8,128)(2,1)} %bitcast.11, bf16[2048,512]{1,0:T(8,128)(2,1)} %bitcast.16, ...), custom_call_target="tpu_custom_call", output_to_operand_aliasing={{0}: (7, {}), {1}: (8, {})} | custom-call | flops 7516192768 | bytes 16777216 | tf_op jit(solution)/shard_map/pallas_call | solution.py:273
  118.3 18.0 %shard_map.87 = (bf16[2048,512]{1,0:T(8,128)(2,1)}, bf16[2048,512]{1,0:T(8,128)(2,1)}, bf16[512,2560]{1,0:T(8,128)(2,1)}, bf16[512,2560]{1,0:T(8,128)(2,1)}) custom-call(s32[16]{0:T(128)} %fusion.2.refs_0_, s32[2]{0:T(128)} %pad_add_fusion.refs_1_, bf16[2048,512]{1,0:T(8,128)(2,1)} %bitcast.12, ...), custom_call_target="tpu_custom_call", output_to_operand_aliasing={{0}: (7, {}), {1}: (8, {})} | custom-call | flops 7516192768 | bytes 16777216 | tf_op jit(solution)/shard_map/pallas_call | solution.py:273
  136.2 0.3 collective-permute-start.4
  136.6 1.5 collective-permute-start.3
  138.0 3.4 %collective-permute-done.4.refs_1_ = bf16[512,2560]{1,0:T(8,128)(2,1)S(1)} collective-permute-done((bf16[512,2560]{1,0:T(8,128)(2,1)}, bf16[512,2560]{1,0:T(8,128)(2,1)S(1)}, u32[]{:S(2)}, u32[]{:S(2)}) %collective-permute-start.4) | collective-permute-done | bytes 2621472 | tf_op jit(solution)/shard_map/ppermute | solution.py:317
  141.4 1.0 add_convert_fusion.3
  142.5 0.6 collective-permute-start.6
  143.1 1.2 add_convert_fusion.1
  144.3 1.5 collective-permute-start.8
  145.9 7.2 %collective-permute-done.6 = bf16[64,2560]{1,0:T(8,128)(2,1)S(1)} collective-permute-done((bf16[64,2560]{1,0:T(8,128)(2,1)S(1)}, bf16[64,2560]{1,0:T(8,128)(2,1)S(1)}, u32[]{:S(2)}, u32[]{:S(2)}) %collective-permute-start.6) | collective-permute-done | bytes 327712 | tf_op jit(solution)/shard_map/ppermute | solution.py:317
  153.1 0.2 add_convert_fusion.2
  153.3 0.0 copy-start.1
  153.3 0.6 collective-permute-start.5
  153.9 1.9 collective-permute-start.7
  155.8 11.3 %collective-permute-done.8 = bf16[128,2560]{1,0:T(8,128)(2,1)S(1)} collective-permute-done((bf16[128,2560]{1,0:T(8,128)(2,1)S(1)}, bf16[128,2560]{1,0:T(8,128)(2,1)S(1)}, u32[]{:S(2)}, u32[]{:S(2)}) %collective-permute-start.8) | collective-permute-done | bytes 655392 | tf_op jit(solution)/shard_map/ppermute | solution.py:317
  167.1 0.2 add_convert_fusion
  167.4 1.6 collective-permute-start.10
  169.0 2.3 %collective-permute-start.9 = (bf16[64,2560]{1,0:T(8,128)(2,1)S(1)}, bf16[64,2560]{1,0:T(8,128)(2,1)S(1)}, u32[]{:S(2)}, u32[]{:S(2)}) collective-permute-start(bf16[64,2560]{1,0:T(8,128)(2,1)S(1)} %get-tuple-element.44), channel_id=1, source_target_pairs={{0,24},{2,26},{4,28},{6,30},{8,0},{10,2},{12,4},{14,6},{16,8},{18,... | collective-permute-start | bytes 983048 | tf_op jit(solution)/shard_map/ppermute | solution.py:333
  171.3 13.3 %collective-permute-done.3.sent_ref = bf16[2048,512]{1,0:T(8,128)(2,1)S(1)} collective-permute-done((bf16[2048,512]{1,0:T(8,128)(2,1)}, bf16[2048,512]{1,0:T(8,128)(2,1)S(1)}, u32[]{:S(2)}, u32[]{:S(2)}) %collective-permute-start.3) | collective-permute-done | bytes 2097184 | tf_op jit(solution)/shard_map/ppermute | solution.py:391
  184.6 0.0 collective-permute-done.5.refs_2_
  184.6 2.5 %shard_map.88 = (bf16[2048,512]{1,0:T(8,128)(2,1)}, f32[64,2048]{1,0:T(8,128)}, f32[64,512]{1,0:T(8,128)}) custom-call(bf16[2048,512]{1,0:T(8,128)(2,1)S(1)} %copy-done.1, bf16[2048,512]{1,0:T(8,128)(2,1)S(1)} %collective-permute-done.3.sent_ref, bf16[512,2560]{1,0:T(8,128)(2,1)S(1)} %copy-done, bf16[512,2560]{1,0:T(8,128)(2,1)S(1)} %collective-permute-done.4.refs_1_, ...), custom_call_target="tpu_custom_call" | custom-call | flops 1048576 | bytes 12582912 | tf_op jit(solution)/shard_map/pallas_call | solution.py:360
  (19 shorter events, 0.2 us)
Async XLA Ops:
  7.2 3.2 %copy-start.3 = (bf16[16,128,512]{2,1,0:T(8,128)(2,1)S(1)}, bf16[16,128,512]{2,1,0:T(8,128)(2,1)}, u32[]{:S(2)}) copy-start(bf16[16,128,512]{2,1,0:T(8,128)(2,1)} %param.7) | copy-start | bytes 6291460
  7.2 62.6 %all-gather.2.cloned.1.call-start = ((), (), s32[]{:S(2)}) async-start(), calls=%async_computation | async-start | bytes 5570560 | tf_op jit(solution)/shard_map/all_gather | solution.py:413
  10.5 4.5 %copy-start.2 = (bf16[16,128,512]{2,1,0:T(8,128)(2,1)S(1)}, bf16[16,128,512]{2,1,0:T(8,128)(2,1)}, u32[]{:S(2)}) copy-start(bf16[16,128,512]{2,1,0:T(8,128)(2,1)} %param.6) | copy-start | bytes 6291460
  10.5 4.5 %copy-start.4 = (bf16[16,128,512]{2,1,0:T(8,128)(2,1)S(1)}, bf16[16,128,512]{2,1,0:T(8,128)(2,1)}, u32[]{:S(2)}) copy-start(bf16[16,128,512]{2,1,0:T(8,128)(2,1)} %param.7) | copy-start | bytes 6291460
  12.0 49.7 %collective-permute-start.2 = (bf16[2048,512]{1,0:T(8,128)(2,1)}, bf16[2048,512]{1,0:T(8,128)(2,1)}, u32[]{:S(2)}, u32[]{:S(2)}) collective-permute-start(bf16[2048,512]{1,0:T(8,128)(2,1)} %pad_maximum_fusion), channel_id=1, source_target_pairs={{0,1},{1,0},{2,3},{3,2},{4,5},{5,4},{6,7},{7,6},{8,9},{9,8},{10,11... | collective-permute-start | bytes 6291464 | tf_op jit(solution)/shard_map/ppermute | solution.py:383
  15.1 2.4 %copy-start.7 = (u32[32]{0:T(128)S(1)}, u32[32]{0:T(128)}, u32[]{:S(2)}) copy-start(u32[32]{0:T(128)} %constant.40) | copy-start | bytes 388
  15.1 3.6 %copy-start.5 = (s32[16]{0:T(128)S(1)}, s32[16]{0:T(128)}, u32[]{:S(2)}) copy-start(s32[16]{0:T(128)} %param.11) | copy-start | bytes 196
  15.2 3.6 %copy-start.6 = (s32[16]{0:T(128)S(1)}, s32[16]{0:T(128)}, u32[]{:S(2)}) copy-start(s32[16]{0:T(128)} %param.10) | copy-start | bytes 196
  15.2 85.5 %collective-permute-start.1 = (bf16[1024,512]{1,0:T(8,128)(2,1)S(1)}, bf16[1024,512]{1,0:T(8,128)(2,1)}, u32[]{:S(2)}, u32[]{:S(2)}) collective-permute-start(bf16[1024,512]{1,0:T(8,128)(2,1)S(1)} %pad_maximum_fusion.1), channel_id=1, source_target_pairs={{0,1},{1,0},{2,3},{3,2},{4,5},{5,4},{6,7},{7,6},{8,9},{9,8},{10,11... | collective-permute-start | bytes 3145736 | tf_op jit(solution)/shard_map/ppermute | solution.py:383
  16.8 101.4 %collective-permute-start = (bf16[1024,512]{1,0:T(8,128)(2,1)S(1)}, bf16[1024,512]{1,0:T(8,128)(2,1)}, u32[]{:S(2)}, u32[]{:S(2)}) collective-permute-start(bf16[1024,512]{1,0:T(8,128)(2,1)S(1)} %pad_maximum_fusion.2), channel_id=1, source_target_pairs={{0,1},{1,0},{2,3},{3,2},{4,5},{5,4},{6,7},{7,6},{8,9},{9,8},{10,11... | collective-permute-start | bytes 3145736 | tf_op jit(solution)/shard_map/ppermute | solution.py:383
  136.2 16.9 %copy-start = (bf16[512,2560]{1,0:T(8,128)(2,1)S(1)}, bf16[512,2560]{1,0:T(8,128)(2,1)}, u32[]{:S(2)}) copy-start(bf16[512,2560]{1,0:T(8,128)(2,1)} %get-tuple-element.32.refs_0_) | copy-start | bytes 7864324
  136.2 5.2 %collective-permute-start.4 = (bf16[512,2560]{1,0:T(8,128)(2,1)}, bf16[512,2560]{1,0:T(8,128)(2,1)S(1)}, u32[]{:S(2)}, u32[]{:S(2)}) collective-permute-start(bf16[512,2560]{1,0:T(8,128)(2,1)} %get-tuple-element.33), channel_id=1, source_target_pairs={{0,2},{2,0},{4,6},{6,4},{8,10},{10,8},{12,14},{14,12},{16,18},{18,... | collective-permute-start | bytes 7864328 | tf_op jit(solution)/shard_map/ppermute | solution.py:317
  136.6 48.0 %collective-permute-start.3 = (bf16[2048,512]{1,0:T(8,128)(2,1)}, bf16[2048,512]{1,0:T(8,128)(2,1)S(1)}, u32[]{:S(2)}, u32[]{:S(2)}) collective-permute-start(bf16[2048,512]{1,0:T(8,128)(2,1)} %get-tuple-element.31), channel_id=1, source_target_pairs={{0,1},{1,0},{2,3},{3,2},{4,5},{5,4},{6,7},{7,6},{8,9},{9,8},{10,11... | collective-permute-start | bytes 6291464 | tf_op jit(solution)/shard_map/ppermute | solution.py:391
  142.5 10.6 %collective-permute-start.6 = (bf16[64,2560]{1,0:T(8,128)(2,1)S(1)}, bf16[64,2560]{1,0:T(8,128)(2,1)S(1)}, u32[]{:S(2)}, u32[]{:S(2)}) collective-permute-start(bf16[64,2560]{1,0:T(8,128)(2,1)S(1)} %add_convert_fusion.3), channel_id=1, source_target_pairs={{0,4},{2,6},{4,0},{6,2},{8,12},{10,14},{12,8},{14,10},{16,20},{18,... | collective-permute-start | bytes 983048 | tf_op jit(solution)/shard_map/ppermute | solution.py:317
  144.3 22.8 %collective-permute-start.8 = (bf16[128,2560]{1,0:T(8,128)(2,1)S(1)}, bf16[128,2560]{1,0:T(8,128)(2,1)S(1)}, u32[]{:S(2)}, u32[]{:S(2)}) collective-permute-start(bf16[128,2560]{1,0:T(8,128)(2,1)S(1)} %add_convert_fusion.1), channel_id=1, source_target_pairs={{0,4},{2,6},{4,0},{6,2},{8,12},{10,14},{12,8},{14,10},{16,20},{18,... | collective-permute-start | bytes 1966088 | tf_op jit(solution)/shard_map/ppermute | solution.py:317
  153.3 31.3 %copy-start.1 = (bf16[2048,512]{1,0:T(8,128)(2,1)S(1)}, bf16[2048,512]{1,0:T(8,128)(2,1)}, u32[]{:S(2)}) copy-start(bf16[2048,512]{1,0:T(8,128)(2,1)} %get-tuple-element.30.kept_ref) | copy-start | bytes 6291460
  153.3 31.3 %collective-permute-start.5 = (bf16[64,2560]{1,0:T(8,128)(2,1)S(1)}, bf16[64,2560]{1,0:T(8,128)(2,1)S(1)}, u32[]{:S(2)}, u32[]{:S(2)}) collective-permute-start(bf16[64,2560]{1,0:T(8,128)(2,1)S(1)} %get-tuple-element.38), channel_id=1, source_target_pairs={{0,4},{2,6},{4,0},{6,2},{8,12},{10,14},{12,8},{14,10},{16,20},{18,... | collective-permute-start | bytes 983048 | tf_op jit(solution)/shard_map/ppermute | solution.py:317
  153.9 30.7 %collective-permute-start.7 = (bf16[64,2560]{1,0:T(8,128)(2,1)S(1)}, bf16[64,2560]{1,0:T(8,128)(2,1)S(1)}, u32[]{:S(2)}, u32[]{:S(2)}) collective-permute-start(bf16[64,2560]{1,0:T(8,128)(2,1)S(1)} %get-tuple-element.37), channel_id=1, source_target_pairs={{0,16},{2,18},{4,20},{6,22},{8,24},{10,26},{12,28},{14,30},{16,0},... | collective-permute-start | bytes 983048 | tf_op jit(solution)/shard_map/ppermute | solution.py:333
  167.4 17.2 %collective-permute-start.10 = (bf16[64,2560]{1,0:T(8,128)(2,1)S(1)}, bf16[64,2560]{1,0:T(8,128)(2,1)S(1)}, u32[]{:S(2)}, u32[]{:S(2)}) collective-permute-start(bf16[64,2560]{1,0:T(8,128)(2,1)S(1)} %get-tuple-element.43), channel_id=1, source_target_pairs={{0,8},{2,10},{4,12},{6,14},{8,16},{10,18},{12,20},{14,22},{16,24},... | collective-permute-start | bytes 983048 | tf_op jit(solution)/shard_map/ppermute | solution.py:333
  169.0 15.6 %collective-permute-start.9 = (bf16[64,2560]{1,0:T(8,128)(2,1)S(1)}, bf16[64,2560]{1,0:T(8,128)(2,1)S(1)}, u32[]{:S(2)}, u32[]{:S(2)}) collective-permute-start(bf16[64,2560]{1,0:T(8,128)(2,1)S(1)} %get-tuple-element.44), channel_id=1, source_target_pairs={{0,24},{2,26},{4,28},{6,30},{8,0},{10,2},{12,4},{14,6},{16,8},{18,... | collective-permute-start | bytes 983048 | tf_op jit(solution)/shard_map/ppermute | solution.py:333
Sparse Core Ops, SparseCore 0:
  10.9 58.8 all-gather.1
where the time goes:
time: 194 us
  waiting for transfers between devices  72.5 us (37%)
  Pallas kernels  68.9 us (36%)
  starting transfers between devices  15.5 us (8%)
  between operations  14.9 us (8%)
  blocking collectives  12.3 us (6%)
  other arithmetic  7.44 us (4%)
  local copies, waits for them, and re-layouts  2.27 us (1%)
    pallas_call x3, Pallas kernels, group_call(): pl.pallas_call(functools.partial(group_kernel, start, steps, first, last,...  66.4 us
    ppermute x3, waiting for transfers between devices, exchange(): return lax.ppermute(block, 'tensor', [(0, 1), (1, 0)])  29.3 us
    ppermute x4, waiting for transfers between devices, swap(): return lax.ppermute(block, 'user', [(i, i ^ bit) for i in range(users)])  21.9 us
    ppermute x1, waiting for transfers between devices, give_back(): return lax.ppermute(block, 'tensor', [(0, 1), (1, 0)])  13.3 us
    unnamed x1, blocking collectives  12.3 us
    all_gather x1, waiting for transfers between devices, local(): lax.all_gather(jnp.concatenate([w_in, w_out], axis=1), 'user', axis=0, ti...  8.03 us
    ppermute x3, starting transfers between devices, scatter_parts(): moved.append(lax.ppermute(block, 'user', pairs))  5.78 us
    ppermute x3, starting transfers between devices, exchange(): return lax.ppermute(block, 'tensor', [(0, 1), (1, 0)])  5.12 us
  transfers between devices with their start and end apart: 12, of which 6 were waited for; matrix products, arithmetic and copies ran while one was open for 4% of the time, Pallas kernels for 25%

commit v1 on v0

--- a/solution.py
+++ b/solution.py
@@ -44,15 +44,13 @@
     lanes = [[pl.ds((4 * h + e) * HEAD_DIM, HEAD_DIM) for e in range(4)] for h, _ in pairs]
     heads = [pl.ds(h * HEAD_DIM, HEAD_DIM) for h, _ in pairs]
     every = range(len(pairs))
-    weight = causal * (1.0 / SEQ_LEN)
-
     def part(i, e):
         return g_s[spans[i], lanes[i][e]]
 
-    s = [(dot_nt(part(i, 2), part(i, 3)) * scale).astype(bf16) for i in every]
+    s = [dot_nt(part(i, 2), part(i, 3)) * scale for i in every]
     pair = [gates(t) for t in s]
-    attn = [silu * weight for silu, _ in pair]
-    slope = [t * weight for _, t in pair]
+    attn = [jnp.where(causal, silu * (1.0 / SEQ_LEN), 0.0).astype(bf16) for silu, _ in pair]
+    slope = [jnp.where(causal, t * (scale / SEQ_LEN), 0.0) for _, t in pair]
     y = [dot_nn(attn[i], part(i, 1)) for i in every]
     cen = [t - row_mean(t) for t in y]
     rstd = [lax.rsqrt(row_mean(t * t) + eps) for t in cen]
@@ -64,10 +62,10 @@
     two = [row_mean(dyn[i] * yn[i]) for i in every]
     dy = [((dyn[i] - one[i] - yn[i] * two[i]) * rstd[i]).astype(bf16) for i in every]
     grad_a = [dot_nt(dy[i], part(i, 1)) for i in every]
-    ds = [(grad_a[i] * scale).astype(bf16) * slope[i] for i in every]
+    ds = [(grad_a[i] * slope[i]).astype(bf16) for i in every]
 
     def store(i, e, grad):
-        dz_s[spans[i], lanes[i][e]] = grad.astype(bf16) * slope_s[spans[i], lanes[i][e]]
+        dz_s[spans[i], lanes[i][e]] = (grad * slope_s[spans[i], lanes[i][e]]).astype(bf16)
 
     for i in every:
         hb_s[spans[i], heads[i]] = (yn[i] * uf[i]).astype(bf16)
@@ -85,10 +83,27 @@
     return rest + [0]
 
 
+def piece_order(far):
+    slow = [0] + split_order(far)[:-1]
+    return [(j, xs, cs) for cs in range(2) for xs in range(2) for j in slow]
+
+
+def gather_parts(shard, users):
+    def swap(block, bit):
+        return lax.ppermute(block, "user", [(i, i ^ bit) for i in range(users)])
+
+    pieces = [shard]
+    for j in split_order(users // 4)[:-1]:
+        pairs = [(i, (i - 4 * j) % users) for i in range(users)]
+        pieces.append(lax.ppermute(shard, "user", pairs))
+    pieces += [swap(piece, 2) for piece in pieces]
+    return pieces + [swap(piece, 1) for piece in pieces]
+
+
 def group_kernel(start, steps, first, last, heads, parts, users, *refs):
     refs = list(refs)
-    lens_ref, where_ref, xo_ref, do_ref, far_ref, w_hbm = refs[:6]
-    refs = refs[6:]
+    lens_ref, where_ref, xo_ref, do_ref, far_ref = refs[:5]
+    pieces, refs = refs[5 : 5 + users], refs[5 + users :]
     acc_hbm = None if first else refs.pop(0)
     refs = refs if first else refs[2:]
     gx_ref, bs_ref = refs[:2]
@@ -109,14 +124,25 @@
         else:
             pl.when(step == index)(run)
 
+    size = width // users
+    far = users // 4
+    zi, xi, ci = user // 4, lax.rem(user // 2, 2), lax.rem(user, 2)
+
+    def rows_of(j, xs, cs):
+        zd = lax.rem(zi + j, far)
+        xd = xi if xs == 0 else 1 - xi
+        cd = ci if cs == 0 else 1 - ci
+        row = ((zd * 2 + xd) * 2 + cd) * size
+        row = lax.rem(row // own - me + parts, parts) * own + lax.rem(row, own)
+        return pl.ds(pl.multiple_of(row, size), size)
+
     loads = []
-    for p in range(parts):
-        source = pl.ds(pl.multiple_of(lax.rem(me + p, parts) * own, own), own)
+    for piece, (j, xs, cs) in zip(pieces, piece_order(far)):
         loads.append(
-            pltpu.make_async_copy(w_hbm.at[source], w_s.at[pl.ds(p * own, own)], load_sems.at[p])
+            pltpu.make_async_copy(piece, w_s.at[rows_of(j, xs, cs)], load_sems.at[len(loads)])
         )
     if not first:
-        acc_load = pltpu.make_async_copy(acc_hbm, acc_s, load_sems.at[parts])
+        acc_load = pltpu.make_async_copy(acc_hbm, acc_s, load_sems.at[users])
 
     def begin():
         for copy in loads:
@@ -135,7 +161,6 @@
     causal = lax.broadcasted_iota(jnp.int32, (SEQ_LEN, SEQ_LEN), 0) >= lax.broadcasted_iota(
         jnp.int32, (SEQ_LEN, SEQ_LEN), 1
     )
-    causal = causal.astype(f32).astype(bf16)
     position = lax.broadcasted_iota(jnp.int32, (SEQ_LEN, 1), 0)
     half = min(2 * SEQ_LEN, rows)
     halves = [slice(lo, lo + half) for lo in range(0, rows, half)]
@@ -161,8 +186,8 @@
     only(0, loaded)
     for h in range(heads):
         c = slice(h * 4 * HEAD_DIM, (h + 1) * 4 * HEAD_DIM)
-        z = dot_nn(nb_s[...], w_s[:, c]).astype(bf16)
-        g_s[:, c], slope_s[:, c] = gates(z)
+        silu, slope_s[:, c] = gates(dot_nn(nb_s[...], w_s[:, c]))
+        g_s[:, c] = silu.astype(bf16)
     for here in halves:
         base = start * histories + step * histories
         valid = jnp.concatenate(
@@ -184,9 +209,6 @@
     if not first:
         only(0, acc_load.wait)
     target = out_s if last else acc_s
-    size = width // users
-    far = users // 4
-    zi, xi, ci = user // 4, lax.rem(user // 2, 2), lax.rem(user, 2)
     stores = []
 
     def ship(lo, wide):
@@ -201,19 +223,13 @@
             return
         keep, send = grads_hbm
         for at, j in enumerate(split_order(far)):
-            zd = lax.rem(zi + far - j, far)
             for xs in range(2):
-                xd = xi if xs == 0 else 1 - xi
                 for cs in range(2):
-                    cd = ci if cs == 0 else 1 - ci
-                    row = ((zd * 2 + xd) * 2 + cd) * size
-                    row = lax.rem(row // own - me + parts, parts) * own + lax.rem(row, own)
-                    slot = xs * far + at
                     there = keep if cs == 0 else send
                     stores.append(
                         pltpu.make_async_copy(
-                            out_s.at[pl.ds(pl.multiple_of(row, size), size), lanes],
-                            there.at[pl.ds(slot * size, size), lanes],
+                            out_s.at[rows_of(far - j, xs, cs), lanes],
+                            there.at[pl.ds((xs * far + at) * size, size), lanes],
                             store_sems.at[len(stores)],
                         )
                     )
@@ -251,20 +267,19 @@
         only(steps - 1, copy.wait)
 
 
-def group_call(group, blocks, users, lens, where, x, d, far, weights, past):
+def group_call(group, blocks, users, parts, lens, where, x, d, far, pieces, past):
     start, steps = group
     first, last = start == 0, start + steps == blocks
     rows, own = x.shape[0] // blocks, x.shape[1]
-    width, cols = weights.shape
-    parts = width // own
+    width, cols = own * parts, pieces[0].shape[1]
     heads = cols // (5 * HEAD_DIM)
     cols_in = heads * 4 * HEAD_DIM
     smem = pl.BlockSpec(memory_space=pltpu.SMEM)
     anywhere = pl.BlockSpec(memory_space=pl.ANY)
     mine = pl.BlockSpec((rows, own), lambda i: (start + i, 0))
     theirs = pl.BlockSpec((2 * rows, width - own), lambda i: (i, 0))
-    args = [lens, where, x, d, far, weights] + past
-    specs = [smem, smem, mine, mine, theirs] + [anywhere] * (1 + len(past))
+    args = [lens, where, x, d, far] + pieces + past
+    specs = [smem, smem, mine, mine, theirs] + [anywhere] * (users + len(past))
     if last:
         grads = [jax.ShapeDtypeStruct((width // 2, cols), bf16)] * 2
     else:
@@ -284,7 +299,7 @@
             pl.BlockSpec((rows, width - own), lambda i: (start + i, 0)),
         ]
         + [anywhere] * len(grads),
-        input_output_aliases={} if first else {7: 0, 8: 1},
+        input_output_aliases={} if first else {users + 6: 0, users + 7: 1},
         scratch_shapes=[
             pltpu.VMEM((width, cols), bf16),
             pltpu.VMEM((width, cols), f32),
@@ -295,10 +310,10 @@
             pltpu.VMEM((rows, cols_in), bf16),
             pltpu.VMEM((rows, cols - cols_in), bf16),
             pltpu.VMEM((rows, cols_in), bf16),
-            pltpu.VMEM((rows, cols_in), bf16),
+            pltpu.VMEM((rows, cols_in), f32),
             pltpu.VMEM((rows, cols - cols_in), f32),
             pltpu.VMEM((width, cols) if last else (16, 128), bf16),
-            pltpu.SemaphoreType.DMA((parts + 1,)),
+            pltpu.SemaphoreType.DMA((users + 1,)),
             pltpu.SemaphoreType.DMA(((users if last else 1) * (heads + 1),)),
         ],
         compiler_params=pltpu.CompilerParams(vmem_limit_bytes=56 * 2**20),
@@ -410,11 +425,10 @@
         ahead = jnp.concatenate([t[span] for span in spans for t in (x, d)], axis=0)
         far.append(exchange(ahead, tensor))
 
-    weights = lax.all_gather(
-        jnp.concatenate([w_in, w_out], axis=1), "user", axis=0, tiled=True
-    )
-    table = lax.all_gather(slot_source * 256 + slot_length, "user", axis=0, tiled=True)
-    table = table.reshape(users, hist)
+    pieces = gather_parts(jnp.concatenate([w_in, w_out], axis=1), users)
+    slots = jnp.pad((slot_source * 256 + slot_length)[None], ((0, 7), (0, 128 - hist)))
+    table = lax.all_gather(slots, "user", axis=0, tiled=True)
+    table = table.reshape(users, 8, 128)[:, 0, :hist]
     user = lax.axis_index("user")
     lens = jnp.sum(jnp.where(table // 256 == user, table % 256, 0), axis=0)
     where = jnp.stack([lax.axis_index("tensor"), user]).astype(jnp.int32)
@@ -422,7 +436,7 @@
     past = []
     for group, theirs in zip(GROUPS, far):
         kept, bs, *grads = group_call(
-            group, blocks, users, lens, where, x, d, theirs, weights, past
+            group, blocks, users, tensor, lens, where, x, d, theirs, pieces, past
         )
         past = grads + [kept, bs]
     sent = give_back(bs, own, tensor)

time: 194 us -> 204 us (1.052); the launches traced: 194 us -> 201 us
  between operations: 14.9 us -> 1.48 us
  blocking collectives: 12.3 us -> 22.2 us
  starting transfers between devices: 15.5 us -> 21.6 us
  local copies, waits for them, and re-layouts: 2.27 us -> 7.15 us
    ppermute x3, waiting for transfers between devices: 29.3 us -> 0.01 us  [exchange(): return lax.ppermute(block, 'tensor', [(0, 1), (1, 0)])]
    all_gather x0 -> x1, blocking collectives: none -> 22.2 us  [local(): table = lax.all_gather(slots, 'user', axis=0, tiled=True)]
    ppermute x0 -> x3, waiting for transfers between devices: none -> 19.3 us  [gather_parts(): pieces.append(lax.ppermute(shard, 'user', pairs))]
    ppermute x4 -> x16, waiting for transfers between devices: 21.9 us -> 37.9 us  [swap(): return lax.ppermute(block, 'user', [(i, i ^ bit) for i in range(users)])]
    unnamed x1 -> x0, blocking collectives: 12.3 us -> none
    all_gather x1 -> x0, waiting for transfers between devices: 8.03 us -> none  [local(): lax.all_gather(jnp.concatenate([w_in, w_out], axis=1), 'user', axis=0, ti...]
    ppermute x4 -> x16, starting transfers between devices: 3.1 us -> 9.14 us  [swap(): return lax.ppermute(block, 'user', [(i, i ^ bit) for i in range(users)])]
    ppermute x0 -> x3, starting transfers between devices: none -> 4.68 us  [gather_parts(): pieces.append(lax.ppermute(shard, 'user', pairs))]
  transfers between devices with their start and end apart: 12 -> 26, of which waited for: 6 -> 7; matrix products, arithmetic and copies ran while one was open for 4% -> 3% of each run, Pallas kernels for 25% -> 25%
where the time goes in v1:
time: 204 us; the launch traced here: 201 us
  waiting for transfers between devices  72.3 us (35%)
  Pallas kernels  70.6 us (35%)
  blocking collectives  22.2 us (11%)
  starting transfers between devices  21.6 us (11%)
  local copies, waits for them, and re-layouts  7.15 us (4%)
  other arithmetic  5.46 us (3%)
    pallas_call x3, Pallas kernels, group_call(): pl.pallas_call(functools.partial(group_kernel, start, steps, first, last,...  68.1 us
    ppermute x16, waiting for transfers between devices, swap(): return lax.ppermute(block, 'user', [(i, i ^ bit) for i in range(users)])  37.9 us
    all_gather x1, blocking collectives, local(): table = lax.all_gather(slots, 'user', axis=0, tiled=True)  22.2 us
    ppermute x3, waiting for transfers between devices, gather_parts(): pieces.append(lax.ppermute(shard, 'user', pairs))  19.3 us
    ppermute x1, waiting for transfers between devices, give_back(): return lax.ppermute(block, 'tensor', [(0, 1), (1, 0)])  15.1 us
    ppermute x16, starting transfers between devices, swap(): return lax.ppermute(block, 'user', [(i, i ^ bit) for i in range(users)])  9.14 us
    ppermute x3, starting transfers between devices, exchange(): return lax.ppermute(block, 'tensor', [(0, 1), (1, 0)])  5.06 us
    ppermute x3, starting transfers between devices, gather_parts(): pieces.append(lax.ppermute(shard, 'user', pairs))  4.68 us
  transfers between devices with their start and end apart: 26, of which 7 were waited for; matrix products, arithmetic and copies ran while one was open for 3% of the time, Pallas kernels for 25%

profile of v1, /device:TPU:0, one launch (start us, length us, event | category | flops | bytes accessed | tf_op | source)
XLA Modules:
  0.0 200.8 jit_solution(17428198471869384403)
XLA Ops:
  0.6 1.4 fusion.6
  2.1 0.5 copy-done.2
  2.7 1.5 pad_maximum_fusion
  4.1 3.0 %collective-permute-start.17 = (bf16[2048,512]{1,0:T(8,128)(2,1)}, bf16[2048,512]{1,0:T(8,128)(2,1)}, u32[]{:S(2)}, u32[]{:S(2)}) collective-permute-start(bf16[2048,512]{1,0:T(8,128)(2,1)} %pad_maximum_fusion), channel_id=1, source_target_pairs={{0,1},{1,0},{2,3},{3,2},{4,5},{5,4},{6,7},{7,6},{8,9},{9,8},{10,11... | collective-permute-start | bytes 6291464 | tf_op jit(solution)/shard_map/ppermute | solution.py:398
  7.2 2.7 %collective-permute-start.1 = (bf16[64,2560]{1,0:T(8,128)(2,1)S(1)}, bf16[64,2560]{1,0:T(8,128)(2,1)}, u32[]{:S(2)}, u32[]{:S(2)}) collective-permute-start(bf16[64,2560]{1,0:T(8,128)(2,1)S(1)} %constant_dynamic-update-slice_fusion.refs_5_), channel_id=1, source_target_pairs={{0,16},{2,18},{4,20},{6,22},{8,24},{10,26},{12,28},{14,30},{16,0},... | collective-permute-start | bytes 983048 | tf_op jit(solution)/shard_map/ppermute | solution.py:98
  9.8 1.3 collective-permute-start.2
  11.2 0.7 collective-permute-start.3
  11.8 1.5 collective-permute-start.4
  13.3 19.3 %collective-permute-done.1.refs_6_ = bf16[64,2560]{1,0:T(8,128)(2,1)} collective-permute-done((bf16[64,2560]{1,0:T(8,128)(2,1)S(1)}, bf16[64,2560]{1,0:T(8,128)(2,1)}, u32[]{:S(2)}, u32[]{:S(2)}) %collective-permute-start.1) | collective-permute-done | bytes 327712 | tf_op jit(solution)/shard_map/ppermute | solution.py:98
  32.7 1.5 collective-permute-start.5
  34.2 0.5 collective-permute-start.6
  34.7 1.1 slice.85
  35.9 1.6 collective-permute-start.7
  37.5 5.9 %collective-permute-done.5.refs_10_ = bf16[64,2560]{1,0:T(8,128)(2,1)S(1)} collective-permute-done((bf16[64,2560]{1,0:T(8,128)(2,1)}, bf16[64,2560]{1,0:T(8,128)(2,1)S(1)}, u32[]{:S(2)}, u32[]{:S(2)}) %collective-permute-start.5) | collective-permute-done | bytes 327712 | tf_op jit(solution)/shard_map/ppermute | solution.py:93
  43.4 7.1 %collective-permute-done.6.refs_11_ = bf16[64,2560]{1,0:T(8,128)(2,1)} collective-permute-done((bf16[64,2560]{1,0:T(8,128)(2,1)}, bf16[64,2560]{1,0:T(8,128)(2,1)}, u32[]{:S(2)}, u32[]{:S(2)}) %collective-permute-start.6) | collective-permute-done | bytes 327712 | tf_op jit(solution)/shard_map/ppermute | solution.py:93
  50.7 22.2 %all_gather.3 = s32[128,128]{1,0:T(8,128)S(1)} all-gather(s32[8,128]{1,0:T(8,128)S(1)} %pad.4), channel_id=1, replica_groups=mesh['user'=16,'tensor'=2] {'user'}, dimensions={0}, use_global_device_ids=true | all-gather | bytes 69632 | tf_op jit(solution)/shard_map/all_gather | solution.py:430
  73.0 1.1 slice.87
  74.1 0.4 collective-permute-start.12
  74.5 0.2 collective-permute-start.13
  74.7 0.3 collective-permute-start.14
  75.0 0.2 collective-permute-start.15
  75.2 0.6 pad_add_fusion.refs_1_
  75.8 0.5 fusion.2.refs_0_
  76.4 0.6 collective-permute-start.16
  77.0 1.5 collective-permute-start
  78.6 0.7 copy-done.15
  79.2 0.1 copy-done.16
  79.4 31.4 %shard_map.85 = (bf16[2048,512]{1,0:T(8,128)(2,1)}, bf16[2048,512]{1,0:T(8,128)(2,1)}, f32[1024,2560]{1,0:T(8,128)}) custom-call(s32[16]{0:T(128)} %fusion.2.refs_0_, s32[2]{0:T(128)} %pad_add_fusion.refs_1_, bf16[2048,512]{1,0:T(8,128)(2,1)} %bitcast.13, bf16[2048,512]{1,0:T(8,128)(2,1)} %bitcast.20, bf16[2048,512]{1,0:T(8,128)(2,1)} %collective-permute-done.17.refs_4_, ...), custom_call_target="tpu_custom_call" | custom-call | flops 15032385536 | bytes 16777216 | tf_op jit(solution)/shard_map/pallas_call | solution.py:288
  110.8 1.0 copy-done.7
  111.7 18.2 %shard_map.86 = (bf16[2048,512]{1,0:T(8,128)(2,1)}, bf16[2048,512]{1,0:T(8,128)(2,1)}, f32[1024,2560]{1,0:T(8,128)}) custom-call(s32[16]{0:T(128)} %fusion.2.refs_0_, s32[2]{0:T(128)} %pad_add_fusion.refs_1_, bf16[2048,512]{1,0:T(8,128)(2,1)} %bitcast.14, bf16[2048,512]{1,0:T(8,128)(2,1)} %bitcast.21, ...), custom_call_target="tpu_custom_call", output_to_operand_aliasing={{0}: (22, {}), {1}: (23, {})} | custom-call | flops 7516192768 | bytes 16777216 | tf_op jit(solution)/shard_map/pallas_call | solution.py:288
  130.0 1.0 copy-done.6
  131.0 18.5 %shard_map.87 = (bf16[2048,512]{1,0:T(8,128)(2,1)}, bf16[2048,512]{1,0:T(8,128)(2,1)}, bf16[512,2560]{1,0:T(8,128)(2,1)}, bf16[512,2560]{1,0:T(8,128)(2,1)}) custom-call(s32[16]{0:T(128)} %fusion.2.refs_0_, s32[2]{0:T(128)} %pad_add_fusion.refs_1_, bf16[2048,512]{1,0:T(8,128)(2,1)} %bitcast.15, ...), custom_call_target="tpu_custom_call", output_to_operand_aliasing={{0}: (22, {}), {1}: (23, {})} | custom-call | flops 7516192768 | bytes 16777216 | tf_op jit(solution)/shard_map/pallas_call | solution.py:288
  149.6 0.6 collective-permute-start.18
  150.1 4.5 %collective-permute-done.19.refs_1_ = bf16[512,2560]{1,0:T(8,128)(2,1)S(1)} collective-permute-done((bf16[512,2560]{1,0:T(8,128)(2,1)}, bf16[512,2560]{1,0:T(8,128)(2,1)S(1)}, u32[]{:S(2)}, u32[]{:S(2)}) %collective-permute-start.19) | collective-permute-done | bytes 2621472 | tf_op jit(solution)/shard_map/ppermute | solution.py:332
  154.7 1.0 add_convert_fusion.3
  155.7 0.6 collective-permute-start.21
  156.3 1.2 add_convert_fusion.1
  157.6 1.6 collective-permute-start.23
  159.1 7.2 %collective-permute-done.21 = bf16[64,2560]{1,0:T(8,128)(2,1)S(1)} collective-permute-done((bf16[64,2560]{1,0:T(8,128)(2,1)S(1)}, bf16[64,2560]{1,0:T(8,128)(2,1)S(1)}, u32[]{:S(2)}, u32[]{:S(2)}) %collective-permute-start.21) | collective-permute-done | bytes 327712 | tf_op jit(solution)/shard_map/ppermute | solution.py:332
  166.4 0.2 add_convert_fusion.2
  166.6 0.6 collective-permute-start.20
  167.2 0.1 collective-permute-start.22
  167.3 13.1 %collective-permute-done.23 = bf16[128,2560]{1,0:T(8,128)(2,1)S(1)} collective-permute-done((bf16[128,2560]{1,0:T(8,128)(2,1)S(1)}, bf16[128,2560]{1,0:T(8,128)(2,1)S(1)}, u32[]{:S(2)}, u32[]{:S(2)}) %collective-permute-start.23) | collective-permute-done | bytes 655392 | tf_op jit(solution)/shard_map/ppermute | solution.py:332
  180.4 0.2 add_convert_fusion
  180.7 0.7 collective-permute-start.24
  181.4 1.4 collective-permute-start.25
  182.8 15.1 %collective-permute-done.18.sent_ref = bf16[2048,512]{1,0:T(8,128)(2,1)S(1)} collective-permute-done((bf16[2048,512]{1,0:T(8,128)(2,1)}, bf16[2048,512]{1,0:T(8,128)(2,1)S(1)}, u32[]{:S(2)}, u32[]{:S(2)}) %collective-permute-start.18) | collective-permute-done | bytes 2097184 | tf_op jit(solution)/shard_map/ppermute | solution.py:406
  197.9 2.5 %shard_map.88 = (bf16[2048,512]{1,0:T(8,128)(2,1)}, f32[64,2048]{1,0:T(8,128)}, f32[64,512]{1,0:T(8,128)}) custom-call(bf16[2048,512]{1,0:T(8,128)(2,1)S(1)} %copy-done.1, bf16[2048,512]{1,0:T(8,128)(2,1)S(1)} %collective-permute-done.18.sent_ref, bf16[512,2560]{1,0:T(8,128)(2,1)S(1)} %copy-done, bf16[512,2560]{1,0:T(8,128)(2,1)S(1)} %collective-permute-done.19.refs_1_, ...), custom_call_target="tpu_custom_call" | custom-call | flops 1048576 | bytes 12582912 | tf_op jit(solution)/shard_map/pallas_call | solution.py:375
  (68 shorter events, 0.7 us)
Async XLA Ops:
  0.6 1.9 copy-start.2
  2.6 4.5 %copy-start.3 = (bf16[64,2048]{1,0:T(8,128)(2,1)S(1)}, bf16[64,2048]{1,0:T(8,128)(2,1)}, u32[]{:S(2)}) copy-start(bf16[64,2048]{1,0:T(8,128)(2,1)} %param.8) | copy-start | bytes 786436
  2.7 4.5 %copy-start.5 = (bf16[64,512]{1,0:T(8,128)(2,1)S(1)}, bf16[64,512]{1,0:T(8,128)(2,1)}, u32[]{:S(2)}) copy-start(bf16[64,512]{1,0:T(8,128)(2,1)} %param.9) | copy-start | bytes 196612
  4.1 74.4 %collective-permute-start.17 = (bf16[2048,512]{1,0:T(8,128)(2,1)}, bf16[2048,512]{1,0:T(8,128)(2,1)}, u32[]{:S(2)}, u32[]{:S(2)}) collective-permute-start(bf16[2048,512]{1,0:T(8,128)(2,1)} %pad_maximum_fusion), channel_id=1, source_target_pairs={{0,1},{1,0},{2,3},{3,2},{4,5},{5,4},{6,7},{7,6},{8,9},{9,8},{10,11... | collective-permute-start | bytes 6291464 | tf_op jit(solution)/shard_map/ppermute | solution.py:398
  7.1 43.5 %copy-start.4 = (bf16[64,2560]{1,0:T(8,128)(2,1)}, bf16[64,2560]{1,0:T(8,128)(2,1)S(1)}, u32[]{:S(2)}) copy-start(bf16[64,2560]{1,0:T(8,128)(2,1)S(1)} %constant_dynamic-update-slice_fusion.refs_5_) | copy-start | bytes 983044
  7.2 25.5 %collective-permute-start.1 = (bf16[64,2560]{1,0:T(8,128)(2,1)S(1)}, bf16[64,2560]{1,0:T(8,128)(2,1)}, u32[]{:S(2)}, u32[]{:S(2)}) collective-permute-start(bf16[64,2560]{1,0:T(8,128)(2,1)S(1)} %constant_dynamic-update-slice_fusion.refs_5_), channel_id=1, source_target_pairs={{0,16},{2,18},{4,20},{6,22},{8,24},{10,26},{12,28},{14,30},{16,0},... | collective-permute-start | bytes 983048 | tf_op jit(solution)/shard_map/ppermute | solution.py:98
  9.8 22.8 %collective-permute-start.2 = (bf16[64,2560]{1,0:T(8,128)(2,1)S(1)}, bf16[64,2560]{1,0:T(8,128)(2,1)}, u32[]{:S(2)}, u32[]{:S(2)}) collective-permute-start(bf16[64,2560]{1,0:T(8,128)(2,1)S(1)} %constant_dynamic-update-slice_fusion.refs_5_), channel_id=1, source_target_pairs={{0,24},{2,26},{4,28},{6,30},{8,0},{10,2},{12,4},{14,6},{16,8},{18,... | collective-permute-start | bytes 983048 | tf_op jit(solution)/shard_map/ppermute | solution.py:98
  11.2 23.0 %collective-permute-start.3 = (bf16[64,2560]{1,0:T(8,128)(2,1)S(1)}, bf16[64,2560]{1,0:T(8,128)(2,1)}, u32[]{:S(2)}, u32[]{:S(2)}) collective-permute-start(bf16[64,2560]{1,0:T(8,128)(2,1)S(1)} %constant_dynamic-update-slice_fusion.refs_5_), channel_id=1, source_target_pairs={{0,8},{2,10},{4,12},{6,14},{8,16},{10,18},{12,20},{14,22},{16,24},... | collective-permute-start | bytes 983048 | tf_op jit(solution)/shard_map/ppermute | solution.py:98
  11.8 24.0 %collective-permute-start.4 = (bf16[64,2560]{1,0:T(8,128)(2,1)S(1)}, bf16[64,2560]{1,0:T(8,128)(2,1)S(1)}, u32[]{:S(2)}, u32[]{:S(2)}) collective-permute-start(bf16[64,2560]{1,0:T(8,128)(2,1)S(1)} %constant_dynamic-update-slice_fusion.refs_5_), channel_id=1, source_target_pairs={{0,4},{2,6},{4,0},{6,2},{8,12},{10,14},{12,8},{14,10},{16,20},{18,... | collective-permute-start | bytes 983048 | tf_op jit(solution)/shard_map/ppermute | solution.py:93
  32.6 3.3 %collective-permute-start.8 = (bf16[64,2560]{1,0:T(8,128)(2,1)S(1)}, bf16[64,2560]{1,0:T(8,128)(2,1)S(1)}, u32[]{:S(2)}, u32[]{:S(2)}) collective-permute-start(bf16[64,2560]{1,0:T(8,128)(2,1)S(1)} %constant_dynamic-update-slice_fusion.refs_5_), channel_id=1, source_target_pairs={{0,2},{2,0},{4,6},{6,4},{8,10},{10,8},{12,14},{14,12},{16,18},{18,... | collective-permute-start | bytes 983048 | tf_op jit(solution)/shard_map/ppermute | solution.py:93
  32.7 10.7 %collective-permute-start.5 = (bf16[64,2560]{1,0:T(8,128)(2,1)}, bf16[64,2560]{1,0:T(8,128)(2,1)S(1)}, u32[]{:S(2)}, u32[]{:S(2)}) collective-permute-start(bf16[64,2560]{1,0:T(8,128)(2,1)} %collective-permute-done.1.refs_6_), channel_id=1, source_target_pairs={{0,4},{2,6},{4,0},{6,2},{8,12},{10,14},{12,8},{14,10},{16,20},{18,... | collective-permute-start | bytes 983048 | tf_op jit(solution)/shard_map/ppermute | solution.py:93
  34.2 16.3 %collective-permute-start.6 = (bf16[64,2560]{1,0:T(8,128)(2,1)}, bf16[64,2560]{1,0:T(8,128)(2,1)}, u32[]{:S(2)}, u32[]{:S(2)}) collective-permute-start(bf16[64,2560]{1,0:T(8,128)(2,1)} %collective-permute-done.2.refs_7_), channel_id=1, source_target_pairs={{0,4},{2,6},{4,0},{6,2},{8,12},{10,14},{12,8},{14,10},{16,20},{18,... | collective-permute-start | bytes 983048 | tf_op jit(solution)/shard_map/ppermute | solution.py:93
  34.7 16.0 %copy-start.17 = (s32[16]{0:T(128)S(1)}, s32[16]{0:T(128)}, u32[]{:S(2)}) copy-start(s32[16]{0:T(128)} %param.11) | copy-start | bytes 196
  34.7 16.0 %copy-start.18 = (s32[16]{0:T(128)S(1)}, s32[16]{0:T(128)}, u32[]{:S(2)}) copy-start(s32[16]{0:T(128)} %param.10) | copy-start | bytes 196
  35.8 14.7 %copy-start.8 = (bf16[64,2560]{1,0:T(8,128)(2,1)}, bf16[64,2560]{1,0:T(8,128)(2,1)S(1)}, u32[]{:S(2)}) copy-start(bf16[64,2560]{1,0:T(8,128)(2,1)S(1)} %collective-permute-done.4.refs_9_) | copy-start | bytes 983044
  35.8 38.7 %collective-permute-start.10 = (bf16[64,2560]{1,0:T(8,128)(2,1)}, bf16[64,2560]{1,0:T(8,128)(2,1)}, u32[]{:S(2)}, u32[]{:S(2)}) collective-permute-start(bf16[64,2560]{1,0:T(8,128)(2,1)} %collective-permute-done.2.refs_7_), channel_id=1, source_target_pairs={{0,2},{2,0},{4,6},{6,4},{8,10},{10,8},{12,14},{14,12},{16,18},{18,... | collective-permute-start | bytes 983048 | tf_op jit(solution)/shard_map/ppermute | solution.py:93
  35.9 14.6 %copy-start.10 = (bf16[64,2560]{1,0:T(8,128)(2,1)}, bf16[64,2560]{1,0:T(8,128)(2,1)S(1)}, u32[]{:S(2)}) copy-start(bf16[64,2560]{1,0:T(8,128)(2,1)S(1)} %collective-permute-done.8.refs_13_) | copy-start | bytes 983044
  35.9 38.1 %collective-permute-start.7 = (bf16[64,2560]{1,0:T(8,128)(2,1)}, bf16[64,2560]{1,0:T(8,128)(2,1)}, u32[]{:S(2)}, u32[]{:S(2)}) collective-permute-start(bf16[64,2560]{1,0:T(8,128)(2,1)} %collective-permute-done.3.refs_8_), channel_id=1, source_target_pairs={{0,4},{2,6},{4,0},{6,2},{8,12},{10,14},{12,8},{14,10},{16,20},{18,... | collective-permute-start | bytes 983048 | tf_op jit(solution)/shard_map/ppermute | solution.py:93
  43.4 7.1 %copy-start.11 = (bf16[64,2560]{1,0:T(8,128)(2,1)}, bf16[64,2560]{1,0:T(8,128)(2,1)S(1)}, u32[]{:S(2)}) copy-start(bf16[64,2560]{1,0:T(8,128)(2,1)S(1)} %collective-permute-done.5.refs_10_) | copy-start | bytes 983044
  43.4 31.3 %collective-permute-start.11 = (bf16[64,2560]{1,0:T(8,128)(2,1)}, bf16[64,2560]{1,0:T(8,128)(2,1)}, u32[]{:S(2)}, u32[]{:S(2)}) collective-permute-start(bf16[64,2560]{1,0:T(8,128)(2,1)} %collective-permute-done.3.refs_8_), channel_id=1, source_target_pairs={{0,2},{2,0},{4,6},{6,4},{8,10},{10,8},{12,14},{14,12},{16,18},{18,... | collective-permute-start | bytes 983048 | tf_op jit(solution)/shard_map/ppermute | solution.py:93
  50.5 24.5 %collective-permute-start.9 = (bf16[64,2560]{1,0:T(8,128)(2,1)}, bf16[64,2560]{1,0:T(8,128)(2,1)}, u32[]{:S(2)}, u32[]{:S(2)}) collective-permute-start(bf16[64,2560]{1,0:T(8,128)(2,1)} %collective-permute-done.1.refs_6_), channel_id=1, source_target_pairs={{0,2},{2,0},{4,6},{6,4},{8,10},{10,8},{12,14},{14,12},{16,18},{18,... | collective-permute-start | bytes 983048 | tf_op jit(solution)/shard_map/ppermute | solution.py:93
  50.7 23.4 %copy-start.9 = (bf16[64,2560]{1,0:T(8,128)(2,1)S(1)}, bf16[64,2560]{1,0:T(8,128)(2,1)}, u32[]{:S(2)}) copy-start(bf16[64,2560]{1,0:T(8,128)(2,1)} %copy-done.8) | copy-start | bytes 983044
  50.7 23.8 %copy-start.12 = (bf16[64,2560]{1,0:T(8,128)(2,1)S(1)}, bf16[64,2560]{1,0:T(8,128)(2,1)}, u32[]{:S(2)}) copy-start(bf16[64,2560]{1,0:T(8,128)(2,1)} %copy-done.11) | copy-start | bytes 983044
  74.1 2.3 %collective-permute-start.12 = (bf16[64,2560]{1,0:T(8,128)(2,1)S(1)}, bf16[64,2560]{1,0:T(8,128)(2,1)S(1)}, u32[]{:S(2)}, u32[]{:S(2)}) collective-permute-start(bf16[64,2560]{1,0:T(8,128)(2,1)S(1)} %copy-done.9), channel_id=1, source_target_pairs={{0,2},{2,0},{4,6},{6,4},{8,10},{10,8},{12,14},{14,12},{16,18},{18,... | collective-permute-start | bytes 983048 | tf_op jit(solution)/shard_map/ppermute | solution.py:93
  74.5 2.5 %collective-permute-start.13 = (bf16[64,2560]{1,0:T(8,128)(2,1)S(1)}, bf16[64,2560]{1,0:T(8,128)(2,1)S(1)}, u32[]{:S(2)}, u32[]{:S(2)}) collective-permute-start(bf16[64,2560]{1,0:T(8,128)(2,1)S(1)} %copy-done.12), channel_id=1, source_target_pairs={{0,2},{2,0},{4,6},{6,4},{8,10},{10,8},{12,14},{14,12},{16,18},{18,... | collective-permute-start | bytes 983048 | tf_op jit(solution)/shard_map/ppermute | solution.py:93
  74.7 3.8 %collective-permute-start.14 = (bf16[64,2560]{1,0:T(8,128)(2,1)}, bf16[64,2560]{1,0:T(8,128)(2,1)S(1)}, u32[]{:S(2)}, u32[]{:S(2)}) collective-permute-start(bf16[64,2560]{1,0:T(8,128)(2,1)} %collective-permute-done.6.refs_11_), channel_id=1, source_target_pairs={{0,2},{2,0},{4,6},{6,4},{8,10},{10,8},{12,14},{14,12},{16,18},{18,... | collective-permute-start | bytes 983048 | tf_op jit(solution)/shard_map/ppermute | solution.py:93
  75.0 3.5 %collective-permute-start.15 = (bf16[64,2560]{1,0:T(8,128)(2,1)}, bf16[64,2560]{1,0:T(8,128)(2,1)S(1)}, u32[]{:S(2)}, u32[]{:S(2)}) collective-permute-start(bf16[64,2560]{1,0:T(8,128)(2,1)} %collective-permute-done.7.refs_12_), channel_id=1, source_target_pairs={{0,2},{2,0},{4,6},{6,4},{8,10},{10,8},{12,14},{14,12},{16,18},{18,... | collective-permute-start | bytes 983048 | tf_op jit(solution)/shard_map/ppermute | solution.py:93
  76.4 2.1 %copy-start.13 = (bf16[64,2560]{1,0:T(8,128)(2,1)}, bf16[64,2560]{1,0:T(8,128)(2,1)S(1)}, u32[]{:S(2)}) copy-start(bf16[64,2560]{1,0:T(8,128)(2,1)S(1)} %collective-permute-done.12.refs_17_) | copy-start | bytes 983044
  76.4 34.4 %collective-permute-start.16 = (bf16[1024,512]{1,0:T(8,128)(2,1)S(1)}, bf16[1024,512]{1,0:T(8,128)(2,1)S(1)}, u32[]{:S(2)}, u32[]{:S(2)}) collective-permute-start(bf16[1024,512]{1,0:T(8,128)(2,1)S(1)} %pad_maximum_fusion.1), channel_id=1, source_target_pairs={{0,1},{1,0},{2,3},{3,2},{4,5},{5,4},{6,7},{7,6},{8,9},{9,8},{10,11... | collective-permute-start | bytes 3145736 | tf_op jit(solution)/shard_map/ppermute | solution.py:398
  77.0 1.6 copy-start.14
  77.0 53.0 %collective-permute-start = (bf16[1024,512]{1,0:T(8,128)(2,1)S(1)}, bf16[1024,512]{1,0:T(8,128)(2,1)S(1)}, u32[]{:S(2)}, u32[]{:S(2)}) collective-permute-start(bf16[1024,512]{1,0:T(8,128)(2,1)S(1)} %pad_maximum_fusion.2), channel_id=1, source_target_pairs={{0,1},{1,0},{2,3},{3,2},{4,5},{5,4},{6,7},{7,6},{8,9},{9,8},{10,11... | collective-permute-start | bytes 3145736 | tf_op jit(solution)/shard_map/ppermute | solution.py:398
  78.5 0.7 copy-start.15
  78.5 0.9 copy-start.16
  110.8 1.0 copy-start.7
  130.0 1.0 copy-start.6
  149.5 16.9 %copy-start = (bf16[512,2560]{1,0:T(8,128)(2,1)S(1)}, bf16[512,2560]{1,0:T(8,128)(2,1)}, u32[]{:S(2)}) copy-start(bf16[512,2560]{1,0:T(8,128)(2,1)} %get-tuple-element.32.refs_0_) | copy-start | bytes 7864324
  149.5 5.2 %collective-permute-start.19 = (bf16[512,2560]{1,0:T(8,128)(2,1)}, bf16[512,2560]{1,0:T(8,128)(2,1)S(1)}, u32[]{:S(2)}, u32[]{:S(2)}) collective-permute-start(bf16[512,2560]{1,0:T(8,128)(2,1)} %get-tuple-element.33), channel_id=1, source_target_pairs={{0,2},{2,0},{4,6},{6,4},{8,10},{10,8},{12,14},{14,12},{16,18},{18,... | collective-permute-start | bytes 7864328 | tf_op jit(solution)/shard_map/ppermute | solution.py:332
  149.6 48.3 %collective-permute-start.18 = (bf16[2048,512]{1,0:T(8,128)(2,1)}, bf16[2048,512]{1,0:T(8,128)(2,1)S(1)}, u32[]{:S(2)}, u32[]{:S(2)}) collective-permute-start(bf16[2048,512]{1,0:T(8,128)(2,1)} %get-tuple-element.31), channel_id=1, source_target_pairs={{0,1},{1,0},{2,3},{3,2},{4,5},{5,4},{6,7},{7,6},{8,9},{9,8},{10,11... | collective-permute-start | bytes 6291464 | tf_op jit(solution)/shard_map/ppermute | solution.py:406
  155.7 10.6 %collective-permute-start.21 = (bf16[64,2560]{1,0:T(8,128)(2,1)S(1)}, bf16[64,2560]{1,0:T(8,128)(2,1)S(1)}, u32[]{:S(2)}, u32[]{:S(2)}) collective-permute-start(bf16[64,2560]{1,0:T(8,128)(2,1)S(1)} %add_convert_fusion.3), channel_id=1, source_target_pairs={{0,4},{2,6},{4,0},{6,2},{8,12},{10,14},{12,8},{14,10},{16,20},{18,... | collective-permute-start | bytes 983048 | tf_op jit(solution)/shard_map/ppermute | solution.py:332
  157.6 22.8 %collective-permute-start.23 = (bf16[128,2560]{1,0:T(8,128)(2,1)S(1)}, bf16[128,2560]{1,0:T(8,128)(2,1)S(1)}, u32[]{:S(2)}, u32[]{:S(2)}) collective-permute-start(bf16[128,2560]{1,0:T(8,128)(2,1)S(1)} %add_convert_fusion.1), channel_id=1, source_target_pairs={{0,4},{2,6},{4,0},{6,2},{8,12},{10,14},{12,8},{14,10},{16,20},{18,... | collective-permute-start | bytes 1966088 | tf_op jit(solution)/shard_map/ppermute | solution.py:332
  166.6 31.3 %copy-start.1 = (bf16[2048,512]{1,0:T(8,128)(2,1)S(1)}, bf16[2048,512]{1,0:T(8,128)(2,1)}, u32[]{:S(2)}) copy-start(bf16[2048,512]{1,0:T(8,128)(2,1)} %get-tuple-element.30.kept_ref) | copy-start | bytes 6291460
  166.6 31.3 %collective-permute-start.20 = (bf16[64,2560]{1,0:T(8,128)(2,1)S(1)}, bf16[64,2560]{1,0:T(8,128)(2,1)S(1)}, u32[]{:S(2)}, u32[]{:S(2)}) collective-permute-start(bf16[64,2560]{1,0:T(8,128)(2,1)S(1)} %get-tuple-element.38), channel_id=1, source_target_pairs={{0,4},{2,6},{4,0},{6,2},{8,12},{10,14},{12,8},{14,10},{16,20},{18,... | collective-permute-start | bytes 983048 | tf_op jit(solution)/shard_map/ppermute | solution.py:332
  167.2 30.7 %collective-permute-start.22 = (bf16[64,2560]{1,0:T(8,128)(2,1)S(1)}, bf16[64,2560]{1,0:T(8,128)(2,1)S(1)}, u32[]{:S(2)}, u32[]{:S(2)}) collective-permute-start(bf16[64,2560]{1,0:T(8,128)(2,1)S(1)} %get-tuple-element.37), channel_id=1, source_target_pairs={{0,16},{2,18},{4,20},{6,22},{8,24},{10,26},{12,28},{14,30},{16,0},... | collective-permute-start | bytes 983048 | tf_op jit(solution)/shard_map/ppermute | solution.py:348
  180.7 17.2 %collective-permute-start.24 = (bf16[64,2560]{1,0:T(8,128)(2,1)S(1)}, bf16[64,2560]{1,0:T(8,128)(2,1)S(1)}, u32[]{:S(2)}, u32[]{:S(2)}) collective-permute-start(bf16[64,2560]{1,0:T(8,128)(2,1)S(1)} %get-tuple-element.44), channel_id=1, source_target_pairs={{0,24},{2,26},{4,28},{6,30},{8,0},{10,2},{12,4},{14,6},{16,8},{18,... | collective-permute-start | bytes 983048 | tf_op jit(solution)/shard_map/ppermute | solution.py:348
  181.4 16.5 %collective-permute-start.25 = (bf16[64,2560]{1,0:T(8,128)(2,1)S(1)}, bf16[64,2560]{1,0:T(8,128)(2,1)S(1)}, u32[]{:S(2)}, u32[]{:S(2)}) collective-permute-start(bf16[64,2560]{1,0:T(8,128)(2,1)S(1)} %get-tuple-element.43), channel_id=1, source_target_pairs={{0,8},{2,10},{4,12},{6,14},{8,16},{10,18},{12,20},{14,22},{16,24},... | collective-permute-start | bytes 983048 | tf_op jit(solution)/shard_map/ppermute | solution.py:348

commit v2 on v1

--- a/solution.py
+++ b/solution.py
@@ -9,6 +9,7 @@
 
 HEAD_DIM = 128
 SEQ_LEN = 128
+SLOTS = 128
 GROUPS = ((0, 2), (2, 1), (3, 1))
 
 eps = 1e-05
@@ -102,8 +103,8 @@
 
 def group_kernel(start, steps, first, last, heads, parts, users, *refs):
     refs = list(refs)
-    lens_ref, where_ref, xo_ref, do_ref, far_ref = refs[:5]
-    pieces, refs = refs[5 : 5 + users], refs[5 + users :]
+    where_ref, xo_ref, do_ref, far_ref = refs[:4]
+    pieces, refs = refs[4 : 4 + users], refs[4 + users :]
     acc_hbm = None if first else refs.pop(0)
     refs = refs if first else refs[2:]
     gx_ref, bs_ref = refs[:2]
@@ -114,6 +115,7 @@
     rows, own = xo_ref.shape
     width = own * parts
     cols_in = heads * 4 * HEAD_DIM
+    cols = cols_in + heads * HEAD_DIM
     histories = rows // SEQ_LEN
     me, user = where_ref[0], where_ref[1]
     step = pl.program_id(0)
@@ -161,7 +163,7 @@
     causal = lax.broadcasted_iota(jnp.int32, (SEQ_LEN, SEQ_LEN), 0) >= lax.broadcasted_iota(
         jnp.int32, (SEQ_LEN, SEQ_LEN), 1
     )
-    position = lax.broadcasted_iota(jnp.int32, (SEQ_LEN, 1), 0)
+    position = lax.broadcasted_iota(jnp.int32, (SEQ_LEN, 1), 0).astype(f32)
     half = min(2 * SEQ_LEN, rows)
     halves = [slice(lo, lo + half) for lo in range(0, rows, half)]
 
@@ -188,11 +190,19 @@
         c = slice(h * 4 * HEAD_DIM, (h + 1) * 4 * HEAD_DIM)
         silu, slope_s[:, c] = gates(dot_nn(nb_s[...], w_s[:, c]))
         g_s[:, c] = silu.astype(bf16)
+    table = w_s[:, cols:].astype(f32)
+    lengths = pltpu.roll(table, SLOTS // 2, 1)
+    lane = lax.broadcasted_iota(jnp.int32, (1, SLOTS), 1)
+    lengths = jnp.where(table == user.astype(f32), lengths, 0.0)
+    lengths = jnp.sum(lengths, axis=0, keepdims=True)
     for here in halves:
         base = start * histories + step * histories
         valid = jnp.concatenate(
             [
-                (position < lens_ref[base + n]).astype(f32)
+                (
+                    position
+                    < jnp.sum(jnp.where(lane == base + n, lengths, 0.0), axis=1, keepdims=True)
+                ).astype(f32)
                 for n in range(here.start // SEQ_LEN, here.stop // SEQ_LEN)
             ],
             axis=0,
@@ -204,7 +214,7 @@
         dm_s[here, own:] = dr
         dt_s[:own, here] = do.T
         dt_s[own:, here] = dr.T
-    dh_s[...] = dot_nn(dm_s[...], w_s[:, cols_in:])
+    dh_s[...] = dot_nn(dm_s[...], w_s[:, cols_in:cols])
 
     if not first:
         only(0, acc_load.wait)
@@ -267,19 +277,19 @@
         only(steps - 1, copy.wait)
 
 
-def group_call(group, blocks, users, parts, lens, where, x, d, far, pieces, past):
+def group_call(group, blocks, users, parts, where, x, d, far, pieces, past):
     start, steps = group
     first, last = start == 0, start + steps == blocks
     rows, own = x.shape[0] // blocks, x.shape[1]
-    width, cols = own * parts, pieces[0].shape[1]
+    width, cols = own * parts, pieces[0].shape[1] - SLOTS
     heads = cols // (5 * HEAD_DIM)
     cols_in = heads * 4 * HEAD_DIM
     smem = pl.BlockSpec(memory_space=pltpu.SMEM)
     anywhere = pl.BlockSpec(memory_space=pl.ANY)
     mine = pl.BlockSpec((rows, own), lambda i: (start + i, 0))
     theirs = pl.BlockSpec((2 * rows, width - own), lambda i: (i, 0))
-    args = [lens, where, x, d, far] + pieces + past
-    specs = [smem, smem, mine, mine, theirs] + [anywhere] * (users + len(past))
+    args = [where, x, d, far] + pieces + past
+    specs = [smem, mine, mine, theirs] + [anywhere] * (users + len(past))
     if last:
         grads = [jax.ShapeDtypeStruct((width // 2, cols), bf16)] * 2
     else:
@@ -299,9 +309,9 @@
             pl.BlockSpec((rows, width - own), lambda i: (start + i, 0)),
         ]
         + [anywhere] * len(grads),
-        input_output_aliases={} if first else {users + 6: 0, users + 7: 1},
+        input_output_aliases={} if first else {users + 5: 0, users + 6: 1},
         scratch_shapes=[
-            pltpu.VMEM((width, cols), bf16),
+            pltpu.VMEM((width, cols + SLOTS), bf16),
             pltpu.VMEM((width, cols), f32),
             pltpu.VMEM((rows, width), bf16),
             pltpu.VMEM((width, rows), bf16),
@@ -425,18 +435,17 @@
         ahead = jnp.concatenate([t[span] for span in spans for t in (x, d)], axis=0)
         far.append(exchange(ahead, tensor))
 
-    pieces = gather_parts(jnp.concatenate([w_in, w_out], axis=1), users)
-    slots = jnp.pad((slot_source * 256 + slot_length)[None], ((0, 7), (0, 128 - hist)))
-    table = lax.all_gather(slots, "user", axis=0, tiled=True)
-    table = table.reshape(users, 8, 128)[:, 0, :hist]
     user = lax.axis_index("user")
-    lens = jnp.sum(jnp.where(table // 256 == user, table % 256, 0), axis=0)
+    slots = jnp.stack([slot_source, slot_length]).astype(bf16)
+    slots = jnp.pad(slots, ((0, 0), (0, SLOTS // 2 - hist)), constant_values=-1)
+    slots = jnp.pad(slots.reshape(1, SLOTS), ((0, w_in.shape[0] - 1), (0, 0)), constant_values=-1)
+    pieces = gather_parts(jnp.concatenate([w_in, w_out, slots], axis=1), users)
     where = jnp.stack([lax.axis_index("tensor"), user]).astype(jnp.int32)
 
     past = []
     for group, theirs in zip(GROUPS, far):
         kept, bs, *grads = group_call(
-            group, blocks, users, tensor, lens, where, x, d, theirs, pieces, past
+            group, blocks, users, tensor, where, x, d, theirs, pieces, past
         )
         past = grads + [kept, bs]
     sent = give_back(bs, own, tensor)

time: 204 us -> 191 us (0.936)
  blocking collectives: 22.2 us -> 0 us
  starting transfers between devices: 21.6 us -> 29.6 us
  waiting for transfers between devices: 72.3 us -> 74.5 us
    all_gather x1 -> x0, blocking collectives: 22.2 us -> none  [local(): table = lax.all_gather(slots, 'user', axis=0, tiled=True)]
    ppermute x3, starting transfers between devices: 2.18 us -> 9.58 us  [scatter_parts(): moved.append(lax.ppermute(block, 'user', pairs))]
    ppermute x1, waiting for transfers between devices: 15.1 us -> 11.7 us  [give_back(): return lax.ppermute(block, 'tensor', [(0, 1), (1, 0)])]
    ppermute x16, waiting for transfers between devices: 37.9 us -> 40.7 us  [swap(): return lax.ppermute(block, 'user', [(i, i ^ bit) for i in range(users)])]
  transfers between devices with their start and end apart: 26 -> 26, of which waited for: 7 -> 9; matrix products, arithmetic and copies ran while one was open for 3% -> 3% of each run, Pallas kernels for 25% -> 27%
where the time goes in v2:
time: 191 us; the launch traced here: 188 us
  waiting for transfers between devices  74.5 us (39%)
  Pallas kernels  70.8 us (37%)
  starting transfers between devices  29.6 us (15%)
  local copies, waits for them, and re-layouts  6.35 us (3%)
  other arithmetic  4.95 us (3%)
    pallas_call x3, Pallas kernels, group_call(): pl.pallas_call(functools.partial(group_kernel, start, steps, first, last,...  68.4 us
    ppermute x16, waiting for transfers between devices, swap(): return lax.ppermute(block, 'user', [(i, i ^ bit) for i in range(users)])  40.7 us
    ppermute x3, waiting for transfers between devices, gather_parts(): pieces.append(lax.ppermute(shard, 'user', pairs))  20.3 us
    ppermute x1, waiting for transfers between devices, give_back(): return lax.ppermute(block, 'tensor', [(0, 1), (1, 0)])  11.7 us
    ppermute x16, starting transfers between devices, swap(): return lax.ppermute(block, 'user', [(i, i ^ bit) for i in range(users)])  9.95 us
    ppermute x3, starting transfers between devices, scatter_parts(): moved.append(lax.ppermute(block, 'user', pairs))  9.58 us
    ppermute x3, starting transfers between devices, exchange(): return lax.ppermute(block, 'tensor', [(0, 1), (1, 0)])  5.06 us
    ppermute x3, starting transfers between devices, gather_parts(): pieces.append(lax.ppermute(shard, 'user', pairs))  4.68 us
  transfers between devices with their start and end apart: 26, of which 9 were waited for; matrix products, arithmetic and copies ran while one was open for 3% of the time, Pallas kernels for 27%

profile of v2, /device:TPU:0, one launch (start us, length us, event | category | flops | bytes accessed | tf_op | source)
XLA Modules:
  0.0 187.6 jit_solution(120094950359478641)
XLA Ops:
  0.6 1.4 fusion.5
  2.1 0.5 copy-done.3
  2.5 0.1 fusion.6
  2.7 1.5 pad_maximum_fusion
  4.2 3.0 %collective-permute-start.17 = (bf16[2048,512]{1,0:T(8,128)(2,1)}, bf16[2048,512]{1,0:T(8,128)(2,1)}, u32[]{:S(2)}, u32[]{:S(2)}) collective-permute-start(bf16[2048,512]{1,0:T(8,128)(2,1)} %pad_maximum_fusion), channel_id=1, source_target_pairs={{0,1},{1,0},{2,3},{3,2},{4,5},{5,4},{6,7},{7,6},{8,9},{9,8},{10,11... | collective-permute-start | bytes 6291464 | tf_op jit(solution)/shard_map/ppermute | solution.py:408
  7.2 0.1 reshape.24
  7.3 2.7 %collective-permute-start.1 = (bf16[64,2688]{1,0:T(8,128)(2,1)S(1)}, bf16[64,2688]{1,0:T(8,128)(2,1)S(1)}, u32[]{:S(2)}, u32[]{:S(2)}) collective-permute-start(bf16[64,2688]{1,0:T(8,128)(2,1)S(1)} %fusion.1.refs_4_), channel_id=1, source_target_pairs={{0,16},{2,18},{4,20},{6,22},{8,24},{10,26},{12,28},{14,30},{16,0},... | collective-permute-start | bytes 1032200 | tf_op jit(solution)/shard_map/ppermute | solution.py:99
  9.9 1.3 collective-permute-start.2
  11.3 0.7 collective-permute-start.3
  12.0 1.5 collective-permute-start.4
  13.5 20.3 %collective-permute-done.1.refs_5_ = bf16[64,2688]{1,0:T(8,128)(2,1)S(1)} collective-permute-done((bf16[64,2688]{1,0:T(8,128)(2,1)S(1)}, bf16[64,2688]{1,0:T(8,128)(2,1)S(1)}, u32[]{:S(2)}, u32[]{:S(2)}) %collective-permute-start.1) | collective-permute-done | bytes 344096 | tf_op jit(solution)/shard_map/ppermute | solution.py:99
  33.8 1.6 collective-permute-start.5
  35.3 0.5 collective-permute-start.6
  35.9 1.5 collective-permute-start.7
  37.4 7.4 %collective-permute-done.5.refs_9_ = bf16[64,2688]{1,0:T(8,128)(2,1)} collective-permute-done((bf16[64,2688]{1,0:T(8,128)(2,1)S(1)}, bf16[64,2688]{1,0:T(8,128)(2,1)}, u32[]{:S(2)}, u32[]{:S(2)}) %collective-permute-start.5) | collective-permute-done | bytes 344096 | tf_op jit(solution)/shard_map/ppermute | solution.py:94
  44.8 7.4 %collective-permute-done.6.refs_10_ = bf16[64,2688]{1,0:T(8,128)(2,1)} collective-permute-done((bf16[64,2688]{1,0:T(8,128)(2,1)S(1)}, bf16[64,2688]{1,0:T(8,128)(2,1)}, u32[]{:S(2)}, u32[]{:S(2)}) %collective-permute-start.6) | collective-permute-done | bytes 344096 | tf_op jit(solution)/shard_map/ppermute | solution.py:94
  52.2 1.1 slice.81
  53.3 5.8 %collective-permute-done.7.refs_11_ = bf16[64,2688]{1,0:T(8,128)(2,1)} collective-permute-done((bf16[64,2688]{1,0:T(8,128)(2,1)S(1)}, bf16[64,2688]{1,0:T(8,128)(2,1)}, u32[]{:S(2)}, u32[]{:S(2)}) %collective-permute-start.7) | collective-permute-done | bytes 344096 | tf_op jit(solution)/shard_map/ppermute | solution.py:94
  59.1 0.5 collective-permute-start.13
  59.6 0.1 collective-permute-start.14
  59.7 0.5 collective-permute-start.15
  60.3 1.1 slice.83
  61.4 0.6 pad_add_fusion.refs_0_
  62.1 0.3 collective-permute-start.16
  62.4 1.8 collective-permute-start
  64.2 31.7 %shard_map.85 = (bf16[2048,512]{1,0:T(8,128)(2,1)}, bf16[2048,512]{1,0:T(8,128)(2,1)}, f32[1024,2560]{1,0:T(8,128)}) custom-call(s32[2]{0:T(128)} %pad_add_fusion.refs_0_, bf16[2048,512]{1,0:T(8,128)(2,1)} %bitcast.13, bf16[2048,512]{1,0:T(8,128)(2,1)} %bitcast.20, bf16[2048,512]{1,0:T(8,128)(2,1)} %collective-permute-done.17.refs_3_, ...), custom_call_target="tpu_custom_call" | custom-call | flops 15032385536 | bytes 16777216 | tf_op jit(solution)/shard_map/pallas_call | solution.py:298
  95.9 1.0 copy-done.10
  96.9 18.2 %shard_map.86 = (bf16[2048,512]{1,0:T(8,128)(2,1)}, bf16[2048,512]{1,0:T(8,128)(2,1)}, f32[1024,2560]{1,0:T(8,128)}) custom-call(s32[2]{0:T(128)} %pad_add_fusion.refs_0_, bf16[2048,512]{1,0:T(8,128)(2,1)} %bitcast.14, bf16[2048,512]{1,0:T(8,128)(2,1)} %bitcast.21, bf16[1024,512]{1,0:T(8,128)(2,1)} %copy-done.10, ...), custom_call_target="tpu_custom_call", output_to_operand_aliasing={{0}: (21, {}), {1}: (22, {})} | custom-call | flops 7516192768 | bytes 16777216 | tf_op jit(solution)/shard_map/pallas_call | solution.py:298
  115.1 1.0 copy-done.9
  116.0 18.5 %shard_map.87 = (bf16[2048,512]{1,0:T(8,128)(2,1)}, bf16[2048,512]{1,0:T(8,128)(2,1)}, bf16[512,2560]{1,0:T(8,128)(2,1)}, bf16[512,2560]{1,0:T(8,128)(2,1)}) custom-call(s32[2]{0:T(128)} %pad_add_fusion.refs_0_, bf16[2048,512]{1,0:T(8,128)(2,1)} %bitcast.15, bf16[2048,512]{1,0:T(8,128)(2,1)} %bitcast.22, ...), custom_call_target="tpu_custom_call", output_to_operand_aliasing={{0}: (21, {}), {1}: (22, {})} | custom-call | flops 7516192768 | bytes 16777216 | tf_op jit(solution)/shard_map/pallas_call | solution.py:298
  134.6 0.1 collective-permute-start.19
  134.6 0.3 collective-permute-start.18
  134.9 4.8 %collective-permute-done.19.refs_1_ = bf16[512,2560]{1,0:T(8,128)(2,1)S(1)} collective-permute-done((bf16[512,2560]{1,0:T(8,128)(2,1)}, bf16[512,2560]{1,0:T(8,128)(2,1)S(1)}, u32[]{:S(2)}, u32[]{:S(2)}) %collective-permute-start.19) | collective-permute-done | bytes 2621472 | tf_op jit(solution)/shard_map/ppermute | solution.py:342
  139.7 1.0 add_convert_fusion.3
  140.8 1.6 collective-permute-start.21
  142.4 1.2 add_convert_fusion.1
  143.6 0.6 collective-permute-start.23
  144.2 7.2 %collective-permute-done.21 = bf16[64,2560]{1,0:T(8,128)(2,1)S(1)} collective-permute-done((bf16[64,2560]{1,0:T(8,128)(2,1)S(1)}, bf16[64,2560]{1,0:T(8,128)(2,1)S(1)}, u32[]{:S(2)}, u32[]{:S(2)}) %collective-permute-start.21) | collective-permute-done | bytes 327712 | tf_op jit(solution)/shard_map/ppermute | solution.py:342
  151.4 0.2 add_convert_fusion.2
  151.6 1.6 collective-permute-start.20
  153.2 4.2 %collective-permute-start.22 = (bf16[64,2560]{1,0:T(8,128)(2,1)S(1)}, bf16[64,2560]{1,0:T(8,128)(2,1)S(1)}, u32[]{:S(2)}, u32[]{:S(2)}) collective-permute-start(bf16[64,2560]{1,0:T(8,128)(2,1)S(1)} %get-tuple-element.37), channel_id=1, source_target_pairs={{0,16},{2,18},{4,20},{6,22},{8,24},{10,26},{12,28},{14,30},{16,0},... | collective-permute-start | bytes 983048 | tf_op jit(solution)/shard_map/ppermute | solution.py:358
  157.4 8.1 %collective-permute-done.23 = bf16[128,2560]{1,0:T(8,128)(2,1)S(1)} collective-permute-done((bf16[128,2560]{1,0:T(8,128)(2,1)S(1)}, bf16[128,2560]{1,0:T(8,128)(2,1)S(1)}, u32[]{:S(2)}, u32[]{:S(2)}) %collective-permute-start.23) | collective-permute-done | bytes 655392 | tf_op jit(solution)/shard_map/ppermute | solution.py:342
  165.5 0.2 add_convert_fusion
  165.8 2.5 %collective-permute-start.24 = (bf16[64,2560]{1,0:T(8,128)(2,1)S(1)}, bf16[64,2560]{1,0:T(8,128)(2,1)S(1)}, u32[]{:S(2)}, u32[]{:S(2)}) collective-permute-start(bf16[64,2560]{1,0:T(8,128)(2,1)S(1)} %get-tuple-element.44), channel_id=1, source_target_pairs={{0,24},{2,26},{4,28},{6,30},{8,0},{10,2},{12,4},{14,6},{16,8},{18,... | collective-permute-start | bytes 983048 | tf_op jit(solution)/shard_map/ppermute | solution.py:358
  168.2 2.9 %collective-permute-start.25 = (bf16[64,2560]{1,0:T(8,128)(2,1)S(1)}, bf16[64,2560]{1,0:T(8,128)(2,1)S(1)}, u32[]{:S(2)}, u32[]{:S(2)}) collective-permute-start(bf16[64,2560]{1,0:T(8,128)(2,1)S(1)} %get-tuple-element.43), channel_id=1, source_target_pairs={{0,8},{2,10},{4,12},{6,14},{8,16},{10,18},{12,20},{14,22},{16,24},... | collective-permute-start | bytes 983048 | tf_op jit(solution)/shard_map/ppermute | solution.py:358
  171.2 11.7 %collective-permute-done.18.sent_ref = bf16[2048,512]{1,0:T(8,128)(2,1)S(1)} collective-permute-done((bf16[2048,512]{1,0:T(8,128)(2,1)}, bf16[2048,512]{1,0:T(8,128)(2,1)S(1)}, u32[]{:S(2)}, u32[]{:S(2)}) %collective-permute-start.18) | collective-permute-done | bytes 2097184 | tf_op jit(solution)/shard_map/ppermute | solution.py:416
  182.9 1.8 collective-permute-done.25.refs_5_
  184.7 2.4 %shard_map.88 = (bf16[2048,512]{1,0:T(8,128)(2,1)}, f32[64,2048]{1,0:T(8,128)}, f32[64,512]{1,0:T(8,128)}) custom-call(bf16[2048,512]{1,0:T(8,128)(2,1)S(1)} %copy-done.1, bf16[2048,512]{1,0:T(8,128)(2,1)S(1)} %collective-permute-done.18.sent_ref, bf16[512,2560]{1,0:T(8,128)(2,1)S(1)} %copy-done, bf16[512,2560]{1,0:T(8,128)(2,1)S(1)} %collective-permute-done.19.refs_1_, ...), custom_call_target="tpu_custom_call" | custom-call | flops 1048576 | bytes 12582912 | tf_op jit(solution)/shard_map/pallas_call | solution.py:385
  (57 shorter events, 0.4 us)
Async XLA Ops:
  0.6 1.9 %copy-start.3 = (bf16[16,128,512]{2,1,0:T(8,128)(2,1)S(1)}, bf16[16,128,512]{2,1,0:T(8,128)(2,1)}, u32[]{:S(2)}) copy-start(bf16[16,128,512]{2,1,0:T(8,128)(2,1)} %param.7) | copy-start | bytes 6291460
  2.6 4.5 %copy-start.7 = (s32[16]{0:T(128)S(1)}, s32[16]{0:T(128)}, u32[]{:S(2)}) copy-start(s32[16]{0:T(128)} %param.11) | copy-start | bytes 196
  2.7 4.5 %copy-start.8 = (s32[16]{0:T(128)S(1)}, s32[16]{0:T(128)}, u32[]{:S(2)}) copy-start(s32[16]{0:T(128)} %param.10) | copy-start | bytes 196
  2.7 4.6 %copy-start.5 = (bf16[64,2048]{1,0:T(8,128)(2,1)S(1)}, bf16[64,2048]{1,0:T(8,128)(2,1)}, u32[]{:S(2)}) copy-start(bf16[64,2048]{1,0:T(8,128)(2,1)} %param.8) | copy-start | bytes 786436
  2.7 4.6 %copy-start.6 = (bf16[64,512]{1,0:T(8,128)(2,1)S(1)}, bf16[64,512]{1,0:T(8,128)(2,1)}, u32[]{:S(2)}) copy-start(bf16[64,512]{1,0:T(8,128)(2,1)} %param.9) | copy-start | bytes 196612
  2.7 49.5 %copy-start.2 = (bf16[16,128,512]{2,1,0:T(8,128)(2,1)S(1)}, bf16[16,128,512]{2,1,0:T(8,128)(2,1)}, u32[]{:S(2)}) copy-start(bf16[16,128,512]{2,1,0:T(8,128)(2,1)} %param.6) | copy-start | bytes 6291460
  4.2 60.0 %collective-permute-start.17 = (bf16[2048,512]{1,0:T(8,128)(2,1)}, bf16[2048,512]{1,0:T(8,128)(2,1)}, u32[]{:S(2)}, u32[]{:S(2)}) collective-permute-start(bf16[2048,512]{1,0:T(8,128)(2,1)} %pad_maximum_fusion), channel_id=1, source_target_pairs={{0,1},{1,0},{2,3},{3,2},{4,5},{5,4},{6,7},{7,6},{8,9},{9,8},{10,11... | collective-permute-start | bytes 6291464 | tf_op jit(solution)/shard_map/ppermute | solution.py:408
  7.3 53.0 %copy-start.4 = (bf16[64,2688]{1,0:T(8,128)(2,1)}, bf16[64,2688]{1,0:T(8,128)(2,1)S(1)}, u32[]{:S(2)}) copy-start(bf16[64,2688]{1,0:T(8,128)(2,1)S(1)} %fusion.1.refs_4_) | copy-start | bytes 1032196
  7.3 26.4 %collective-permute-start.1 = (bf16[64,2688]{1,0:T(8,128)(2,1)S(1)}, bf16[64,2688]{1,0:T(8,128)(2,1)S(1)}, u32[]{:S(2)}, u32[]{:S(2)}) collective-permute-start(bf16[64,2688]{1,0:T(8,128)(2,1)S(1)} %fusion.1.refs_4_), channel_id=1, source_target_pairs={{0,16},{2,18},{4,20},{6,22},{8,24},{10,26},{12,28},{14,30},{16,0},... | collective-permute-start | bytes 1032200 | tf_op jit(solution)/shard_map/ppermute | solution.py:99
  9.9 23.8 %collective-permute-start.2 = (bf16[64,2688]{1,0:T(8,128)(2,1)S(1)}, bf16[64,2688]{1,0:T(8,128)(2,1)S(1)}, u32[]{:S(2)}, u32[]{:S(2)}) collective-permute-start(bf16[64,2688]{1,0:T(8,128)(2,1)S(1)} %fusion.1.refs_4_), channel_id=1, source_target_pairs={{0,24},{2,26},{4,28},{6,30},{8,0},{10,2},{12,4},{14,6},{16,8},{18,... | collective-permute-start | bytes 1032200 | tf_op jit(solution)/shard_map/ppermute | solution.py:99
  11.3 24.0 %collective-permute-start.3 = (bf16[64,2688]{1,0:T(8,128)(2,1)S(1)}, bf16[64,2688]{1,0:T(8,128)(2,1)S(1)}, u32[]{:S(2)}, u32[]{:S(2)}) collective-permute-start(bf16[64,2688]{1,0:T(8,128)(2,1)S(1)} %fusion.1.refs_4_), channel_id=1, source_target_pairs={{0,8},{2,10},{4,12},{6,14},{8,16},{10,18},{12,20},{14,22},{16,24},... | collective-permute-start | bytes 1032200 | tf_op jit(solution)/shard_map/ppermute | solution.py:99
  12.0 23.9 %collective-permute-start.4 = (bf16[64,2688]{1,0:T(8,128)(2,1)S(1)}, bf16[64,2688]{1,0:T(8,128)(2,1)}, u32[]{:S(2)}, u32[]{:S(2)}) collective-permute-start(bf16[64,2688]{1,0:T(8,128)(2,1)S(1)} %fusion.1.refs_4_), channel_id=1, source_target_pairs={{0,4},{2,6},{4,0},{6,2},{8,12},{10,14},{12,8},{14,10},{16,20},{18,... | collective-permute-start | bytes 1032200 | tf_op jit(solution)/shard_map/ppermute | solution.py:94
  33.7 25.9 %copy-start.11 = (bf16[64,2688]{1,0:T(8,128)(2,1)}, bf16[64,2688]{1,0:T(8,128)(2,1)S(1)}, u32[]{:S(2)}) copy-start(bf16[64,2688]{1,0:T(8,128)(2,1)S(1)} %collective-permute-done.1.refs_5_) | copy-start | bytes 1032196
  33.7 3.6 %collective-permute-start.8 = (bf16[64,2688]{1,0:T(8,128)(2,1)S(1)}, bf16[64,2688]{1,0:T(8,128)(2,1)S(1)}, u32[]{:S(2)}, u32[]{:S(2)}) collective-permute-start(bf16[64,2688]{1,0:T(8,128)(2,1)S(1)} %fusion.1.refs_4_), channel_id=1, source_target_pairs={{0,2},{2,0},{4,6},{6,4},{8,10},{10,8},{12,14},{14,12},{16,18},{18,... | collective-permute-start | bytes 1032200 | tf_op jit(solution)/shard_map/ppermute | solution.py:94
  33.7 25.9 %copy-start.12 = (bf16[64,2688]{1,0:T(8,128)(2,1)}, bf16[64,2688]{1,0:T(8,128)(2,1)S(1)}, u32[]{:S(2)}) copy-start(bf16[64,2688]{1,0:T(8,128)(2,1)S(1)} %collective-permute-done.2.refs_6_) | copy-start | bytes 1032196
  33.8 11.0 %collective-permute-start.5 = (bf16[64,2688]{1,0:T(8,128)(2,1)S(1)}, bf16[64,2688]{1,0:T(8,128)(2,1)}, u32[]{:S(2)}, u32[]{:S(2)}) collective-permute-start(bf16[64,2688]{1,0:T(8,128)(2,1)S(1)} %collective-permute-done.1.refs_5_), channel_id=1, source_target_pairs={{0,4},{2,6},{4,0},{6,2},{8,12},{10,14},{12,8},{14,10},{16,20},{18,... | collective-permute-start | bytes 1032200 | tf_op jit(solution)/shard_map/ppermute | solution.py:94
  35.3 24.4 %copy-start.13 = (bf16[64,2688]{1,0:T(8,128)(2,1)}, bf16[64,2688]{1,0:T(8,128)(2,1)S(1)}, u32[]{:S(2)}) copy-start(bf16[64,2688]{1,0:T(8,128)(2,1)S(1)} %collective-permute-done.3.refs_7_) | copy-start | bytes 1032196
  35.3 16.8 %collective-permute-start.6 = (bf16[64,2688]{1,0:T(8,128)(2,1)S(1)}, bf16[64,2688]{1,0:T(8,128)(2,1)}, u32[]{:S(2)}, u32[]{:S(2)}) collective-permute-start(bf16[64,2688]{1,0:T(8,128)(2,1)S(1)} %collective-permute-done.2.refs_6_), channel_id=1, source_target_pairs={{0,4},{2,6},{4,0},{6,2},{8,12},{10,14},{12,8},{14,10},{16,20},{18,... | collective-permute-start | bytes 1032200 | tf_op jit(solution)/shard_map/ppermute | solution.py:94
  35.9 23.2 %collective-permute-start.7 = (bf16[64,2688]{1,0:T(8,128)(2,1)S(1)}, bf16[64,2688]{1,0:T(8,128)(2,1)}, u32[]{:S(2)}, u32[]{:S(2)}) collective-permute-start(bf16[64,2688]{1,0:T(8,128)(2,1)S(1)} %collective-permute-done.3.refs_7_), channel_id=1, source_target_pairs={{0,4},{2,6},{4,0},{6,2},{8,12},{10,14},{12,8},{14,10},{16,20},{18,... | collective-permute-start | bytes 1032200 | tf_op jit(solution)/shard_map/ppermute | solution.py:94
  37.4 14.8 %copy-start.14 = (bf16[64,2688]{1,0:T(8,128)(2,1)}, bf16[64,2688]{1,0:T(8,128)(2,1)S(1)}, u32[]{:S(2)}) copy-start(bf16[64,2688]{1,0:T(8,128)(2,1)S(1)} %collective-permute-done.8.refs_12_) | copy-start | bytes 1032196
  37.4 21.7 %collective-permute-start.10 = (bf16[64,2688]{1,0:T(8,128)(2,1)S(1)}, bf16[64,2688]{1,0:T(8,128)(2,1)}, u32[]{:S(2)}, u32[]{:S(2)}) collective-permute-start(bf16[64,2688]{1,0:T(8,128)(2,1)S(1)} %collective-permute-done.2.refs_6_), channel_id=1, source_target_pairs={{0,2},{2,0},{4,6},{6,4},{8,10},{10,8},{12,14},{14,12},{16,18},{18,... | collective-permute-start | bytes 1032200 | tf_op jit(solution)/shard_map/ppermute | solution.py:94
  44.8 14.8 %collective-permute-start.11 = (bf16[64,2688]{1,0:T(8,128)(2,1)S(1)}, bf16[64,2688]{1,0:T(8,128)(2,1)}, u32[]{:S(2)}, u32[]{:S(2)}) collective-permute-start(bf16[64,2688]{1,0:T(8,128)(2,1)S(1)} %collective-permute-done.3.refs_7_), channel_id=1, source_target_pairs={{0,2},{2,0},{4,6},{6,4},{8,10},{10,8},{12,14},{14,12},{16,18},{18,... | collective-permute-start | bytes 1032200 | tf_op jit(solution)/shard_map/ppermute | solution.py:94
  52.2 7.5 %collective-permute-start.9 = (bf16[64,2688]{1,0:T(8,128)(2,1)S(1)}, bf16[64,2688]{1,0:T(8,128)(2,1)}, u32[]{:S(2)}, u32[]{:S(2)}) collective-permute-start(bf16[64,2688]{1,0:T(8,128)(2,1)S(1)} %collective-permute-done.1.refs_5_), channel_id=1, source_target_pairs={{0,2},{2,0},{4,6},{6,4},{8,10},{10,8},{12,14},{14,12},{16,18},{18,... | collective-permute-start | bytes 1032200 | tf_op jit(solution)/shard_map/ppermute | solution.py:94
  59.1 3.0 %collective-permute-start.12 = (bf16[64,2688]{1,0:T(8,128)(2,1)}, bf16[64,2688]{1,0:T(8,128)(2,1)}, u32[]{:S(2)}, u32[]{:S(2)}) collective-permute-start(bf16[64,2688]{1,0:T(8,128)(2,1)} %collective-permute-done.4.refs_8_), channel_id=1, source_target_pairs={{0,2},{2,0},{4,6},{6,4},{8,10},{10,8},{12,14},{14,12},{16,18},{18,... | collective-permute-start | bytes 1032200 | tf_op jit(solution)/shard_map/ppermute | solution.py:94
  59.1 3.3 %collective-permute-start.13 = (bf16[64,2688]{1,0:T(8,128)(2,1)}, bf16[64,2688]{1,0:T(8,128)(2,1)}, u32[]{:S(2)}, u32[]{:S(2)}) collective-permute-start(bf16[64,2688]{1,0:T(8,128)(2,1)} %collective-permute-done.5.refs_9_), channel_id=1, source_target_pairs={{0,2},{2,0},{4,6},{6,4},{8,10},{10,8},{12,14},{14,12},{16,18},{18,... | collective-permute-start | bytes 1032200 | tf_op jit(solution)/shard_map/ppermute | solution.py:94
  59.6 4.6 %collective-permute-start.14 = (bf16[64,2688]{1,0:T(8,128)(2,1)}, bf16[64,2688]{1,0:T(8,128)(2,1)}, u32[]{:S(2)}, u32[]{:S(2)}) collective-permute-start(bf16[64,2688]{1,0:T(8,128)(2,1)} %collective-permute-done.6.refs_10_), channel_id=1, source_target_pairs={{0,2},{2,0},{4,6},{6,4},{8,10},{10,8},{12,14},{14,12},{16,18},{18,... | collective-permute-start | bytes 1032200 | tf_op jit(solution)/shard_map/ppermute | solution.py:94
  59.7 4.5 %collective-permute-start.15 = (bf16[64,2688]{1,0:T(8,128)(2,1)}, bf16[64,2688]{1,0:T(8,128)(2,1)}, u32[]{:S(2)}, u32[]{:S(2)}) collective-permute-start(bf16[64,2688]{1,0:T(8,128)(2,1)} %collective-permute-done.7.refs_11_), channel_id=1, source_target_pairs={{0,2},{2,0},{4,6},{6,4},{8,10},{10,8},{12,14},{14,12},{16,18},{18,... | collective-permute-start | bytes 1032200 | tf_op jit(solution)/shard_map/ppermute | solution.py:94
  62.1 33.8 %collective-permute-start.16 = (bf16[1024,512]{1,0:T(8,128)(2,1)S(1)}, bf16[1024,512]{1,0:T(8,128)(2,1)S(1)}, u32[]{:S(2)}, u32[]{:S(2)}) collective-permute-start(bf16[1024,512]{1,0:T(8,128)(2,1)S(1)} %pad_maximum_fusion.1), channel_id=1, source_target_pairs={{0,1},{1,0},{2,3},{3,2},{4,5},{5,4},{6,7},{7,6},{8,9},{9,8},{10,11... | collective-permute-start | bytes 3145736 | tf_op jit(solution)/shard_map/ppermute | solution.py:408
  62.4 52.7 %collective-permute-start = (bf16[1024,512]{1,0:T(8,128)(2,1)S(1)}, bf16[1024,512]{1,0:T(8,128)(2,1)S(1)}, u32[]{:S(2)}, u32[]{:S(2)}) collective-permute-start(bf16[1024,512]{1,0:T(8,128)(2,1)S(1)} %pad_maximum_fusion.2), channel_id=1, source_target_pairs={{0,1},{1,0},{2,3},{3,2},{4,5},{5,4},{6,7},{7,6},{8,9},{9,8},{10,11... | collective-permute-start | bytes 3145736 | tf_op jit(solution)/shard_map/ppermute | solution.py:408
  95.9 1.0 copy-start.10
  115.1 1.0 copy-start.9
  134.6 16.9 %copy-start = (bf16[512,2560]{1,0:T(8,128)(2,1)S(1)}, bf16[512,2560]{1,0:T(8,128)(2,1)}, u32[]{:S(2)}) copy-start(bf16[512,2560]{1,0:T(8,128)(2,1)} %get-tuple-element.32.refs_0_) | copy-start | bytes 7864324
  134.6 5.2 %collective-permute-start.19 = (bf16[512,2560]{1,0:T(8,128)(2,1)}, bf16[512,2560]{1,0:T(8,128)(2,1)S(1)}, u32[]{:S(2)}, u32[]{:S(2)}) collective-permute-start(bf16[512,2560]{1,0:T(8,128)(2,1)} %get-tuple-element.33), channel_id=1, source_target_pairs={{0,2},{2,0},{4,6},{6,4},{8,10},{10,8},{12,14},{14,12},{16,18},{18,... | collective-permute-start | bytes 7864328 | tf_op jit(solution)/shard_map/ppermute | solution.py:342
  134.6 48.3 %collective-permute-start.18 = (bf16[2048,512]{1,0:T(8,128)(2,1)}, bf16[2048,512]{1,0:T(8,128)(2,1)S(1)}, u32[]{:S(2)}, u32[]{:S(2)}) collective-permute-start(bf16[2048,512]{1,0:T(8,128)(2,1)} %get-tuple-element.31), channel_id=1, source_target_pairs={{0,1},{1,0},{2,3},{3,2},{4,5},{5,4},{6,7},{7,6},{8,9},{9,8},{10,11... | collective-permute-start | bytes 6291464 | tf_op jit(solution)/shard_map/ppermute | solution.py:416
  140.8 10.6 %collective-permute-start.21 = (bf16[64,2560]{1,0:T(8,128)(2,1)S(1)}, bf16[64,2560]{1,0:T(8,128)(2,1)S(1)}, u32[]{:S(2)}, u32[]{:S(2)}) collective-permute-start(bf16[64,2560]{1,0:T(8,128)(2,1)S(1)} %add_convert_fusion.3), channel_id=1, source_target_pairs={{0,4},{2,6},{4,0},{6,2},{8,12},{10,14},{12,8},{14,10},{16,20},{18,... | collective-permute-start | bytes 983048 | tf_op jit(solution)/shard_map/ppermute | solution.py:342
  143.6 21.9 %collective-permute-start.23 = (bf16[128,2560]{1,0:T(8,128)(2,1)S(1)}, bf16[128,2560]{1,0:T(8,128)(2,1)S(1)}, u32[]{:S(2)}, u32[]{:S(2)}) collective-permute-start(bf16[128,2560]{1,0:T(8,128)(2,1)S(1)} %add_convert_fusion.1), channel_id=1, source_target_pairs={{0,4},{2,6},{4,0},{6,2},{8,12},{10,14},{12,8},{14,10},{16,20},{18,... | collective-permute-start | bytes 1966088 | tf_op jit(solution)/shard_map/ppermute | solution.py:342
  151.6 33.1 %copy-start.1 = (bf16[2048,512]{1,0:T(8,128)(2,1)S(1)}, bf16[2048,512]{1,0:T(8,128)(2,1)}, u32[]{:S(2)}) copy-start(bf16[2048,512]{1,0:T(8,128)(2,1)} %get-tuple-element.30.kept_ref) | copy-start | bytes 6291460
  151.6 31.3 %collective-permute-start.20 = (bf16[64,2560]{1,0:T(8,128)(2,1)S(1)}, bf16[64,2560]{1,0:T(8,128)(2,1)S(1)}, u32[]{:S(2)}, u32[]{:S(2)}) collective-permute-start(bf16[64,2560]{1,0:T(8,128)(2,1)S(1)} %get-tuple-element.38), channel_id=1, source_target_pairs={{0,4},{2,6},{4,0},{6,2},{8,12},{10,14},{12,8},{14,10},{16,20},{18,... | collective-permute-start | bytes 983048 | tf_op jit(solution)/shard_map/ppermute | solution.py:342
  153.2 29.7 %collective-permute-start.22 = (bf16[64,2560]{1,0:T(8,128)(2,1)S(1)}, bf16[64,2560]{1,0:T(8,128)(2,1)S(1)}, u32[]{:S(2)}, u32[]{:S(2)}) collective-permute-start(bf16[64,2560]{1,0:T(8,128)(2,1)S(1)} %get-tuple-element.37), channel_id=1, source_target_pairs={{0,16},{2,18},{4,20},{6,22},{8,24},{10,26},{12,28},{14,30},{16,0},... | collective-permute-start | bytes 983048 | tf_op jit(solution)/shard_map/ppermute | solution.py:358
  165.8 17.2 %collective-permute-start.24 = (bf16[64,2560]{1,0:T(8,128)(2,1)S(1)}, bf16[64,2560]{1,0:T(8,128)(2,1)S(1)}, u32[]{:S(2)}, u32[]{:S(2)}) collective-permute-start(bf16[64,2560]{1,0:T(8,128)(2,1)S(1)} %get-tuple-element.44), channel_id=1, source_target_pairs={{0,24},{2,26},{4,28},{6,30},{8,0},{10,2},{12,4},{14,6},{16,8},{18,... | collective-permute-start | bytes 983048 | tf_op jit(solution)/shard_map/ppermute | solution.py:358
  168.2 16.4 %collective-permute-start.25 = (bf16[64,2560]{1,0:T(8,128)(2,1)S(1)}, bf16[64,2560]{1,0:T(8,128)(2,1)S(1)}, u32[]{:S(2)}, u32[]{:S(2)}) collective-permute-start(bf16[64,2560]{1,0:T(8,128)(2,1)S(1)} %get-tuple-element.43), channel_id=1, source_target_pairs={{0,8},{2,10},{4,12},{6,14},{8,16},{10,18},{12,20},{14,22},{16,24},... | collective-permute-start | bytes 983048 | tf_op jit(solution)/shard_map/ppermute | solution.py:358

commit v3 on v2

--- a/solution.py
+++ b/solution.py
@@ -84,27 +84,42 @@
     return rest + [0]
 
 
-def piece_order(far):
-    slow = [0] + split_order(far)[:-1]
-    return [(j, xs, cs) for cs in range(2) for xs in range(2) for j in slow]
-
-
-def gather_parts(shard, users):
+def piece_order(far, cut):
+    slow = split_order(far)[:-1]
+    return [
+        (lo, [(j, xs, cs) for j in js])
+        for lo, js in ((0, [0]), (0, slow), (cut, slow))
+        for cs in range(2)
+        for xs in range(2)
+    ]
+
+
+def gather_parts(shard, cut, users, user):
     def swap(block, bit):
         return lax.ppermute(block, "user", [(i, i ^ bit) for i in range(users)])
 
-    pieces = [shard]
-    for j in split_order(users // 4)[:-1]:
-        pairs = [(i, (i - 4 * j) % users) for i in range(users)]
-        pieces.append(lax.ppermute(shard, "user", pairs))
-    pieces += [swap(piece, 2) for piece in pieces]
-    return pieces + [swap(piece, 1) for piece in pieces]
+    def spread(block):
+        across = swap(block, 2)
+        return [block, across, swap(block, 1), swap(across, 1)]
+
+    arrays, moved = spread(shard), []
+    for part in (shard[:, :cut], shard[:, cut:]):
+        if moved:
+            part = jnp.where(user < 0, sum(t[:1, :1] for t in moved), part)
+        moved = []
+        for j in split_order(users // 4)[:-1]:
+            pairs = [(i, (i - 4 * j) % users) for i in range(users)]
+            moved.append(lax.ppermute(part, "user", pairs))
+        block = jnp.concatenate(moved, axis=0)
+        block = jnp.where(user < 0, arrays[-3][:1, :1], block)
+        arrays += spread(block)
+    return arrays
 
 
 def group_kernel(start, steps, first, last, heads, parts, users, *refs):
     refs = list(refs)
     where_ref, xo_ref, do_ref, far_ref = refs[:4]
-    pieces, refs = refs[4 : 4 + users], refs[4 + users :]
+    pieces, refs = refs[4:16], refs[16:]
     acc_hbm = None if first else refs.pop(0)
     refs = refs if first else refs[2:]
     gx_ref, bs_ref = refs[:2]
@@ -139,12 +154,13 @@
         return pl.ds(pl.multiple_of(row, size), size)
 
     loads = []
-    for piece, (j, xs, cs) in zip(pieces, piece_order(far)):
-        loads.append(
-            pltpu.make_async_copy(piece, w_s.at[rows_of(j, xs, cs)], load_sems.at[len(loads)])
-        )
+    for piece, (lo, offsets) in zip(pieces, piece_order(far, pieces[4].shape[1])):
+        for at, offset in enumerate(offsets):
+            there = w_s.at[rows_of(*offset), pl.ds(lo, piece.shape[1])]
+            here = piece.at[pl.ds(at * size, size)]
+            loads.append(pltpu.make_async_copy(here, there, load_sems.at[len(loads)]))
     if not first:
-        acc_load = pltpu.make_async_copy(acc_hbm, acc_s, load_sems.at[users])
+        acc_load = pltpu.make_async_copy(acc_hbm, acc_s, load_sems.at[2 * users])
 
     def begin():
         for copy in loads:
@@ -256,12 +272,14 @@
     stride = max(1, 8 // histories)
     for lo in range(0, heads, stride):
         hi = min(lo + stride, heads)
-        pairs = [(h, n) for h in range(lo, hi) for n in range(histories)]
-        attention(pairs, causal, g_s, dh_s, slope_s, hb_s, dz_s)
+        units = [(h, n) for h in range(lo, hi) for n in range(histories)]
+        attention(units, causal, g_s, dh_s, slope_s, hb_s, dz_s)
         for h in range(max(0, lo - stride), lo):
             add(nt_s, dz_s.at[:, h * block : (h + 1) * block], h * block, block)
+    for h in range((heads - 1) // stride * stride, heads):
+        add(nt_s, dz_s.at[:, h * block : (h + 1) * block], h * block, block)
+    add(dt_s, hb_s, cols_in, heads * HEAD_DIM)
     dn_all = dot_nt(dz_s[...], w_s[:, :cols_in])
-    add(dt_s, hb_s, cols_in, heads * HEAD_DIM)
     for here, rstd in zip(halves, rstds):
         dn = dn_all[here, :]
         nf = nb_s[here, :].astype(f32)
@@ -270,8 +288,6 @@
         branch = (dn - one - nf * two) * rstd
         gx_ref[here, :] = (dm_s[here, :own].astype(f32) + branch[:, :own]).astype(bf16)
         bs_ref[here, :] = branch[:, own:].astype(bf16)
-    for h in range((heads - 1) // stride * stride, heads):
-        add(nt_s, dz_s.at[:, h * block : (h + 1) * block], h * block, block)
 
     for copy in stores:
         only(steps - 1, copy.wait)
@@ -281,7 +297,8 @@
     start, steps = group
     first, last = start == 0, start + steps == blocks
     rows, own = x.shape[0] // blocks, x.shape[1]
-    width, cols = own * parts, pieces[0].shape[1] - SLOTS
+    width = own * parts
+    cols = pieces[0].shape[1] - SLOTS
     heads = cols // (5 * HEAD_DIM)
     cols_in = heads * 4 * HEAD_DIM
     smem = pl.BlockSpec(memory_space=pltpu.SMEM)
@@ -289,7 +306,7 @@
     mine = pl.BlockSpec((rows, own), lambda i: (start + i, 0))
     theirs = pl.BlockSpec((2 * rows, width - own), lambda i: (i, 0))
     args = [where, x, d, far] + pieces + past
-    specs = [smem, mine, mine, theirs] + [anywhere] * (users + len(past))
+    specs = [smem, mine, mine, theirs] + [anywhere] * (len(pieces) + len(past))
     if last:
         grads = [jax.ShapeDtypeStruct((width // 2, cols), bf16)] * 2
     else:
@@ -309,7 +326,7 @@
             pl.BlockSpec((rows, width - own), lambda i: (start + i, 0)),
         ]
         + [anywhere] * len(grads),
-        input_output_aliases={} if first else {users + 5: 0, users + 6: 1},
+        input_output_aliases={} if first else {len(pieces) + 5: 0, len(pieces) + 6: 1},
         scratch_shapes=[
             pltpu.VMEM((width, cols + SLOTS), bf16),
             pltpu.VMEM((width, cols), f32),
@@ -323,7 +340,7 @@
             pltpu.VMEM((rows, cols_in), f32),
             pltpu.VMEM((rows, cols - cols_in), f32),
             pltpu.VMEM((width, cols) if last else (16, 128), bf16),
-            pltpu.SemaphoreType.DMA((users + 1,)),
+            pltpu.SemaphoreType.DMA((2 * users + 1,)),
             pltpu.SemaphoreType.DMA(((users if last else 1) * (heads + 1),)),
         ],
         compiler_params=pltpu.CompilerParams(vmem_limit_bytes=56 * 2**20),
@@ -439,7 +456,8 @@
     slots = jnp.stack([slot_source, slot_length]).astype(bf16)
     slots = jnp.pad(slots, ((0, 0), (0, SLOTS // 2 - hist)), constant_values=-1)
     slots = jnp.pad(slots.reshape(1, SLOTS), ((0, w_in.shape[0] - 1), (0, 0)), constant_values=-1)
-    pieces = gather_parts(jnp.concatenate([w_in, w_out, slots], axis=1), users)
+    shard = jnp.concatenate([w_in, w_out, slots], axis=1)
+    pieces = gather_parts(shard, shard.shape[1] // 256 * 128, users, user)
     where = jnp.stack([lax.axis_index("tensor"), user]).astype(jnp.int32)
 
     past = []

time: 191 us -> 186 us (0.974)
  waiting for transfers between devices: 74.5 us -> 54.1 us
  starting transfers between devices: 29.6 us -> 37.4 us
  other arithmetic: 4.95 us -> 9.68 us
  local copies, waits for them, and re-layouts: 6.35 us -> 10.8 us
  Pallas kernels: 70.8 us -> 67.4 us
    ppermute x3 -> x6, waiting for transfers between devices: 20.3 us -> 6.54 us  [gather_parts(): moved.append(lax.ppermute(part, 'user', pairs))]
    ppermute x3 -> x6, starting transfers between devices: 4.68 us -> 13.2 us  [gather_parts(): moved.append(lax.ppermute(part, 'user', pairs))]
    ppermute x16 -> x13, waiting for transfers between devices: 40.7 us -> 32.9 us  [swap(): return lax.ppermute(block, 'user', [(i, i ^ bit) for i in range(users)])]
    slice x0 -> x6, local copies, waits for them, and re-layouts: none -> 4.4 us  [the longest x2 1.79 us: gather_parts(): block = jnp.where(user < 0, arrays[-3][:1, :1], block)]
    pallas_call x3, Pallas kernels: 68.4 us -> 65 us  [group_call(): pl.pallas_call(functools.partial(group_kernel, start, steps, first, last,...]
    select_n x0 -> x3, other arithmetic: none -> 3.06 us  [the longest x2 3.04 us: gather_parts(): block = jnp.where(user < 0, arrays[-3][:1, :1], block)]
    ppermute x16 -> x13, starting transfers between devices: 9.95 us -> 8.66 us  [swap(): return lax.ppermute(block, 'user', [(i, i ^ bit) for i in range(users)])]
  transfers between devices with their start and end apart: 26 -> 26, of which waited for: 9 -> 9; matrix products, arithmetic and copies ran while one was open for 3% -> 9% of each run, Pallas kernels for 27% -> 26%
where the time goes in v3:
time: 186 us; the launch traced here: 183 us
  Pallas kernels  67.4 us (36%)
  waiting for transfers between devices  54.1 us (29%)
  starting transfers between devices  37.4 us (20%)
  local copies, waits for them, and re-layouts  10.8 us (6%)
  other arithmetic  9.68 us (5%)
  between operations  3.21 us (2%)
    pallas_call x3, Pallas kernels, group_call(): pl.pallas_call(functools.partial(group_kernel, start, steps, first, last,...  65 us
    ppermute x13, waiting for transfers between devices, swap(): return lax.ppermute(block, 'user', [(i, i ^ bit) for i in range(users)])  32.9 us
    ppermute x6, starting transfers between devices, gather_parts(): moved.append(lax.ppermute(part, 'user', pairs))  13.2 us
    ppermute x1, waiting for transfers between devices, give_back(): return lax.ppermute(block, 'tensor', [(0, 1), (1, 0)])  11.6 us
    ppermute x3, starting transfers between devices, scatter_parts(): moved.append(lax.ppermute(block, 'user', pairs))  10.3 us
    ppermute x13, starting transfers between devices, swap(): return lax.ppermute(block, 'user', [(i, i ^ bit) for i in range(users)])  8.66 us
    ppermute x6, waiting for transfers between devices, gather_parts(): moved.append(lax.ppermute(part, 'user', pairs))  6.54 us
  transfers between devices with their start and end apart: 26, of which 9 were waited for; matrix products, arithmetic and copies ran while one was open for 9% of the time, Pallas kernels for 26%

profile of v3, /device:TPU:0, one launch (start us, length us, event | category | flops | bytes accessed | tf_op | source)
XLA Modules:
  0.0 182.7 jit_solution(4177970159086553968)
XLA Ops:
  0.6 1.1 slice.106
  1.7 4.1 %collective-permute-start.4 = (bf16[64,1280]{1,0:T(8,128)(2,1)S(1)}, bf16[64,1280]{1,0:T(8,128)(2,1)S(1)}, u32[]{:S(2)}, u32[]{:S(2)}) collective-permute-start(bf16[64,1280]{1,0:T(8,128)(2,1)S(1)} %slice.106), channel_id=1, source_target_pairs={{0,16},{2,18},{4,20},{6,22},{8,24},{10,26},{12,28},{14,30},{16,0},... | collective-permute-start | bytes 491528 | tf_op jit(solution)/shard_map/ppermute | solution.py:112
  5.8 1.3 collective-permute-start.5
  7.2 0.7 collective-permute-start.6
  7.9 0.7 convert_bitcast_fusion
  8.6 1.0 fusion.1.refs_4_
  9.7 1.6 collective-permute-start.1
  11.2 1.3 fusion.5
  12.6 1.5 pad_maximum_fusion
  14.0 1.5 collective-permute-start.17
  15.6 0.5 slice.126
  18.3 0.5 slice.128
  19.5 0.6 slice.124
  20.1 1.5 maximum_select_fusion.1.refs_8_
  21.6 1.5 collective-permute-start.7
  23.1 5.0 %collective-permute-start.10 = (bf16[64,1408]{1,0:T(8,128)(2,1)S(1)}, bf16[64,1408]{1,0:T(8,128)(2,1)S(1)}, u32[]{:S(2)}, u32[]{:S(2)}) collective-permute-start(bf16[64,1408]{1,0:T(8,128)(2,1)S(1)} %slice_select_fusion), channel_id=1, source_target_pairs={{0,16},{2,18},{4,20},{6,22},{8,24},{10,26},{12,28},{14,30},{16,0},... | collective-permute-start | bytes 540680 | tf_op jit(solution)/shard_map/ppermute | solution.py:112
  28.2 2.0 %collective-permute-start.11 = (bf16[64,1408]{1,0:T(8,128)(2,1)S(1)}, bf16[64,1408]{1,0:T(8,128)(2,1)S(1)}, u32[]{:S(2)}, u32[]{:S(2)}) collective-permute-start(bf16[64,1408]{1,0:T(8,128)(2,1)S(1)} %slice_select_fusion), channel_id=1, source_target_pairs={{0,24},{2,26},{4,28},{6,30},{8,0},{10,2},{12,4},{14,6},{16,8},{18,... | collective-permute-start | bytes 540680 | tf_op jit(solution)/shard_map/ppermute | solution.py:112
  30.2 3.8 %collective-permute-done.7.refs_9_ = bf16[192,1280]{1,0:T(8,128)(2,1)} collective-permute-done((bf16[192,1280]{1,0:T(8,128)(2,1)}, bf16[192,1280]{1,0:T(8,128)(2,1)}, u32[]{:S(2)}, u32[]{:S(2)}) %collective-permute-start.7) | collective-permute-done | bytes 491552 | tf_op jit(solution)/shard_map/ppermute | solution.py:99
  34.0 1.2 slice.125
  35.2 6.1 %collective-permute-done.10 = bf16[64,1408]{1,0:T(8,128)(2,1)S(1)} collective-permute-done((bf16[64,1408]{1,0:T(8,128)(2,1)S(1)}, bf16[64,1408]{1,0:T(8,128)(2,1)S(1)}, u32[]{:S(2)}, u32[]{:S(2)}) %collective-permute-start.10) | collective-permute-done | bytes 180256 | tf_op jit(solution)/shard_map/ppermute | solution.py:112
  41.3 1.5 maximum_select_fusion.refs_12_
  42.8 0.8 collective-permute-start.13
  44.1 10.8 %collective-permute-done.13.refs_13_ = bf16[192,1408]{1,0:T(8,128)(2,1)} collective-permute-done((bf16[192,1408]{1,0:T(8,128)(2,1)}, bf16[192,1408]{1,0:T(8,128)(2,1)}, u32[]{:S(2)}, u32[]{:S(2)}) %collective-permute-start.13) | collective-permute-done | bytes 540704 | tf_op jit(solution)/shard_map/ppermute | solution.py:99
  55.4 0.8 copy-done.9
  56.3 1.1 slice.102
  57.5 1.1 slice.104
  58.6 0.6 pad_add_fusion.refs_0_
  59.3 1.6 collective-permute-start.16
  61.4 30.2 %shard_map.85 = (bf16[2048,512]{1,0:T(8,128)(2,1)}, bf16[2048,512]{1,0:T(8,128)(2,1)}, f32[1024,2560]{1,0:T(8,128)}) custom-call(s32[2]{0:T(128)} %pad_add_fusion.refs_0_, bf16[2048,512]{1,0:T(8,128)(2,1)} %bitcast.16, bf16[2048,512]{1,0:T(8,128)(2,1)} %bitcast.23, bf16[2048,512]{1,0:T(8,128)(2,1)} %collective-permute-done.17.refs_3_, ...), custom_call_target="tpu_custom_call" | custom-call | flops 15032385536 | bytes 16777216 | tf_op jit(solution)/shard_map/pallas_call | solution.py:315
  91.7 1.0 copy-done.6
  92.6 17.0 %shard_map.86 = (bf16[2048,512]{1,0:T(8,128)(2,1)}, bf16[2048,512]{1,0:T(8,128)(2,1)}, f32[1024,2560]{1,0:T(8,128)}) custom-call(s32[2]{0:T(128)} %pad_add_fusion.refs_0_, bf16[2048,512]{1,0:T(8,128)(2,1)} %bitcast.17, bf16[2048,512]{1,0:T(8,128)(2,1)} %bitcast.24, bf16[1024,512]{1,0:T(8,128)(2,1)} %copy-done.6, ...), custom_call_target="tpu_custom_call", output_to_operand_aliasing={{0}: (17, {}), {1}: (18, {})} | custom-call | flops 7516192768 | bytes 16777216 | tf_op jit(solution)/shard_map/pallas_call | solution.py:315
  109.6 1.0 copy-done.5
  110.6 17.8 %shard_map.87 = (bf16[2048,512]{1,0:T(8,128)(2,1)}, bf16[2048,512]{1,0:T(8,128)(2,1)}, bf16[512,2560]{1,0:T(8,128)(2,1)}, bf16[512,2560]{1,0:T(8,128)(2,1)}) custom-call(s32[2]{0:T(128)} %pad_add_fusion.refs_0_, bf16[2048,512]{1,0:T(8,128)(2,1)} %bitcast.18, bf16[2048,512]{1,0:T(8,128)(2,1)} %bitcast.25, ...), custom_call_target="tpu_custom_call", output_to_operand_aliasing={{0}: (17, {}), {1}: (18, {})} | custom-call | flops 7516192768 | bytes 16777216 | tf_op jit(solution)/shard_map/pallas_call | solution.py:315
  128.5 1.6 collective-permute-start.18
  130.1 3.5 %collective-permute-done.19.refs_1_ = bf16[512,2560]{1,0:T(8,128)(2,1)S(1)} collective-permute-done((bf16[512,2560]{1,0:T(8,128)(2,1)}, bf16[512,2560]{1,0:T(8,128)(2,1)S(1)}, u32[]{:S(2)}, u32[]{:S(2)}) %collective-permute-start.19) | collective-permute-done | bytes 2621472 | tf_op jit(solution)/shard_map/ppermute | solution.py:359
  133.6 1.0 add_convert_fusion.3
  134.7 1.4 collective-permute-start.21
  136.1 1.2 add_convert_fusion.1
  137.3 0.7 collective-permute-start.23
  138.1 7.2 %collective-permute-done.21 = bf16[64,2560]{1,0:T(8,128)(2,1)S(1)} collective-permute-done((bf16[64,2560]{1,0:T(8,128)(2,1)S(1)}, bf16[64,2560]{1,0:T(8,128)(2,1)S(1)}, u32[]{:S(2)}, u32[]{:S(2)}) %collective-permute-start.21) | collective-permute-done | bytes 327712 | tf_op jit(solution)/shard_map/ppermute | solution.py:359
  145.5 1.4 collective-permute-start.20
  146.9 4.8 %collective-permute-start.22 = (bf16[64,2560]{1,0:T(8,128)(2,1)S(1)}, bf16[64,2560]{1,0:T(8,128)(2,1)S(1)}, u32[]{:S(2)}, u32[]{:S(2)}) collective-permute-start(bf16[64,2560]{1,0:T(8,128)(2,1)S(1)} %get-tuple-element.37), channel_id=1, source_target_pairs={{0,16},{2,18},{4,20},{6,22},{8,24},{10,26},{12,28},{14,30},{16,0},... | collective-permute-start | bytes 983048 | tf_op jit(solution)/shard_map/ppermute | solution.py:375
  151.7 7.6 %collective-permute-done.23 = bf16[128,2560]{1,0:T(8,128)(2,1)S(1)} collective-permute-done((bf16[128,2560]{1,0:T(8,128)(2,1)S(1)}, bf16[128,2560]{1,0:T(8,128)(2,1)S(1)}, u32[]{:S(2)}, u32[]{:S(2)}) %collective-permute-start.23) | collective-permute-done | bytes 655392 | tf_op jit(solution)/shard_map/ppermute | solution.py:359
  159.6 2.6 %collective-permute-start.24 = (bf16[64,2560]{1,0:T(8,128)(2,1)S(1)}, bf16[64,2560]{1,0:T(8,128)(2,1)S(1)}, u32[]{:S(2)}, u32[]{:S(2)}) collective-permute-start(bf16[64,2560]{1,0:T(8,128)(2,1)S(1)} %get-tuple-element.44), channel_id=1, source_target_pairs={{0,24},{2,26},{4,28},{6,30},{8,0},{10,2},{12,4},{14,6},{16,8},{18,... | collective-permute-start | bytes 983048 | tf_op jit(solution)/shard_map/ppermute | solution.py:375
  162.2 3.0 %collective-permute-start.25 = (bf16[64,2560]{1,0:T(8,128)(2,1)S(1)}, bf16[64,2560]{1,0:T(8,128)(2,1)S(1)}, u32[]{:S(2)}, u32[]{:S(2)}) collective-permute-start(bf16[64,2560]{1,0:T(8,128)(2,1)S(1)} %get-tuple-element.43), channel_id=1, source_target_pairs={{0,8},{2,10},{4,12},{6,14},{8,16},{10,18},{12,20},{14,22},{16,24},... | collective-permute-start | bytes 983048 | tf_op jit(solution)/shard_map/ppermute | solution.py:375
  165.2 11.6 %collective-permute-done.18.sent_ref = bf16[2048,512]{1,0:T(8,128)(2,1)S(1)} collective-permute-done((bf16[2048,512]{1,0:T(8,128)(2,1)}, bf16[2048,512]{1,0:T(8,128)(2,1)S(1)}, u32[]{:S(2)}, u32[]{:S(2)}) %collective-permute-start.18) | collective-permute-done | bytes 2097184 | tf_op jit(solution)/shard_map/ppermute | solution.py:433
  176.8 3.1 %collective-permute-done.25.refs_5_ = bf16[64,2560]{1,0:T(8,128)(2,1)S(1)} collective-permute-done((bf16[64,2560]{1,0:T(8,128)(2,1)S(1)}, bf16[64,2560]{1,0:T(8,128)(2,1)S(1)}, u32[]{:S(2)}, u32[]{:S(2)}) %collective-permute-start.25) | collective-permute-done | bytes 327712 | tf_op jit(solution)/shard_map/ppermute | solution.py:375
  179.8 2.4 %shard_map.88 = (bf16[2048,512]{1,0:T(8,128)(2,1)}, f32[64,2048]{1,0:T(8,128)}, f32[64,512]{1,0:T(8,128)}) custom-call(bf16[2048,512]{1,0:T(8,128)(2,1)S(1)} %copy-done.1, bf16[2048,512]{1,0:T(8,128)(2,1)S(1)} %collective-permute-done.18.sent_ref, bf16[512,2560]{1,0:T(8,128)(2,1)S(1)} %copy-done, bf16[512,2560]{1,0:T(8,128)(2,1)S(1)} %collective-permute-done.19.refs_1_, ...), custom_call_target="tpu_custom_call" | custom-call | flops 1048576 | bytes 12582912 | tf_op jit(solution)/shard_map/pallas_call | solution.py:402
  (56 shorter events, 3.6 us)
Async XLA Ops:
  0.6 11.9 %copy-start.3 = (bf16[16,128,512]{2,1,0:T(8,128)(2,1)S(1)}, bf16[16,128,512]{2,1,0:T(8,128)(2,1)}, u32[]{:S(2)}) copy-start(bf16[16,128,512]{2,1,0:T(8,128)(2,1)} %param.7) | copy-start | bytes 6291460
  1.7 13.8 %collective-permute-start.4 = (bf16[64,1280]{1,0:T(8,128)(2,1)S(1)}, bf16[64,1280]{1,0:T(8,128)(2,1)S(1)}, u32[]{:S(2)}, u32[]{:S(2)}) collective-permute-start(bf16[64,1280]{1,0:T(8,128)(2,1)S(1)} %slice.106), channel_id=1, source_target_pairs={{0,16},{2,18},{4,20},{6,22},{8,24},{10,26},{12,28},{14,30},{16,0},... | collective-permute-start | bytes 491528 | tf_op jit(solution)/shard_map/ppermute | solution.py:112
  5.8 10.2 %collective-permute-start.5 = (bf16[64,1280]{1,0:T(8,128)(2,1)S(1)}, bf16[64,1280]{1,0:T(8,128)(2,1)S(1)}, u32[]{:S(2)}, u32[]{:S(2)}) collective-permute-start(bf16[64,1280]{1,0:T(8,128)(2,1)S(1)} %slice.106), channel_id=1, source_target_pairs={{0,24},{2,26},{4,28},{6,30},{8,0},{10,2},{12,4},{14,6},{16,8},{18,... | collective-permute-start | bytes 491528 | tf_op jit(solution)/shard_map/ppermute | solution.py:112
  7.2 11.1 %collective-permute-start.6 = (bf16[64,1280]{1,0:T(8,128)(2,1)S(1)}, bf16[64,1280]{1,0:T(8,128)(2,1)S(1)}, u32[]{:S(2)}, u32[]{:S(2)}) collective-permute-start(bf16[64,1280]{1,0:T(8,128)(2,1)S(1)} %slice.106), channel_id=1, source_target_pairs={{0,8},{2,10},{4,12},{6,14},{8,16},{10,18},{12,20},{14,22},{16,24},... | collective-permute-start | bytes 491528 | tf_op jit(solution)/shard_map/ppermute | solution.py:112
  9.6 33.9 %copy-start.4 = (bf16[64,2688]{1,0:T(8,128)(2,1)}, bf16[64,2688]{1,0:T(8,128)(2,1)S(1)}, u32[]{:S(2)}) copy-start(bf16[64,2688]{1,0:T(8,128)(2,1)S(1)} %fusion.1.refs_4_) | copy-start | bytes 1032196
  9.7 9.8 %collective-permute-start.1 = (bf16[64,2688]{1,0:T(8,128)(2,1)S(1)}, bf16[64,2688]{1,0:T(8,128)(2,1)S(1)}, u32[]{:S(2)}, u32[]{:S(2)}) collective-permute-start(bf16[64,2688]{1,0:T(8,128)(2,1)S(1)} %fusion.1.refs_4_), channel_id=1, source_target_pairs={{0,4},{2,6},{4,0},{6,2},{8,12},{10,14},{12,8},{14,10},{16,20},{18,... | collective-permute-start | bytes 1032200 | tf_op jit(solution)/shard_map/ppermute | solution.py:99
  14.0 42.2 %copy-start.2 = (bf16[16,128,512]{2,1,0:T(8,128)(2,1)S(1)}, bf16[16,128,512]{2,1,0:T(8,128)(2,1)}, u32[]{:S(2)}) copy-start(bf16[16,128,512]{2,1,0:T(8,128)(2,1)} %param.6) | copy-start | bytes 6291460
  14.0 47.4 %collective-permute-start.17 = (bf16[2048,512]{1,0:T(8,128)(2,1)}, bf16[2048,512]{1,0:T(8,128)(2,1)}, u32[]{:S(2)}, u32[]{:S(2)}) collective-permute-start(bf16[2048,512]{1,0:T(8,128)(2,1)} %pad_maximum_fusion), channel_id=1, source_target_pairs={{0,1},{1,0},{2,3},{3,2},{4,5},{5,4},{6,7},{7,6},{8,9},{9,8},{10,11... | collective-permute-start | bytes 6291464 | tf_op jit(solution)/shard_map/ppermute | solution.py:425
  19.4 36.8 %copy-start.7 = (bf16[64,2688]{1,0:T(8,128)(2,1)}, bf16[64,2688]{1,0:T(8,128)(2,1)S(1)}, u32[]{:S(2)}) copy-start(bf16[64,2688]{1,0:T(8,128)(2,1)S(1)} %collective-permute-done.1.refs_5_) | copy-start | bytes 1032196
  21.6 12.4 %collective-permute-start.7 = (bf16[192,1280]{1,0:T(8,128)(2,1)}, bf16[192,1280]{1,0:T(8,128)(2,1)}, u32[]{:S(2)}, u32[]{:S(2)}) collective-permute-start(bf16[192,1280]{1,0:T(8,128)(2,1)} %maximum_select_fusion.1.refs_8_), channel_id=1, source_target_pairs={{0,4},{2,6},{4,0},{6,2},{8,12},{10,14},{12,8},{14,10},{16,20},{18,... | collective-permute-start | bytes 1474568 | tf_op jit(solution)/shard_map/ppermute | solution.py:99
  23.1 18.1 %collective-permute-start.10 = (bf16[64,1408]{1,0:T(8,128)(2,1)S(1)}, bf16[64,1408]{1,0:T(8,128)(2,1)S(1)}, u32[]{:S(2)}, u32[]{:S(2)}) collective-permute-start(bf16[64,1408]{1,0:T(8,128)(2,1)S(1)} %slice_select_fusion), channel_id=1, source_target_pairs={{0,16},{2,18},{4,20},{6,22},{8,24},{10,26},{12,28},{14,30},{16,0},... | collective-permute-start | bytes 540680 | tf_op jit(solution)/shard_map/ppermute | solution.py:112
  28.2 13.1 %collective-permute-start.11 = (bf16[64,1408]{1,0:T(8,128)(2,1)S(1)}, bf16[64,1408]{1,0:T(8,128)(2,1)S(1)}, u32[]{:S(2)}, u32[]{:S(2)}) collective-permute-start(bf16[64,1408]{1,0:T(8,128)(2,1)S(1)} %slice_select_fusion), channel_id=1, source_target_pairs={{0,24},{2,26},{4,28},{6,30},{8,0},{10,2},{12,4},{14,6},{16,8},{18,... | collective-permute-start | bytes 540680 | tf_op jit(solution)/shard_map/ppermute | solution.py:112
  30.2 11.0 %collective-permute-start.12 = (bf16[64,1408]{1,0:T(8,128)(2,1)S(1)}, bf16[64,1408]{1,0:T(8,128)(2,1)S(1)}, u32[]{:S(2)}, u32[]{:S(2)}) collective-permute-start(bf16[64,1408]{1,0:T(8,128)(2,1)S(1)} %slice_select_fusion), channel_id=1, source_target_pairs={{0,8},{2,10},{4,12},{6,14},{8,16},{10,18},{12,20},{14,22},{16,24},... | collective-permute-start | bytes 540680 | tf_op jit(solution)/shard_map/ppermute | solution.py:112
  42.8 12.1 %collective-permute-start.13 = (bf16[192,1408]{1,0:T(8,128)(2,1)}, bf16[192,1408]{1,0:T(8,128)(2,1)}, u32[]{:S(2)}, u32[]{:S(2)}) collective-permute-start(bf16[192,1408]{1,0:T(8,128)(2,1)} %maximum_select_fusion.refs_12_), channel_id=1, source_target_pairs={{0,4},{2,6},{4,0},{6,2},{8,12},{10,14},{12,8},{14,10},{16,20},{18,... | collective-permute-start | bytes 1622024 | tf_op jit(solution)/shard_map/ppermute | solution.py:99
  43.6 11.3 %collective-permute-start.2 = (bf16[64,2688]{1,0:T(8,128)(2,1)S(1)}, bf16[64,2688]{1,0:T(8,128)(2,1)S(1)}, u32[]{:S(2)}, u32[]{:S(2)}) collective-permute-start(bf16[64,2688]{1,0:T(8,128)(2,1)S(1)} %fusion.1.refs_4_), channel_id=1, source_target_pairs={{0,2},{2,0},{4,6},{6,4},{8,10},{10,8},{12,14},{14,12},{16,18},{18,... | collective-permute-start | bytes 1032200 | tf_op jit(solution)/shard_map/ppermute | solution.py:99
  43.6 11.8 %collective-permute-start.3 = (bf16[64,2688]{1,0:T(8,128)(2,1)S(1)}, bf16[64,2688]{1,0:T(8,128)(2,1)S(1)}, u32[]{:S(2)}, u32[]{:S(2)}) collective-permute-start(bf16[64,2688]{1,0:T(8,128)(2,1)S(1)} %collective-permute-done.1.refs_5_), channel_id=1, source_target_pairs={{0,2},{2,0},{4,6},{6,4},{8,10},{10,8},{12,14},{14,12},{16,18},{18,... | collective-permute-start | bytes 1032200 | tf_op jit(solution)/shard_map/ppermute | solution.py:99
  44.1 17.3 %collective-permute-start.14 = (bf16[192,1408]{1,0:T(8,128)(2,1)}, bf16[192,1408]{1,0:T(8,128)(2,1)}, u32[]{:S(2)}, u32[]{:S(2)}) collective-permute-start(bf16[192,1408]{1,0:T(8,128)(2,1)} %maximum_select_fusion.refs_12_), channel_id=1, source_target_pairs={{0,2},{2,0},{4,6},{6,4},{8,10},{10,8},{12,14},{14,12},{16,18},{18,... | collective-permute-start | bytes 1622024 | tf_op jit(solution)/shard_map/ppermute | solution.py:99
  54.9 6.6 %collective-permute-start.15 = (bf16[192,1408]{1,0:T(8,128)(2,1)}, bf16[192,1408]{1,0:T(8,128)(2,1)}, u32[]{:S(2)}, u32[]{:S(2)}) collective-permute-start(bf16[192,1408]{1,0:T(8,128)(2,1)} %collective-permute-done.13.refs_13_), channel_id=1, source_target_pairs={{0,2},{2,0},{4,6},{6,4},{8,10},{10,8},{12,14},{14,12},{16,18},{18,... | collective-permute-start | bytes 1622024 | tf_op jit(solution)/shard_map/ppermute | solution.py:99
  54.9 1.4 copy-start.8
  54.9 4.4 %collective-permute-start.8 = (bf16[192,1280]{1,0:T(8,128)(2,1)}, bf16[192,1280]{1,0:T(8,128)(2,1)}, u32[]{:S(2)}, u32[]{:S(2)}) collective-permute-start(bf16[192,1280]{1,0:T(8,128)(2,1)} %maximum_select_fusion.1.refs_8_), channel_id=1, source_target_pairs={{0,2},{2,0},{4,6},{6,4},{8,10},{10,8},{12,14},{14,12},{16,18},{18,... | collective-permute-start | bytes 1474568 | tf_op jit(solution)/shard_map/ppermute | solution.py:99
  55.4 0.8 copy-start.9
  56.1 4.8 %collective-permute-start.9 = (bf16[192,1280]{1,0:T(8,128)(2,1)}, bf16[192,1280]{1,0:T(8,128)(2,1)}, u32[]{:S(2)}, u32[]{:S(2)}) collective-permute-start(bf16[192,1280]{1,0:T(8,128)(2,1)} %collective-permute-done.7.refs_9_), channel_id=1, source_target_pairs={{0,2},{2,0},{4,6},{6,4},{8,10},{10,8},{12,14},{14,12},{16,18},{18,... | collective-permute-start | bytes 1474568 | tf_op jit(solution)/shard_map/ppermute | solution.py:99
  59.3 32.4 %collective-permute-start.16 = (bf16[1024,512]{1,0:T(8,128)(2,1)S(1)}, bf16[1024,512]{1,0:T(8,128)(2,1)S(1)}, u32[]{:S(2)}, u32[]{:S(2)}) collective-permute-start(bf16[1024,512]{1,0:T(8,128)(2,1)S(1)} %pad_maximum_fusion.1), channel_id=1, source_target_pairs={{0,1},{1,0},{2,3},{3,2},{4,5},{5,4},{6,7},{7,6},{8,9},{9,8},{10,11... | collective-permute-start | bytes 3145736 | tf_op jit(solution)/shard_map/ppermute | solution.py:425
  60.9 48.7 %collective-permute-start = (bf16[1024,512]{1,0:T(8,128)(2,1)S(1)}, bf16[1024,512]{1,0:T(8,128)(2,1)S(1)}, u32[]{:S(2)}, u32[]{:S(2)}) collective-permute-start(bf16[1024,512]{1,0:T(8,128)(2,1)S(1)} %pad_maximum_fusion.2), channel_id=1, source_target_pairs={{0,1},{1,0},{2,3},{3,2},{4,5},{5,4},{6,7},{7,6},{8,9},{9,8},{10,11... | collective-permute-start | bytes 3145736 | tf_op jit(solution)/shard_map/ppermute | solution.py:425
  91.6 1.0 copy-start.6
  109.6 1.0 copy-start.5
  128.4 16.9 %copy-start = (bf16[512,2560]{1,0:T(8,128)(2,1)S(1)}, bf16[512,2560]{1,0:T(8,128)(2,1)}, u32[]{:S(2)}) copy-start(bf16[512,2560]{1,0:T(8,128)(2,1)} %get-tuple-element.32.refs_0_) | copy-start | bytes 7864324
  128.4 5.2 %collective-permute-start.19 = (bf16[512,2560]{1,0:T(8,128)(2,1)}, bf16[512,2560]{1,0:T(8,128)(2,1)S(1)}, u32[]{:S(2)}, u32[]{:S(2)}) collective-permute-start(bf16[512,2560]{1,0:T(8,128)(2,1)} %get-tuple-element.33), channel_id=1, source_target_pairs={{0,2},{2,0},{4,6},{6,4},{8,10},{10,8},{12,14},{14,12},{16,18},{18,... | collective-permute-start | bytes 7864328 | tf_op jit(solution)/shard_map/ppermute | solution.py:359
  128.5 48.3 %collective-permute-start.18 = (bf16[2048,512]{1,0:T(8,128)(2,1)}, bf16[2048,512]{1,0:T(8,128)(2,1)S(1)}, u32[]{:S(2)}, u32[]{:S(2)}) collective-permute-start(bf16[2048,512]{1,0:T(8,128)(2,1)} %get-tuple-element.31), channel_id=1, source_target_pairs={{0,1},{1,0},{2,3},{3,2},{4,5},{5,4},{6,7},{7,6},{8,9},{9,8},{10,11... | collective-permute-start | bytes 6291464 | tf_op jit(solution)/shard_map/ppermute | solution.py:433
  134.7 10.6 %collective-permute-start.21 = (bf16[64,2560]{1,0:T(8,128)(2,1)S(1)}, bf16[64,2560]{1,0:T(8,128)(2,1)S(1)}, u32[]{:S(2)}, u32[]{:S(2)}) collective-permute-start(bf16[64,2560]{1,0:T(8,128)(2,1)S(1)} %add_convert_fusion.3), channel_id=1, source_target_pairs={{0,4},{2,6},{4,0},{6,2},{8,12},{10,14},{12,8},{14,10},{16,20},{18,... | collective-permute-start | bytes 983048 | tf_op jit(solution)/shard_map/ppermute | solution.py:359
  137.3 22.0 %collective-permute-start.23 = (bf16[128,2560]{1,0:T(8,128)(2,1)S(1)}, bf16[128,2560]{1,0:T(8,128)(2,1)S(1)}, u32[]{:S(2)}, u32[]{:S(2)}) collective-permute-start(bf16[128,2560]{1,0:T(8,128)(2,1)S(1)} %add_convert_fusion.1), channel_id=1, source_target_pairs={{0,4},{2,6},{4,0},{6,2},{8,12},{10,14},{12,8},{14,10},{16,20},{18,... | collective-permute-start | bytes 1966088 | tf_op jit(solution)/shard_map/ppermute | solution.py:359
  145.5 34.4 %copy-start.1 = (bf16[2048,512]{1,0:T(8,128)(2,1)S(1)}, bf16[2048,512]{1,0:T(8,128)(2,1)}, u32[]{:S(2)}) copy-start(bf16[2048,512]{1,0:T(8,128)(2,1)} %get-tuple-element.30.kept_ref) | copy-start | bytes 6291460
  145.5 31.3 %collective-permute-start.20 = (bf16[64,2560]{1,0:T(8,128)(2,1)S(1)}, bf16[64,2560]{1,0:T(8,128)(2,1)S(1)}, u32[]{:S(2)}, u32[]{:S(2)}) collective-permute-start(bf16[64,2560]{1,0:T(8,128)(2,1)S(1)} %get-tuple-element.38), channel_id=1, source_target_pairs={{0,4},{2,6},{4,0},{6,2},{8,12},{10,14},{12,8},{14,10},{16,20},{18,... | collective-permute-start | bytes 983048 | tf_op jit(solution)/shard_map/ppermute | solution.py:359
  146.9 29.8 %collective-permute-start.22 = (bf16[64,2560]{1,0:T(8,128)(2,1)S(1)}, bf16[64,2560]{1,0:T(8,128)(2,1)S(1)}, u32[]{:S(2)}, u32[]{:S(2)}) collective-permute-start(bf16[64,2560]{1,0:T(8,128)(2,1)S(1)} %get-tuple-element.37), channel_id=1, source_target_pairs={{0,16},{2,18},{4,20},{6,22},{8,24},{10,26},{12,28},{14,30},{16,0},... | collective-permute-start | bytes 983048 | tf_op jit(solution)/shard_map/ppermute | solution.py:375
  159.6 17.2 %collective-permute-start.24 = (bf16[64,2560]{1,0:T(8,128)(2,1)S(1)}, bf16[64,2560]{1,0:T(8,128)(2,1)S(1)}, u32[]{:S(2)}, u32[]{:S(2)}) collective-permute-start(bf16[64,2560]{1,0:T(8,128)(2,1)S(1)} %get-tuple-element.44), channel_id=1, source_target_pairs={{0,24},{2,26},{4,28},{6,30},{8,0},{10,2},{12,4},{14,6},{16,8},{18,... | collective-permute-start | bytes 983048 | tf_op jit(solution)/shard_map/ppermute | solution.py:375
  162.2 17.7 %collective-permute-start.25 = (bf16[64,2560]{1,0:T(8,128)(2,1)S(1)}, bf16[64,2560]{1,0:T(8,128)(2,1)S(1)}, u32[]{:S(2)}, u32[]{:S(2)}) collective-permute-start(bf16[64,2560]{1,0:T(8,128)(2,1)S(1)} %get-tuple-element.43), channel_id=1, source_target_pairs={{0,8},{2,10},{4,12},{6,14},{8,16},{10,18},{12,20},{14,22},{16,24},... | collective-permute-start | bytes 983048 | tf_op jit(solution)/shard_map/ppermute | solution.py:375

commit v4 on v3

--- a/solution.py
+++ b/solution.py
@@ -116,12 +116,12 @@
     return arrays
 
 
-def group_kernel(start, steps, first, last, heads, parts, users, *refs):
+def group_kernel(start, steps, first, last, heads, parts, users, shared, *refs):
     refs = list(refs)
     where_ref, xo_ref, do_ref, far_ref = refs[:4]
     pieces, refs = refs[4:16], refs[16:]
     acc_hbm = None if first else refs.pop(0)
-    refs = refs if first else refs[2:]
+    refs = refs[shared:]
     gx_ref, bs_ref = refs[:2]
     refs = refs[2:]
     grads_hbm = [refs.pop(0) for _ in range(2 if last else 1)]
@@ -305,6 +305,9 @@
     anywhere = pl.BlockSpec(memory_space=pl.ANY)
     mine = pl.BlockSpec((rows, own), lambda i: (start + i, 0))
     theirs = pl.BlockSpec((2 * rows, width - own), lambda i: (i, 0))
+    shared = max(0, len(past) - 1)
+    alone = GROUPS[0][1]
+    base, held = (0, alone) if first else (alone, blocks - alone)
     args = [where, x, d, far] + pieces + past
     specs = [smem, mine, mine, theirs] + [anywhere] * (len(pieces) + len(past))
     if last:
@@ -313,20 +316,20 @@
         grads = [jax.ShapeDtypeStruct((width, cols), f32)]
     flops = steps * (4 * rows * width * cols + 2 * rows * width * cols_in)
     return pl.pallas_call(
-        functools.partial(group_kernel, start, steps, first, last, heads, parts, users),
+        functools.partial(group_kernel, start, steps, first, last, heads, parts, users, shared),
         grid=(steps,),
         out_shape=[
             jax.ShapeDtypeStruct((blocks * rows, own), bf16),
-            jax.ShapeDtypeStruct((blocks * rows, width - own), bf16),
+            jax.ShapeDtypeStruct((held * rows, width - own), bf16),
         ]
         + grads,
         in_specs=specs,
         out_specs=[
             pl.BlockSpec((rows, own), lambda i: (start + i, 0)),
-            pl.BlockSpec((rows, width - own), lambda i: (start + i, 0)),
+            pl.BlockSpec((rows, width - own), lambda i: (start - base + i, 0)),
         ]
         + [anywhere] * len(grads),
-        input_output_aliases={} if first else {len(pieces) + 5: 0, len(pieces) + 6: 1},
+        input_output_aliases={len(pieces) + 5 + i: i for i in range(shared)},
         scratch_shapes=[
             pltpu.VMEM((width, cols + SLOTS), bf16),
             pltpu.VMEM((width, cols), f32),
@@ -350,7 +353,7 @@
     )(*args)
 
 
-def scatter_parts(keep, send, users):
+def scatter_parts(keep, send, users, user, early):
     far = users // 4
     order = split_order(far)
     size = keep.shape[0] // (2 * far)
@@ -358,30 +361,39 @@
     def swap(block, bit):
         return lax.ppermute(block, "user", [(i, i ^ bit) for i in range(users)])
 
-    got = swap(send, 1)
+    got = swap(jnp.where(user < 0, early[:1, :1], send), 1)
 
     def both(lo, hi):
         span = slice(lo * size, hi * size)
         return keep[span].astype(f32) + got[span].astype(f32)
 
     cuts = [(0, 1), (1, far - 1), (far - 1, far)]
-    across = [swap(both(far + lo, far + hi).astype(bf16), 2) for lo, hi in cuts]
-    moved = []
+    across, moved = [], []
+    for at, (lo, hi) in enumerate(cuts):
+        block = both(far + lo, far + hi).astype(bf16)
+        if at == 2:
+            block = jnp.where(user < 0, across[1][:1, :1], block)
+        across.append(swap(block, 2))
     for (lo, hi), other in zip(cuts[:2], across):
         near = (both(lo, hi) + other.astype(f32)).astype(bf16)
         for at in range(lo, hi):
             pairs = [(i, (i - 4 * order[at]) % users) for i in range(users)]
             block = near[(at - lo) * size : (at - lo + 1) * size]
             moved.append(lax.ppermute(block, "user", pairs))
-    return got, [across[2]] + moved
-
-
-def finish_kernel(cols_in, kept_ref, sent_ref, *refs):
+    return got, [across[-1]] + moved
+
+
+def finish_kernel(cols_in, alone, kept_ref, sent_a, sent_b, *refs):
     terms = refs[:-3]
     gx_ref, win_ref, wout_ref = refs[-3:]
-    gx_ref[...] = (kept_ref[...].astype(f32) + sent_ref[...].astype(f32)).astype(bf16)
-
-    @pl.when(pl.program_id(0) == 0)
+    step = pl.program_id(0)
+    for at, sent_ref in ((step < alone, sent_a), (step >= alone, sent_b)):
+
+        @pl.when(at)
+        def _(sent_ref=sent_ref):
+            gx_ref[...] = (kept_ref[...].astype(f32) + sent_ref[...].astype(f32)).astype(bf16)
+
+    @pl.when(step == 0)
     def _():
         total = terms[0][...].astype(f32)
         for term in terms[1:]:
@@ -394,13 +406,18 @@
     rows, own = kept.shape
     size, cols = rest[0].shape
     slot = keep.shape[0] // (2 * size) - 1
-    steps = 4
+    alone = GROUPS[0][1]
+    steps = sum(count for _, count in GROUPS)
     lines = pl.BlockSpec((rows // steps, own), lambda i: (i, 0))
-    specs = [lines] * 2
+    specs = [
+        lines,
+        pl.BlockSpec((rows // steps, own), lambda i: (jnp.minimum(i, alone - 1), 0)),
+        pl.BlockSpec((rows // steps, own), lambda i: (jnp.maximum(i - alone, 0), 0)),
+    ]
     specs += [pl.BlockSpec((size, cols), lambda i: (slot, 0))] * 2
     specs += [pl.BlockSpec((size, cols), lambda i: (0, 0))] * len(rest)
     return pl.pallas_call(
-        functools.partial(finish_kernel, cols_in),
+        functools.partial(finish_kernel, cols_in, alone),
         grid=(steps,),
         out_shape=[
             jax.ShapeDtypeStruct((rows, own), bf16),
@@ -417,7 +434,7 @@
         cost_estimate=pl.CostEstimate(
             flops=rows * own, bytes_accessed=12 * 2**20, transcendentals=0
         ),
-    )(kept, sent, keep, got, *rest)
+    )(kept, *sent, keep, got, *rest)
 
 
 def exchange(block, tensor):
@@ -460,15 +477,19 @@
     pieces = gather_parts(shard, shard.shape[1] // 256 * 128, users, user)
     where = jnp.stack([lax.axis_index("tensor"), user]).astype(jnp.int32)
 
-    past = []
+    past, early = [], None
     for group, theirs in zip(GROUPS, far):
         kept, bs, *grads = group_call(
             group, blocks, users, tensor, where, x, d, theirs, pieces, past
         )
-        past = grads + [kept, bs]
-    sent = give_back(bs, own, tensor)
+        if early is None:
+            early = give_back(bs, own, tensor)
+            past = grads + [kept]
+        else:
+            past = grads + [kept, bs]
+    sent = [early, give_back(bs, own, tensor)]
     keep, send = grads
-    got, rest = scatter_parts(keep, send, users)
+    got, rest = scatter_parts(keep, send, users, user, early)
     grad_x, grad_in, grad_out = finish(kept, sent, keep, got, rest, w_in.shape[1])
     return (grad_x.reshape(hist, seq_len, own), grad_in, grad_out)
 

time: 186 us -> 190 us (1.022)
    ppermute x1 -> x2, waiting for transfers between devices: 11.6 us -> 0.01 us  [give_back(): return lax.ppermute(block, 'tensor', [(0, 1), (1, 0)])]
    ppermute x3, waiting for transfers between devices: 3.08 us -> 13.5 us  [scatter_parts(): moved.append(lax.ppermute(block, 'user', pairs))]
    select_n x0 -> x2, other arithmetic: none -> 3.77 us  [the longest x1 3.03 us: scatter_parts(): got = swap(jnp.where(user < 0, early[:1, :1], send), 1)]
    convert_element_type x2, other arithmetic: 2.29 us -> 0.23 us  [scatter_parts(): block = both(far + lo, far + hi).astype(bf16)]
  transfers between devices with their start and end apart: 26 -> 27, of which waited for: 9 -> 9; matrix products, arithmetic and copies ran while one was open for 9% -> 8% of each run, Pallas kernels for 26% -> 35%
where the time goes in v4:
time: 190 us; the launch traced here: 187 us
  Pallas kernels  67.5 us (36%)
  waiting for transfers between devices  53.9 us (28%)
  starting transfers between devices  38.9 us (20%)
  local copies, waits for them, and re-layouts  11.8 us (6%)
  other arithmetic  11.4 us (6%)
  between operations  3.19 us (2%)
    pallas_call x3, Pallas kernels, group_call(): pl.pallas_call(functools.partial(group_kernel, start, steps, first, last,...  65 us
    ppermute x13, waiting for transfers between devices, swap(): return lax.ppermute(block, 'user', [(i, i ^ bit) for i in range(users)])  33.9 us
    ppermute x3, waiting for transfers between devices, scatter_parts(): moved.append(lax.ppermute(block, 'user', pairs))  13.5 us
    ppermute x6, starting transfers between devices, gather_parts(): moved.append(lax.ppermute(part, 'user', pairs))  13.2 us
    ppermute x3, starting transfers between devices, scatter_parts(): moved.append(lax.ppermute(block, 'user', pairs))  11.3 us
    ppermute x13, starting transfers between devices, swap(): return lax.ppermute(block, 'user', [(i, i ^ bit) for i in range(users)])  7.82 us
    ppermute x6, waiting for transfers between devices, gather_parts(): moved.append(lax.ppermute(part, 'user', pairs))  6.53 us
  transfers between devices with their start and end apart: 27, of which 9 were waited for; matrix products, arithmetic and copies ran while one was open for 8% of the time, Pallas kernels for 35%

profile of v4, /device:TPU:0, one launch (start us, length us, event | category | flops | bytes accessed | tf_op | source)
XLA Modules:
  0.0 186.7 jit_solution(17713620914271669001)
XLA Ops:
  0.6 1.1 slice.112
  1.7 4.1 %collective-permute-start.4 = (bf16[64,1280]{1,0:T(8,128)(2,1)S(1)}, bf16[64,1280]{1,0:T(8,128)(2,1)S(1)}, u32[]{:S(2)}, u32[]{:S(2)}) collective-permute-start(bf16[64,1280]{1,0:T(8,128)(2,1)S(1)} %slice.112), channel_id=1, source_target_pairs={{0,16},{2,18},{4,20},{6,22},{8,24},{10,26},{12,28},{14,30},{16,0},... | collective-permute-start | bytes 491528 | tf_op jit(solution)/shard_map/ppermute | solution.py:112
  5.8 1.3 collective-permute-start.5
  7.2 0.7 collective-permute-start.6
  7.9 0.7 convert_bitcast_fusion
  8.6 1.0 fusion.1.refs_4_
  9.7 1.6 collective-permute-start.1
  11.2 1.3 fusion.6
  12.6 1.5 pad_maximum_fusion
  14.0 1.5 collective-permute-start.17
  19.5 0.6 slice.132
  20.0 1.5 maximum_select_fusion.1.refs_8_
  21.5 1.5 collective-permute-start.7
  23.0 5.0 %collective-permute-start.10 = (bf16[64,1408]{1,0:T(8,128)(2,1)S(1)}, bf16[64,1408]{1,0:T(8,128)(2,1)S(1)}, u32[]{:S(2)}, u32[]{:S(2)}) collective-permute-start(bf16[64,1408]{1,0:T(8,128)(2,1)S(1)} %slice_select_fusion), channel_id=1, source_target_pairs={{0,16},{2,18},{4,20},{6,22},{8,24},{10,26},{12,28},{14,30},{16,0},... | collective-permute-start | bytes 540680 | tf_op jit(solution)/shard_map/ppermute | solution.py:112
  28.1 2.0 %collective-permute-start.11 = (bf16[64,1408]{1,0:T(8,128)(2,1)S(1)}, bf16[64,1408]{1,0:T(8,128)(2,1)S(1)}, u32[]{:S(2)}, u32[]{:S(2)}) collective-permute-start(bf16[64,1408]{1,0:T(8,128)(2,1)S(1)} %slice_select_fusion), channel_id=1, source_target_pairs={{0,24},{2,26},{4,28},{6,30},{8,0},{10,2},{12,4},{14,6},{16,8},{18,... | collective-permute-start | bytes 540680 | tf_op jit(solution)/shard_map/ppermute | solution.py:112
  30.1 3.8 %collective-permute-done.7.refs_9_ = bf16[192,1280]{1,0:T(8,128)(2,1)} collective-permute-done((bf16[192,1280]{1,0:T(8,128)(2,1)}, bf16[192,1280]{1,0:T(8,128)(2,1)}, u32[]{:S(2)}, u32[]{:S(2)}) %collective-permute-start.7) | collective-permute-done | bytes 491552 | tf_op jit(solution)/shard_map/ppermute | solution.py:99
  33.9 1.2 slice.133
  35.1 6.0 %collective-permute-done.10 = bf16[64,1408]{1,0:T(8,128)(2,1)S(1)} collective-permute-done((bf16[64,1408]{1,0:T(8,128)(2,1)S(1)}, bf16[64,1408]{1,0:T(8,128)(2,1)S(1)}, u32[]{:S(2)}, u32[]{:S(2)}) %collective-permute-start.10) | collective-permute-done | bytes 180256 | tf_op jit(solution)/shard_map/ppermute | solution.py:112
  41.1 1.6 maximum_select_fusion.refs_12_
  42.7 0.8 collective-permute-start.13
  44.0 10.8 %collective-permute-done.13.refs_13_ = bf16[192,1408]{1,0:T(8,128)(2,1)} collective-permute-done((bf16[192,1408]{1,0:T(8,128)(2,1)}, bf16[192,1408]{1,0:T(8,128)(2,1)}, u32[]{:S(2)}, u32[]{:S(2)}) %collective-permute-start.13) | collective-permute-done | bytes 540704 | tf_op jit(solution)/shard_map/ppermute | solution.py:99
  55.3 0.7 copy-done.10
  56.3 1.1 slice.108
  57.5 1.1 slice.110
  58.6 0.6 pad_add_fusion.refs_0_
  59.2 1.6 collective-permute-start.16
  61.4 30.2 %shard_map.85 = (bf16[2048,512]{1,0:T(8,128)(2,1)}, bf16[1024,512]{1,0:T(8,128)(2,1)}, f32[1024,2560]{1,0:T(8,128)}) custom-call(s32[2]{0:T(128)} %pad_add_fusion.refs_0_, bf16[2048,512]{1,0:T(8,128)(2,1)} %bitcast.18, bf16[2048,512]{1,0:T(8,128)(2,1)} %bitcast.25, bf16[2048,512]{1,0:T(8,128)(2,1)} %collective-permute-done.17.refs_3_, ...), custom_call_target="tpu_custom_call" | custom-call | flops 15032385536 | bytes 16777216 | tf_op jit(solution)/shard_map/pallas_call | solution.py:318
  91.6 1.6 collective-permute-start.18
  93.2 1.0 copy-done.6
  94.2 17.0 %shard_map.86 = (bf16[2048,512]{1,0:T(8,128)(2,1)}, bf16[1024,512]{1,0:T(8,128)(2,1)}, f32[1024,2560]{1,0:T(8,128)}) custom-call(s32[2]{0:T(128)} %pad_add_fusion.refs_0_, bf16[2048,512]{1,0:T(8,128)(2,1)} %bitcast.19, bf16[2048,512]{1,0:T(8,128)(2,1)} %bitcast.26, bf16[1024,512]{1,0:T(8,128)(2,1)} %copy-done.6, ...), custom_call_target="tpu_custom_call", output_to_operand_aliasing={{0}: (17, {})} | custom-call | flops 7516192768 | bytes 16777216 | tf_op jit(solution)/shard_map/pallas_call | solution.py:318
  111.2 1.0 copy-done.5
  112.1 17.8 %shard_map.87 = (bf16[2048,512]{1,0:T(8,128)(2,1)}, bf16[1024,512]{1,0:T(8,128)(2,1)}, bf16[512,2560]{1,0:T(8,128)(2,1)}, bf16[512,2560]{1,0:T(8,128)(2,1)}) custom-call(s32[2]{0:T(128)} %pad_add_fusion.refs_0_, bf16[2048,512]{1,0:T(8,128)(2,1)} %bitcast.20, bf16[2048,512]{1,0:T(8,128)(2,1)} %bitcast.27, ...), custom_call_target="tpu_custom_call", output_to_operand_aliasing={{0}: (17, {}), {1}: (18, {})} | custom-call | flops 7516192768 | bytes 16777216 | tf_op jit(solution)/shard_map/pallas_call | solution.py:318
  130.0 0.5 slice.138
  130.5 3.0 %broadcast_select_fusion = bf16[512,2560]{1,0:T(8,128)(2,1)S(1)} fusion(bf16[512,2560]{1,0:T(8,128)(2,1)} %get-tuple-element.33, pred[]{:T(512)S(6)} %lt.2, bf16[]{:T(256)} %bitcast.13), kind=kLoop, calls=%fused_computation | loop fusion | flops 1310720 | bytes 5242883 | tf_op jit(solution)/shard_map/jit(_where)/select_n | solution.py:364
  133.6 1.3 collective-permute-start.19
  134.9 3.6 %collective-permute-done.20.refs_1_ = bf16[512,2560]{1,0:T(8,128)(2,1)S(1)} collective-permute-done((bf16[512,2560]{1,0:T(8,128)(2,1)S(1)}, bf16[512,2560]{1,0:T(8,128)(2,1)S(1)}, u32[]{:S(2)}, u32[]{:S(2)}) %collective-permute-start.20) | collective-permute-done | bytes 2621472 | tf_op jit(solution)/shard_map/ppermute | solution.py:362
  138.6 1.2 collective-permute-start.23
  139.9 1.0 collective-permute-start.21
  140.9 8.3 %collective-permute-done.23 = bf16[64,2560]{1,0:T(8,128)(2,1)S(1)} collective-permute-done((bf16[64,2560]{1,0:T(8,128)(2,1)S(1)}, bf16[64,2560]{1,0:T(8,128)(2,1)S(1)}, u32[]{:S(2)}, u32[]{:S(2)}) %collective-permute-start.23) | collective-permute-done | bytes 327712 | tf_op jit(solution)/shard_map/ppermute | solution.py:362
  149.3 5.7 %collective-permute-start.24 = (bf16[64,2560]{1,0:T(8,128)(2,1)S(1)}, bf16[64,2560]{1,0:T(8,128)(2,1)S(1)}, u32[]{:S(2)}, u32[]{:S(2)}) collective-permute-start(bf16[64,2560]{1,0:T(8,128)(2,1)S(1)} %add_convert_fusion.2), channel_id=1, source_target_pairs={{0,16},{2,18},{4,20},{6,22},{8,24},{10,26},{12,28},{14,30},{16,0},... | collective-permute-start | bytes 983048 | tf_op jit(solution)/shard_map/ppermute | solution.py:382
  155.0 7.4 %collective-permute-done.21 = bf16[128,2560]{1,0:T(8,128)(2,1)S(1)} collective-permute-done((bf16[128,2560]{1,0:T(8,128)(2,1)S(1)}, bf16[128,2560]{1,0:T(8,128)(2,1)S(1)}, u32[]{:S(2)}, u32[]{:S(2)}) %collective-permute-start.21) | collective-permute-done | bytes 655392 | tf_op jit(solution)/shard_map/ppermute | solution.py:362
  162.7 2.5 %collective-permute-start.25 = (bf16[64,2560]{1,0:T(8,128)(2,1)S(1)}, bf16[64,2560]{1,0:T(8,128)(2,1)S(1)}, u32[]{:S(2)}, u32[]{:S(2)}) collective-permute-start(bf16[64,2560]{1,0:T(8,128)(2,1)S(1)} %get-tuple-element.42), channel_id=1, source_target_pairs={{0,24},{2,26},{4,28},{6,30},{8,0},{10,2},{12,4},{14,6},{16,8},{18,... | collective-permute-start | bytes 983048 | tf_op jit(solution)/shard_map/ppermute | solution.py:382
  165.2 3.1 %collective-permute-start.26 = (bf16[64,2560]{1,0:T(8,128)(2,1)S(1)}, bf16[64,2560]{1,0:T(8,128)(2,1)S(1)}, u32[]{:S(2)}, u32[]{:S(2)}) collective-permute-start(bf16[64,2560]{1,0:T(8,128)(2,1)S(1)} %get-tuple-element.41), channel_id=1, source_target_pairs={{0,8},{2,10},{4,12},{6,14},{8,16},{10,18},{12,20},{14,22},{16,24},... | collective-permute-start | bytes 983048 | tf_op jit(solution)/shard_map/ppermute | solution.py:382
  168.9 0.7 fusion.2
  169.6 0.6 collective-permute-start.22
  170.3 5.7 %collective-permute-done.25.refs_4_ = bf16[64,2560]{1,0:T(8,128)(2,1)S(1)} collective-permute-done((bf16[64,2560]{1,0:T(8,128)(2,1)S(1)}, bf16[64,2560]{1,0:T(8,128)(2,1)S(1)}, u32[]{:S(2)}, u32[]{:S(2)}) %collective-permute-start.25) | collective-permute-done | bytes 327712 | tf_op jit(solution)/shard_map/ppermute | solution.py:382
  176.0 7.7 %collective-permute-done.26.refs_5_ = bf16[64,2560]{1,0:T(8,128)(2,1)S(1)} collective-permute-done((bf16[64,2560]{1,0:T(8,128)(2,1)S(1)}, bf16[64,2560]{1,0:T(8,128)(2,1)S(1)}, u32[]{:S(2)}, u32[]{:S(2)}) %collective-permute-start.26) | collective-permute-done | bytes 327712 | tf_op jit(solution)/shard_map/ppermute | solution.py:382
  183.8 2.5 %shard_map.88 = (bf16[2048,512]{1,0:T(8,128)(2,1)}, f32[64,2048]{1,0:T(8,128)}, f32[64,512]{1,0:T(8,128)}) custom-call(bf16[2048,512]{1,0:T(8,128)(2,1)S(1)} %copy-done.1, bf16[1024,512]{1,0:T(8,128)(2,1)S(1)} %collective-permute-done.18.sent_a, bf16[1024,512]{1,0:T(8,128)(2,1)S(1)} %collective-permute-done.19.sent_b, bf16[512,2560]{1,0:T(8,128)(2,1)S(1)} %copy-done, ...), custom_call_target="tpu_custom_call" | custom-call | flops 1048576 | bytes 12582912 | tf_op jit(solution)/shard_map/pallas_call | solution.py:419
  (64 shorter events, 5.4 us)
Async XLA Ops:
  0.6 11.9 %copy-start.3 = (bf16[16,128,512]{2,1,0:T(8,128)(2,1)S(1)}, bf16[16,128,512]{2,1,0:T(8,128)(2,1)}, u32[]{:S(2)}) copy-start(bf16[16,128,512]{2,1,0:T(8,128)(2,1)} %param.7) | copy-start | bytes 6291460
  1.7 13.8 %collective-permute-start.4 = (bf16[64,1280]{1,0:T(8,128)(2,1)S(1)}, bf16[64,1280]{1,0:T(8,128)(2,1)S(1)}, u32[]{:S(2)}, u32[]{:S(2)}) collective-permute-start(bf16[64,1280]{1,0:T(8,128)(2,1)S(1)} %slice.112), channel_id=1, source_target_pairs={{0,16},{2,18},{4,20},{6,22},{8,24},{10,26},{12,28},{14,30},{16,0},... | collective-permute-start | bytes 491528 | tf_op jit(solution)/shard_map/ppermute | solution.py:112
  5.8 10.2 %collective-permute-start.5 = (bf16[64,1280]{1,0:T(8,128)(2,1)S(1)}, bf16[64,1280]{1,0:T(8,128)(2,1)S(1)}, u32[]{:S(2)}, u32[]{:S(2)}) collective-permute-start(bf16[64,1280]{1,0:T(8,128)(2,1)S(1)} %slice.112), channel_id=1, source_target_pairs={{0,24},{2,26},{4,28},{6,30},{8,0},{10,2},{12,4},{14,6},{16,8},{18,... | collective-permute-start | bytes 491528 | tf_op jit(solution)/shard_map/ppermute | solution.py:112
  7.2 11.1 %collective-permute-start.6 = (bf16[64,1280]{1,0:T(8,128)(2,1)S(1)}, bf16[64,1280]{1,0:T(8,128)(2,1)S(1)}, u32[]{:S(2)}, u32[]{:S(2)}) collective-permute-start(bf16[64,1280]{1,0:T(8,128)(2,1)S(1)} %slice.112), channel_id=1, source_target_pairs={{0,8},{2,10},{4,12},{6,14},{8,16},{10,18},{12,20},{14,22},{16,24},... | collective-permute-start | bytes 491528 | tf_op jit(solution)/shard_map/ppermute | solution.py:112
  9.6 33.9 %copy-start.4 = (bf16[64,2688]{1,0:T(8,128)(2,1)}, bf16[64,2688]{1,0:T(8,128)(2,1)S(1)}, u32[]{:S(2)}) copy-start(bf16[64,2688]{1,0:T(8,128)(2,1)S(1)} %fusion.1.refs_4_) | copy-start | bytes 1032196
  9.7 9.8 %collective-permute-start.1 = (bf16[64,2688]{1,0:T(8,128)(2,1)S(1)}, bf16[64,2688]{1,0:T(8,128)(2,1)S(1)}, u32[]{:S(2)}, u32[]{:S(2)}) collective-permute-start(bf16[64,2688]{1,0:T(8,128)(2,1)S(1)} %fusion.1.refs_4_), channel_id=1, source_target_pairs={{0,4},{2,6},{4,0},{6,2},{8,12},{10,14},{12,8},{14,10},{16,20},{18,... | collective-permute-start | bytes 1032200 | tf_op jit(solution)/shard_map/ppermute | solution.py:99
  14.0 42.2 %copy-start.2 = (bf16[16,128,512]{2,1,0:T(8,128)(2,1)S(1)}, bf16[16,128,512]{2,1,0:T(8,128)(2,1)}, u32[]{:S(2)}) copy-start(bf16[16,128,512]{2,1,0:T(8,128)(2,1)} %param.6) | copy-start | bytes 6291460
  14.0 47.3 %collective-permute-start.17 = (bf16[2048,512]{1,0:T(8,128)(2,1)}, bf16[2048,512]{1,0:T(8,128)(2,1)}, u32[]{:S(2)}, u32[]{:S(2)}) collective-permute-start(bf16[2048,512]{1,0:T(8,128)(2,1)} %pad_maximum_fusion), channel_id=1, source_target_pairs={{0,1},{1,0},{2,3},{3,2},{4,5},{5,4},{6,7},{7,6},{8,9},{9,8},{10,11... | collective-permute-start | bytes 6291464 | tf_op jit(solution)/shard_map/ppermute | solution.py:442
  19.4 36.8 %copy-start.8 = (bf16[64,2688]{1,0:T(8,128)(2,1)}, bf16[64,2688]{1,0:T(8,128)(2,1)S(1)}, u32[]{:S(2)}) copy-start(bf16[64,2688]{1,0:T(8,128)(2,1)S(1)} %collective-permute-done.1.refs_5_) | copy-start | bytes 1032196
  21.5 12.4 %collective-permute-start.7 = (bf16[192,1280]{1,0:T(8,128)(2,1)}, bf16[192,1280]{1,0:T(8,128)(2,1)}, u32[]{:S(2)}, u32[]{:S(2)}) collective-permute-start(bf16[192,1280]{1,0:T(8,128)(2,1)} %maximum_select_fusion.1.refs_8_), channel_id=1, source_target_pairs={{0,4},{2,6},{4,0},{6,2},{8,12},{10,14},{12,8},{14,10},{16,20},{18,... | collective-permute-start | bytes 1474568 | tf_op jit(solution)/shard_map/ppermute | solution.py:99
  23.0 18.1 %collective-permute-start.10 = (bf16[64,1408]{1,0:T(8,128)(2,1)S(1)}, bf16[64,1408]{1,0:T(8,128)(2,1)S(1)}, u32[]{:S(2)}, u32[]{:S(2)}) collective-permute-start(bf16[64,1408]{1,0:T(8,128)(2,1)S(1)} %slice_select_fusion), channel_id=1, source_target_pairs={{0,16},{2,18},{4,20},{6,22},{8,24},{10,26},{12,28},{14,30},{16,0},... | collective-permute-start | bytes 540680 | tf_op jit(solution)/shard_map/ppermute | solution.py:112
  28.1 13.0 %collective-permute-start.11 = (bf16[64,1408]{1,0:T(8,128)(2,1)S(1)}, bf16[64,1408]{1,0:T(8,128)(2,1)S(1)}, u32[]{:S(2)}, u32[]{:S(2)}) collective-permute-start(bf16[64,1408]{1,0:T(8,128)(2,1)S(1)} %slice_select_fusion), channel_id=1, source_target_pairs={{0,24},{2,26},{4,28},{6,30},{8,0},{10,2},{12,4},{14,6},{16,8},{18,... | collective-permute-start | bytes 540680 | tf_op jit(solution)/shard_map/ppermute | solution.py:112
  30.1 11.0 %collective-permute-start.12 = (bf16[64,1408]{1,0:T(8,128)(2,1)S(1)}, bf16[64,1408]{1,0:T(8,128)(2,1)S(1)}, u32[]{:S(2)}, u32[]{:S(2)}) collective-permute-start(bf16[64,1408]{1,0:T(8,128)(2,1)S(1)} %slice_select_fusion), channel_id=1, source_target_pairs={{0,8},{2,10},{4,12},{6,14},{8,16},{10,18},{12,20},{14,22},{16,24},... | collective-permute-start | bytes 540680 | tf_op jit(solution)/shard_map/ppermute | solution.py:112
  42.7 12.1 %collective-permute-start.13 = (bf16[192,1408]{1,0:T(8,128)(2,1)}, bf16[192,1408]{1,0:T(8,128)(2,1)}, u32[]{:S(2)}, u32[]{:S(2)}) collective-permute-start(bf16[192,1408]{1,0:T(8,128)(2,1)} %maximum_select_fusion.refs_12_), channel_id=1, source_target_pairs={{0,4},{2,6},{4,0},{6,2},{8,12},{10,14},{12,8},{14,10},{16,20},{18,... | collective-permute-start | bytes 1622024 | tf_op jit(solution)/shard_map/ppermute | solution.py:99
  43.5 11.3 %collective-permute-start.2 = (bf16[64,2688]{1,0:T(8,128)(2,1)S(1)}, bf16[64,2688]{1,0:T(8,128)(2,1)S(1)}, u32[]{:S(2)}, u32[]{:S(2)}) collective-permute-start(bf16[64,2688]{1,0:T(8,128)(2,1)S(1)} %fusion.1.refs_4_), channel_id=1, source_target_pairs={{0,2},{2,0},{4,6},{6,4},{8,10},{10,8},{12,14},{14,12},{16,18},{18,... | collective-permute-start | bytes 1032200 | tf_op jit(solution)/shard_map/ppermute | solution.py:99
  43.5 11.8 %collective-permute-start.3 = (bf16[64,2688]{1,0:T(8,128)(2,1)S(1)}, bf16[64,2688]{1,0:T(8,128)(2,1)S(1)}, u32[]{:S(2)}, u32[]{:S(2)}) collective-permute-start(bf16[64,2688]{1,0:T(8,128)(2,1)S(1)} %collective-permute-done.1.refs_5_), channel_id=1, source_target_pairs={{0,2},{2,0},{4,6},{6,4},{8,10},{10,8},{12,14},{14,12},{16,18},{18,... | collective-permute-start | bytes 1032200 | tf_op jit(solution)/shard_map/ppermute | solution.py:99
  44.0 17.3 %collective-permute-start.14 = (bf16[192,1408]{1,0:T(8,128)(2,1)}, bf16[192,1408]{1,0:T(8,128)(2,1)}, u32[]{:S(2)}, u32[]{:S(2)}) collective-permute-start(bf16[192,1408]{1,0:T(8,128)(2,1)} %maximum_select_fusion.refs_12_), channel_id=1, source_target_pairs={{0,2},{2,0},{4,6},{6,4},{8,10},{10,8},{12,14},{14,12},{16,18},{18,... | collective-permute-start | bytes 1622024 | tf_op jit(solution)/shard_map/ppermute | solution.py:99
  54.8 6.5 %collective-permute-start.15 = (bf16[192,1408]{1,0:T(8,128)(2,1)}, bf16[192,1408]{1,0:T(8,128)(2,1)}, u32[]{:S(2)}, u32[]{:S(2)}) collective-permute-start(bf16[192,1408]{1,0:T(8,128)(2,1)} %collective-permute-done.13.refs_13_), channel_id=1, source_target_pairs={{0,2},{2,0},{4,6},{6,4},{8,10},{10,8},{12,14},{14,12},{16,18},{18,... | collective-permute-start | bytes 1622024 | tf_op jit(solution)/shard_map/ppermute | solution.py:99
  54.8 1.4 copy-start.9
  54.8 4.4 %collective-permute-start.8 = (bf16[192,1280]{1,0:T(8,128)(2,1)}, bf16[192,1280]{1,0:T(8,128)(2,1)}, u32[]{:S(2)}, u32[]{:S(2)}) collective-permute-start(bf16[192,1280]{1,0:T(8,128)(2,1)} %maximum_select_fusion.1.refs_8_), channel_id=1, source_target_pairs={{0,2},{2,0},{4,6},{6,4},{8,10},{10,8},{12,14},{14,12},{16,18},{18,... | collective-permute-start | bytes 1474568 | tf_op jit(solution)/shard_map/ppermute | solution.py:99
  55.3 0.8 copy-start.10
  56.1 4.8 %collective-permute-start.9 = (bf16[192,1280]{1,0:T(8,128)(2,1)}, bf16[192,1280]{1,0:T(8,128)(2,1)}, u32[]{:S(2)}, u32[]{:S(2)}) collective-permute-start(bf16[192,1280]{1,0:T(8,128)(2,1)} %collective-permute-done.7.refs_9_), channel_id=1, source_target_pairs={{0,2},{2,0},{4,6},{6,4},{8,10},{10,8},{12,14},{14,12},{16,18},{18,... | collective-permute-start | bytes 1474568 | tf_op jit(solution)/shard_map/ppermute | solution.py:99
  59.2 33.9 %collective-permute-start.16 = (bf16[1024,512]{1,0:T(8,128)(2,1)S(1)}, bf16[1024,512]{1,0:T(8,128)(2,1)S(1)}, u32[]{:S(2)}, u32[]{:S(2)}) collective-permute-start(bf16[1024,512]{1,0:T(8,128)(2,1)S(1)} %pad_maximum_fusion.1), channel_id=1, source_target_pairs={{0,1},{1,0},{2,3},{3,2},{4,5},{5,4},{6,7},{7,6},{8,9},{9,8},{10,11... | collective-permute-start | bytes 3145736 | tf_op jit(solution)/shard_map/ppermute | solution.py:442
  60.9 50.3 %collective-permute-start = (bf16[1024,512]{1,0:T(8,128)(2,1)S(1)}, bf16[1024,512]{1,0:T(8,128)(2,1)S(1)}, u32[]{:S(2)}, u32[]{:S(2)}) collective-permute-start(bf16[1024,512]{1,0:T(8,128)(2,1)S(1)} %pad_maximum_fusion.2), channel_id=1, source_target_pairs={{0,1},{1,0},{2,3},{3,2},{4,5},{5,4},{6,7},{7,6},{8,9},{9,8},{10,11... | collective-permute-start | bytes 3145736 | tf_op jit(solution)/shard_map/ppermute | solution.py:442
  91.6 38.3 %collective-permute-start.18 = (bf16[1024,512]{1,0:T(8,128)(2,1)}, bf16[1024,512]{1,0:T(8,128)(2,1)S(1)}, u32[]{:S(2)}, u32[]{:S(2)}) collective-permute-start(bf16[1024,512]{1,0:T(8,128)(2,1)} %get-tuple-element.30), channel_id=1, source_target_pairs={{0,1},{1,0},{2,3},{3,2},{4,5},{5,4},{6,7},{7,6},{8,9},{9,8},{10,11... | collective-permute-start | bytes 3145736 | tf_op jit(solution)/shard_map/ppermute | solution.py:450
  93.2 1.0 copy-start.6
  111.2 1.0 copy-start.5
  130.5 3.1 %copy-start.7 = (bf16[1024,512]{1,0:T(8,128)(2,1)S(1)}, bf16[1024,512]{1,0:T(8,128)(2,1)}, u32[]{:S(2)}) copy-start(bf16[1024,512]{1,0:T(8,128)(2,1)} %get-tuple-element.31) | copy-start | bytes 3145732
  130.5 8.0 %copy-start = (bf16[512,2560]{1,0:T(8,128)(2,1)S(1)}, bf16[512,2560]{1,0:T(8,128)(2,1)}, u32[]{:S(2)}) copy-start(bf16[512,2560]{1,0:T(8,128)(2,1)} %get-tuple-element.32.refs_0_) | copy-start | bytes 7864324
  133.5 5.0 %collective-permute-start.20 = (bf16[512,2560]{1,0:T(8,128)(2,1)S(1)}, bf16[512,2560]{1,0:T(8,128)(2,1)S(1)}, u32[]{:S(2)}, u32[]{:S(2)}) collective-permute-start(bf16[512,2560]{1,0:T(8,128)(2,1)S(1)} %broadcast_select_fusion), channel_id=1, source_target_pairs={{0,2},{2,0},{4,6},{6,4},{8,10},{10,8},{12,14},{14,12},{16,18},{18,... | collective-permute-start | bytes 7864328 | tf_op jit(solution)/shard_map/ppermute | solution.py:362
  133.6 36.7 %collective-permute-start.19 = (bf16[1024,512]{1,0:T(8,128)(2,1)S(1)}, bf16[1024,512]{1,0:T(8,128)(2,1)S(1)}, u32[]{:S(2)}, u32[]{:S(2)}) collective-permute-start(bf16[1024,512]{1,0:T(8,128)(2,1)S(1)} %copy-done.7), channel_id=1, source_target_pairs={{0,1},{1,0},{2,3},{3,2},{4,5},{5,4},{6,7},{7,6},{8,9},{9,8},{10,11... | collective-permute-start | bytes 3145736 | tf_op jit(solution)/shard_map/ppermute | solution.py:450
  138.6 10.6 %collective-permute-start.23 = (bf16[64,2560]{1,0:T(8,128)(2,1)S(1)}, bf16[64,2560]{1,0:T(8,128)(2,1)S(1)}, u32[]{:S(2)}, u32[]{:S(2)}) collective-permute-start(bf16[64,2560]{1,0:T(8,128)(2,1)S(1)} %add_convert_fusion.3), channel_id=1, source_target_pairs={{0,4},{2,6},{4,0},{6,2},{8,12},{10,14},{12,8},{14,10},{16,20},{18,... | collective-permute-start | bytes 983048 | tf_op jit(solution)/shard_map/ppermute | solution.py:362
  139.9 22.5 %collective-permute-start.21 = (bf16[128,2560]{1,0:T(8,128)(2,1)S(1)}, bf16[128,2560]{1,0:T(8,128)(2,1)S(1)}, u32[]{:S(2)}, u32[]{:S(2)}) collective-permute-start(bf16[128,2560]{1,0:T(8,128)(2,1)S(1)} %add_convert_fusion.1), channel_id=1, source_target_pairs={{0,4},{2,6},{4,0},{6,2},{8,12},{10,14},{12,8},{14,10},{16,20},{18,... | collective-permute-start | bytes 1966088 | tf_op jit(solution)/shard_map/ppermute | solution.py:362
  149.3 34.5 %copy-start.1 = (bf16[2048,512]{1,0:T(8,128)(2,1)S(1)}, bf16[2048,512]{1,0:T(8,128)(2,1)}, u32[]{:S(2)}) copy-start(bf16[2048,512]{1,0:T(8,128)(2,1)} %get-tuple-element.29.kept_ref) | copy-start | bytes 6291460
  149.3 20.9 %collective-permute-start.24 = (bf16[64,2560]{1,0:T(8,128)(2,1)S(1)}, bf16[64,2560]{1,0:T(8,128)(2,1)S(1)}, u32[]{:S(2)}, u32[]{:S(2)}) collective-permute-start(bf16[64,2560]{1,0:T(8,128)(2,1)S(1)} %add_convert_fusion.2), channel_id=1, source_target_pairs={{0,16},{2,18},{4,20},{6,22},{8,24},{10,26},{12,28},{14,30},{16,0},... | collective-permute-start | bytes 983048 | tf_op jit(solution)/shard_map/ppermute | solution.py:382
  162.7 13.3 %collective-permute-start.25 = (bf16[64,2560]{1,0:T(8,128)(2,1)S(1)}, bf16[64,2560]{1,0:T(8,128)(2,1)S(1)}, u32[]{:S(2)}, u32[]{:S(2)}) collective-permute-start(bf16[64,2560]{1,0:T(8,128)(2,1)S(1)} %get-tuple-element.42), channel_id=1, source_target_pairs={{0,24},{2,26},{4,28},{6,30},{8,0},{10,2},{12,4},{14,6},{16,8},{18,... | collective-permute-start | bytes 983048 | tf_op jit(solution)/shard_map/ppermute | solution.py:382
  165.2 18.5 %collective-permute-start.26 = (bf16[64,2560]{1,0:T(8,128)(2,1)S(1)}, bf16[64,2560]{1,0:T(8,128)(2,1)S(1)}, u32[]{:S(2)}, u32[]{:S(2)}) collective-permute-start(bf16[64,2560]{1,0:T(8,128)(2,1)S(1)} %get-tuple-element.41), channel_id=1, source_target_pairs={{0,8},{2,10},{4,12},{6,14},{8,16},{10,18},{12,20},{14,22},{16,24},... | collective-permute-start | bytes 983048 | tf_op jit(solution)/shard_map/ppermute | solution.py:382
  169.6 14.1 %collective-permute-start.22 = (bf16[64,2560]{1,0:T(8,128)(2,1)S(1)}, bf16[64,2560]{1,0:T(8,128)(2,1)S(1)}, u32[]{:S(2)}, u32[]{:S(2)}) collective-permute-start(bf16[64,2560]{1,0:T(8,128)(2,1)S(1)} %fusion.2), channel_id=1, source_target_pairs={{0,4},{2,6},{4,0},{6,2},{8,12},{10,14},{12,8},{14,10},{16,20},{18,... | collective-permute-start | bytes 983048 | tf_op jit(solution)/shard_map/ppermute | solution.py:362

commit v5 on v3

--- a/solution.py
+++ b/solution.py
@@ -84,6 +84,34 @@
     return rest + [0]
 
 
+def stage_kernel(rows, x_ref, d_ref, w_ref, head_ref, out_ref, sems):
+    jobs = [(w_ref.at[:, pl.ds(0, head_ref.shape[1])], head_ref)]
+    for i in range(GROUPS[0][1]):
+        span = pl.ds(i * rows, rows)
+        jobs.append((x_ref.at[span], out_ref.at[pl.ds(2 * i * rows, rows)]))
+        jobs.append((d_ref.at[span], out_ref.at[pl.ds((2 * i + 1) * rows, rows)]))
+    copies = [pltpu.make_async_copy(a, b, sems.at[n]) for n, (a, b) in enumerate(jobs)]
+    for copy in copies:
+        copy.start()
+    for copy in copies:
+        copy.wait()
+
+
+def stage(x, d, w_in, rows, cut):
+    anywhere = pl.BlockSpec(memory_space=pl.ANY)
+    own = x.shape[1]
+    shapes = [jax.ShapeDtypeStruct((w_in.shape[0], cut), bf16)]
+    shapes += [jax.ShapeDtypeStruct((2 * GROUPS[0][1] * rows, own), bf16)]
+    return pl.pallas_call(
+        functools.partial(stage_kernel, rows),
+        out_shape=shapes,
+        in_specs=[anywhere] * 3,
+        out_specs=[anywhere] * len(shapes),
+        scratch_shapes=[pltpu.SemaphoreType.DMA((2 * GROUPS[0][1] + 1,))],
+        cost_estimate=pl.CostEstimate(flops=0, bytes_accessed=4 * x.size, transcendentals=0),
+    )(x, d, w_in)
+
+
 def piece_order(far, cut):
     slow = split_order(far)[:-1]
     return [
@@ -94,7 +122,7 @@
     ]
 
 
-def gather_parts(shard, cut, users, user):
+def gather_parts(head, shard, users, user):
     def swap(block, bit):
         return lax.ppermute(block, "user", [(i, i ^ bit) for i in range(users)])
 
@@ -103,7 +131,7 @@
         return [block, across, swap(block, 1), swap(across, 1)]
 
     arrays, moved = spread(shard), []
-    for part in (shard[:, :cut], shard[:, cut:]):
+    for part in (head, shard[:, head.shape[1] :]):
         if moved:
             part = jnp.where(user < 0, sum(t[:1, :1] for t in moved), part)
         moved = []
@@ -444,12 +472,13 @@
     d = cotangent.reshape(hist * seq_len, own)
     blocks = sum(steps for _, steps in GROUPS)
     rows = hist // blocks * seq_len
-    far, ahead = [], None
-    for start, steps in GROUPS:
+    cut = (w_in.shape[1] + w_out.shape[1] + SLOTS) // 128 * 5 // 8 * 128
+    head, ahead = stage(x, d, w_in, rows, cut)
+    far = [exchange(ahead, tensor)]
+    for start, steps in GROUPS[1:]:
         spans = [slice(i * rows, (i + 1) * rows) for i in range(start, start + steps)]
-        if ahead is not None:
-            x, d, _ = lax.optimization_barrier((x, d, ahead))
-        ahead = jnp.concatenate([t[span] for span in spans for t in (x, d)], axis=0)
+        x_late, d_late, _ = lax.optimization_barrier((x, d, ahead))
+        ahead = jnp.concatenate([t[span] for span in spans for t in (x_late, d_late)], axis=0)
         far.append(exchange(ahead, tensor))
 
     user = lax.axis_index("user")
@@ -457,7 +486,7 @@
     slots = jnp.pad(slots, ((0, 0), (0, SLOTS // 2 - hist)), constant_values=-1)
     slots = jnp.pad(slots.reshape(1, SLOTS), ((0, w_in.shape[0] - 1), (0, 0)), constant_values=-1)
     shard = jnp.concatenate([w_in, w_out, slots], axis=1)
-    pieces = gather_parts(shard, shard.shape[1] // 256 * 128, users, user)
+    pieces = gather_parts(head, shard, users, user)
     where = jnp.stack([lax.axis_index("tensor"), user]).astype(jnp.int32)
 
     past = []

time: 186 us -> 259 us (1.39)
  Pallas kernels: 67.4 us -> 139 us
  waiting for transfers between devices: 54.1 us -> 71.5 us
  starting transfers between devices: 37.4 us -> 26.3 us
    pallas_call x0 -> x1, Pallas kernels: none -> 71.1 us  [stage(): pl.pallas_call(functools.partial(stage_kernel, rows), out_shape=shapes, i...]
    ppermute x6, waiting for transfers between devices: 6.54 us -> 17.9 us  [gather_parts(): moved.append(lax.ppermute(part, 'user', pairs))]
    ppermute x13, waiting for transfers between devices: 32.9 us -> 40.3 us  [swap(): return lax.ppermute(block, 'user', [(i, i ^ bit) for i in range(users)])]
    ppermute x3, starting transfers between devices: 10.3 us -> 3.94 us  [scatter_parts(): moved.append(lax.ppermute(block, 'user', pairs))]
    ppermute x6, starting transfers between devices: 13.2 us -> 8.49 us  [gather_parts(): moved.append(lax.ppermute(part, 'user', pairs))]
    ppermute x3, waiting for transfers between devices: 3.08 us -> 0.01 us  [scatter_parts(): moved.append(lax.ppermute(block, 'user', pairs))]
  transfers between devices with their start and end apart: 26 -> 26, of which waited for: 9 -> 11; matrix products, arithmetic and copies ran while one was open for 9% -> 5% of each run, Pallas kernels for 26% -> 46%
where the time goes in v5:
time: 259 us; the launch traced here: 256 us
  Pallas kernels  139 us (54%)
  waiting for transfers between devices  71.5 us (28%)
  starting transfers between devices  26.3 us (10%)
  local copies, waits for them, and re-layouts  9.02 us (3%)
  other arithmetic  7.54 us (3%)
  between operations  3.34 us (1%)
    pallas_call x1, Pallas kernels, stage(): pl.pallas_call(functools.partial(stage_kernel, rows), out_shape=shapes, i...  71.1 us
    pallas_call x3, Pallas kernels, group_call(): pl.pallas_call(functools.partial(group_kernel, start, steps, first, last,...  65 us
    ppermute x13, waiting for transfers between devices, swap(): return lax.ppermute(block, 'user', [(i, i ^ bit) for i in range(users)])  40.3 us
    ppermute x6, waiting for transfers between devices, gather_parts(): moved.append(lax.ppermute(part, 'user', pairs))  17.9 us
    ppermute x1, waiting for transfers between devices, give_back(): return lax.ppermute(block, 'tensor', [(0, 1), (1, 0)])  13.3 us
    ppermute x13, starting transfers between devices, swap(): return lax.ppermute(block, 'user', [(i, i ^ bit) for i in range(users)])  9.58 us
    ppermute x6, starting transfers between devices, gather_parts(): moved.append(lax.ppermute(part, 'user', pairs))  8.49 us
  transfers between devices with their start and end apart: 26, of which 11 were waited for; matrix products, arithmetic and copies ran while one was open for 5% of the time, Pallas kernels for 46%

profile of v5, /device:TPU:0, one launch (start us, length us, event | category | flops | bytes accessed | tf_op | source)
XLA Modules:
  0.0 256.3 jit_solution(8528989847591674763)
XLA Ops:
  0.6 0.7 convert_bitcast_fusion
  1.4 1.0 fusion.1.refs_4_
  2.4 3.0 %collective-permute-start.1 = (bf16[64,2688]{1,0:T(8,128)(2,1)S(1)}, bf16[64,2688]{1,0:T(8,128)(2,1)S(1)}, u32[]{:S(2)}, u32[]{:S(2)}) collective-permute-start(bf16[64,2688]{1,0:T(8,128)(2,1)S(1)} %fusion.1.refs_4_), channel_id=1, source_target_pairs={{0,4},{2,6},{4,0},{6,2},{8,12},{10,14},{12,8},{14,10},{16,20},{18,... | collective-permute-start | bytes 1032200 | tf_op jit(solution)/shard_map/ppermute | solution.py:127
  5.4 71.1 %shard_map.85 = (bf16[64,1664]{1,0:T(8,128)(2,1)}, bf16[2048,512]{1,0:T(8,128)(2,1)}) custom-call(bf16[2048,512]{1,0:T(8,128)(2,1)} %bitcast.12, bf16[2048,512]{1,0:T(8,128)(2,1)} %bitcast.18, bf16[64,2048]{1,0:T(8,128)(2,1)} %w_ref.1), custom_call_target="tpu_custom_call" | custom-call | bytes 4194304 | tf_op jit(solution)/shard_map/pallas_call | solution.py:105
  76.6 1.6 collective-permute-start.17
  78.2 1.6 collective-permute-start.6
  79.7 2.2 collective-permute-start.5
  82.0 0.8 collective-permute-start.4
  83.3 5.1 %collective-permute-done.6 = bf16[64,1664]{1,0:T(8,128)(2,1)S(1)} collective-permute-done((bf16[64,1664]{1,0:T(8,128)(2,1)}, bf16[64,1664]{1,0:T(8,128)(2,1)S(1)}, u32[]{:S(2)}, u32[]{:S(2)}) %collective-permute-start.6) | collective-permute-done | bytes 213024 | tf_op jit(solution)/shard_map/ppermute | solution.py:140
  88.4 2.3 collective-permute-done.5
  90.7 9.7 %collective-permute-done.4 = bf16[64,1664]{1,0:T(8,128)(2,1)S(1)} collective-permute-done((bf16[64,1664]{1,0:T(8,128)(2,1)}, bf16[64,1664]{1,0:T(8,128)(2,1)S(1)}, u32[]{:S(2)}, u32[]{:S(2)}) %collective-permute-start.4) | collective-permute-done | bytes 213024 | tf_op jit(solution)/shard_map/ppermute | solution.py:140
  100.4 0.7 copy-done.6
  101.0 1.6 maximum_select_fusion.refs_8_
  102.6 0.6 collective-permute-start.7
  103.2 0.5 slice.91
  103.8 1.3 slice.90
  106.3 0.5 slice.92
  107.6 3.8 %collective-permute-start.11 = (bf16[64,1024]{1,0:T(8,128)(2,1)S(1)}, bf16[64,1024]{1,0:T(8,128)(2,1)S(1)}, u32[]{:S(2)}, u32[]{:S(2)}) collective-permute-start(bf16[64,1024]{1,0:T(8,128)(2,1)S(1)} %slice_select_fusion), channel_id=1, source_target_pairs={{0,24},{2,26},{4,28},{6,30},{8,0},{10,2},{12,4},{14,6},{16,8},{18,... | collective-permute-start | bytes 393224 | tf_op jit(solution)/shard_map/ppermute | solution.py:140
  111.4 7.7 %collective-permute-done.7.refs_9_ = bf16[192,1664]{1,0:T(8,128)(2,1)} collective-permute-done((bf16[192,1664]{1,0:T(8,128)(2,1)S(1)}, bf16[192,1664]{1,0:T(8,128)(2,1)}, u32[]{:S(2)}, u32[]{:S(2)}) %collective-permute-start.7) | collective-permute-done | bytes 639008 | tf_op jit(solution)/shard_map/ppermute | solution.py:127
  119.1 1.2 slice.89
  120.3 0.8 collective-permute-done.10
  121.2 0.7 maximum_select_fusion.1.refs_12_
  121.9 1.6 collective-permute-start.13
  123.5 0.5 collective-permute-start.8
  124.0 1.7 collective-permute-done.3.refs_7_
  125.9 6.8 %collective-permute-done.13.refs_13_ = bf16[192,1024]{1,0:T(8,128)(2,1)} collective-permute-done((bf16[192,1024]{1,0:T(8,128)(2,1)S(1)}, bf16[192,1024]{1,0:T(8,128)(2,1)}, u32[]{:S(2)}, u32[]{:S(2)}) %collective-permute-start.13) | collective-permute-done | bytes 393248 | tf_op jit(solution)/shard_map/ppermute | solution.py:127
  132.8 1.1 slice.67
  134.0 1.1 slice.69
  135.1 0.7 pad_add_fusion.refs_0_
  135.9 0.6 collective-permute-start.16
  136.5 1.5 collective-permute-start
  138.0 30.2 %shard_map.86 = (bf16[2048,512]{1,0:T(8,128)(2,1)}, bf16[2048,512]{1,0:T(8,128)(2,1)}, f32[1024,2560]{1,0:T(8,128)}) custom-call(s32[2]{0:T(128)} %pad_add_fusion.refs_0_, bf16[2048,512]{1,0:T(8,128)(2,1)} %bitcast.13, bf16[2048,512]{1,0:T(8,128)(2,1)} %bitcast.21, bf16[2048,512]{1,0:T(8,128)(2,1)} %collective-permute-done.17.refs_3_, ...), custom_call_target="tpu_custom_call" | custom-call | flops 15032385536 | bytes 16777216 | tf_op jit(solution)/shard_map/pallas_call | solution.py:343
  168.2 1.0 copy-done.8
  169.2 17.0 %shard_map.87 = (bf16[2048,512]{1,0:T(8,128)(2,1)}, bf16[2048,512]{1,0:T(8,128)(2,1)}, f32[1024,2560]{1,0:T(8,128)}) custom-call(s32[2]{0:T(128)} %pad_add_fusion.refs_0_, bf16[2048,512]{1,0:T(8,128)(2,1)} %bitcast.14, bf16[2048,512]{1,0:T(8,128)(2,1)} %bitcast.22, bf16[1024,512]{1,0:T(8,128)(2,1)} %copy-done.8, ...), custom_call_target="tpu_custom_call", output_to_operand_aliasing={{0}: (17, {}), {1}: (18, {})} | custom-call | flops 7516192768 | bytes 16777216 | tf_op jit(solution)/shard_map/pallas_call | solution.py:343
  186.2 1.0 copy-done.7
  187.2 17.8 %shard_map.88 = (bf16[2048,512]{1,0:T(8,128)(2,1)}, bf16[2048,512]{1,0:T(8,128)(2,1)}, bf16[512,2560]{1,0:T(8,128)(2,1)}, bf16[512,2560]{1,0:T(8,128)(2,1)}) custom-call(s32[2]{0:T(128)} %pad_add_fusion.refs_0_, bf16[2048,512]{1,0:T(8,128)(2,1)} %bitcast.15, bf16[2048,512]{1,0:T(8,128)(2,1)} %bitcast.23, ...), custom_call_target="tpu_custom_call", output_to_operand_aliasing={{0}: (17, {}), {1}: (18, {})} | custom-call | flops 7516192768 | bytes 16777216 | tf_op jit(solution)/shard_map/pallas_call | solution.py:343
  205.1 0.6 collective-permute-start.18
  205.6 4.5 %collective-permute-done.19.refs_1_ = bf16[512,2560]{1,0:T(8,128)(2,1)S(1)} collective-permute-done((bf16[512,2560]{1,0:T(8,128)(2,1)}, bf16[512,2560]{1,0:T(8,128)(2,1)S(1)}, u32[]{:S(2)}, u32[]{:S(2)}) %collective-permute-start.19) | collective-permute-done | bytes 2621472 | tf_op jit(solution)/shard_map/ppermute | solution.py:387
  210.2 1.0 add_convert_fusion.3
  211.2 1.5 collective-permute-start.21
  212.7 1.2 add_convert_fusion.1
  213.9 0.7 collective-permute-start.23
  214.6 7.2 %collective-permute-done.21 = bf16[64,2560]{1,0:T(8,128)(2,1)S(1)} collective-permute-done((bf16[64,2560]{1,0:T(8,128)(2,1)S(1)}, bf16[64,2560]{1,0:T(8,128)(2,1)S(1)}, u32[]{:S(2)}, u32[]{:S(2)}) %collective-permute-start.21) | collective-permute-done | bytes 327712 | tf_op jit(solution)/shard_map/ppermute | solution.py:387
  222.1 1.5 collective-permute-start.20
  223.6 12.3 %collective-permute-done.23 = bf16[128,2560]{1,0:T(8,128)(2,1)S(1)} collective-permute-done((bf16[128,2560]{1,0:T(8,128)(2,1)S(1)}, bf16[128,2560]{1,0:T(8,128)(2,1)S(1)}, u32[]{:S(2)}, u32[]{:S(2)}) %collective-permute-start.23) | collective-permute-done | bytes 655392 | tf_op jit(solution)/shard_map/ppermute | solution.py:387
  236.2 3.8 %collective-permute-start.24 = (bf16[64,2560]{1,0:T(8,128)(2,1)S(1)}, bf16[64,2560]{1,0:T(8,128)(2,1)S(1)}, u32[]{:S(2)}, u32[]{:S(2)}) collective-permute-start(bf16[64,2560]{1,0:T(8,128)(2,1)S(1)} %get-tuple-element.44), channel_id=1, source_target_pairs={{0,24},{2,26},{4,28},{6,30},{8,0},{10,2},{12,4},{14,6},{16,8},{18,... | collective-permute-start | bytes 983048 | tf_op jit(solution)/shard_map/ppermute | solution.py:403
  240.0 13.3 %collective-permute-done.18.sent_ref = bf16[2048,512]{1,0:T(8,128)(2,1)S(1)} collective-permute-done((bf16[2048,512]{1,0:T(8,128)(2,1)}, bf16[2048,512]{1,0:T(8,128)(2,1)S(1)}, u32[]{:S(2)}, u32[]{:S(2)}) %collective-permute-start.18) | collective-permute-done | bytes 2097184 | tf_op jit(solution)/shard_map/ppermute | solution.py:461
  253.3 2.5 shard_map.89
  (57 shorter events, 1.9 us)
Async XLA Ops:
  2.4 116.7 %copy-start.3 = (bf16[64,2688]{1,0:T(8,128)(2,1)}, bf16[64,2688]{1,0:T(8,128)(2,1)S(1)}, u32[]{:S(2)}) copy-start(bf16[64,2688]{1,0:T(8,128)(2,1)S(1)} %fusion.1.refs_4_) | copy-start | bytes 1032196
  2.4 80.4 %collective-permute-start.1 = (bf16[64,2688]{1,0:T(8,128)(2,1)S(1)}, bf16[64,2688]{1,0:T(8,128)(2,1)S(1)}, u32[]{:S(2)}, u32[]{:S(2)}) collective-permute-start(bf16[64,2688]{1,0:T(8,128)(2,1)S(1)} %fusion.1.refs_4_), channel_id=1, source_target_pairs={{0,4},{2,6},{4,0},{6,2},{8,12},{10,14},{12,8},{14,10},{16,20},{18,... | collective-permute-start | bytes 1032200 | tf_op jit(solution)/shard_map/ppermute | solution.py:127
  76.6 56.2 %copy-start.2 = (bf16[16,128,512]{2,1,0:T(8,128)(2,1)S(1)}, bf16[16,128,512]{2,1,0:T(8,128)(2,1)}, u32[]{:S(2)}) copy-start(bf16[16,128,512]{2,1,0:T(8,128)(2,1)} %param.6) | copy-start | bytes 6291460
  76.6 61.4 %collective-permute-start.17 = (bf16[2048,512]{1,0:T(8,128)(2,1)}, bf16[2048,512]{1,0:T(8,128)(2,1)}, u32[]{:S(2)}, u32[]{:S(2)}) collective-permute-start(bf16[2048,512]{1,0:T(8,128)(2,1)} %get-tuple-element.22), channel_id=1, source_target_pairs={{0,1},{1,0},{2,3},{3,2},{4,5},{5,4},{6,7},{7,6},{8,9},{9,8},{10,11... | collective-permute-start | bytes 6291464 | tf_op jit(solution)/shard_map/ppermute | solution.py:453
  78.2 10.2 %collective-permute-start.6 = (bf16[64,1664]{1,0:T(8,128)(2,1)}, bf16[64,1664]{1,0:T(8,128)(2,1)S(1)}, u32[]{:S(2)}, u32[]{:S(2)}) collective-permute-start(bf16[64,1664]{1,0:T(8,128)(2,1)} %get-tuple-element.27), channel_id=1, source_target_pairs={{0,8},{2,10},{4,12},{6,14},{8,16},{10,18},{12,20},{14,22},{16,24},... | collective-permute-start | bytes 638984 | tf_op jit(solution)/shard_map/ppermute | solution.py:140
  79.7 10.9 %collective-permute-start.5 = (bf16[64,1664]{1,0:T(8,128)(2,1)}, bf16[64,1664]{1,0:T(8,128)(2,1)S(1)}, u32[]{:S(2)}, u32[]{:S(2)}) collective-permute-start(bf16[64,1664]{1,0:T(8,128)(2,1)} %get-tuple-element.27), channel_id=1, source_target_pairs={{0,24},{2,26},{4,28},{6,30},{8,0},{10,2},{12,4},{14,6},{16,8},{18,... | collective-permute-start | bytes 638984 | tf_op jit(solution)/shard_map/ppermute | solution.py:140
  82.0 18.4 %collective-permute-start.4 = (bf16[64,1664]{1,0:T(8,128)(2,1)}, bf16[64,1664]{1,0:T(8,128)(2,1)S(1)}, u32[]{:S(2)}, u32[]{:S(2)}) collective-permute-start(bf16[64,1664]{1,0:T(8,128)(2,1)} %get-tuple-element.27), channel_id=1, source_target_pairs={{0,16},{2,18},{4,20},{6,22},{8,24},{10,26},{12,28},{14,30},{16,0},... | collective-permute-start | bytes 638984 | tf_op jit(solution)/shard_map/ppermute | solution.py:140
  82.8 17.6 %copy-start.9 = (bf16[64,2688]{1,0:T(8,128)(2,1)}, bf16[64,2688]{1,0:T(8,128)(2,1)S(1)}, u32[]{:S(2)}) copy-start(bf16[64,2688]{1,0:T(8,128)(2,1)S(1)} %collective-permute-done.1.refs_5_) | copy-start | bytes 1032196
  100.4 0.7 copy-start.6
  102.6 31.4 %copy-start.4 = (bf16[192,1664]{1,0:T(8,128)(2,1)}, bf16[192,1664]{1,0:T(8,128)(2,1)S(1)}, u32[]{:S(2)}) copy-start(bf16[192,1664]{1,0:T(8,128)(2,1)S(1)} %maximum_select_fusion.refs_8_) | copy-start | bytes 1916932
  102.6 16.5 %collective-permute-start.7 = (bf16[192,1664]{1,0:T(8,128)(2,1)S(1)}, bf16[192,1664]{1,0:T(8,128)(2,1)}, u32[]{:S(2)}, u32[]{:S(2)}) collective-permute-start(bf16[192,1664]{1,0:T(8,128)(2,1)S(1)} %maximum_select_fusion.refs_8_), channel_id=1, source_target_pairs={{0,4},{2,6},{4,0},{6,2},{8,12},{10,14},{12,8},{14,10},{16,20},{18,... | collective-permute-start | bytes 1916936 | tf_op jit(solution)/shard_map/ppermute | solution.py:127
  107.5 12.8 %collective-permute-start.12 = (bf16[64,1024]{1,0:T(8,128)(2,1)S(1)}, bf16[64,1024]{1,0:T(8,128)(2,1)S(1)}, u32[]{:S(2)}, u32[]{:S(2)}) collective-permute-start(bf16[64,1024]{1,0:T(8,128)(2,1)S(1)} %slice_select_fusion), channel_id=1, source_target_pairs={{0,8},{2,10},{4,12},{6,14},{8,16},{10,18},{12,20},{14,22},{16,24},... | collective-permute-start | bytes 393224 | tf_op jit(solution)/shard_map/ppermute | solution.py:140
  107.6 12.7 %collective-permute-start.11 = (bf16[64,1024]{1,0:T(8,128)(2,1)S(1)}, bf16[64,1024]{1,0:T(8,128)(2,1)S(1)}, u32[]{:S(2)}, u32[]{:S(2)}) collective-permute-start(bf16[64,1024]{1,0:T(8,128)(2,1)S(1)} %slice_select_fusion), channel_id=1, source_target_pairs={{0,24},{2,26},{4,28},{6,30},{8,0},{10,2},{12,4},{14,6},{16,8},{18,... | collective-permute-start | bytes 393224 | tf_op jit(solution)/shard_map/ppermute | solution.py:140
  111.4 9.7 %collective-permute-start.10 = (bf16[64,1024]{1,0:T(8,128)(2,1)S(1)}, bf16[64,1024]{1,0:T(8,128)(2,1)S(1)}, u32[]{:S(2)}, u32[]{:S(2)}) collective-permute-start(bf16[64,1024]{1,0:T(8,128)(2,1)S(1)} %slice_select_fusion), channel_id=1, source_target_pairs={{0,16},{2,18},{4,20},{6,22},{8,24},{10,26},{12,28},{14,30},{16,0},... | collective-permute-start | bytes 393224 | tf_op jit(solution)/shard_map/ppermute | solution.py:140
  119.1 4.8 %collective-permute-start.2 = (bf16[64,2688]{1,0:T(8,128)(2,1)S(1)}, bf16[64,2688]{1,0:T(8,128)(2,1)S(1)}, u32[]{:S(2)}, u32[]{:S(2)}) collective-permute-start(bf16[64,2688]{1,0:T(8,128)(2,1)S(1)} %fusion.1.refs_4_), channel_id=1, source_target_pairs={{0,2},{2,0},{4,6},{6,4},{8,10},{10,8},{12,14},{14,12},{16,18},{18,... | collective-permute-start | bytes 1032200 | tf_op jit(solution)/shard_map/ppermute | solution.py:127
  121.9 12.1 %copy-start.5 = (bf16[192,1024]{1,0:T(8,128)(2,1)}, bf16[192,1024]{1,0:T(8,128)(2,1)S(1)}, u32[]{:S(2)}) copy-start(bf16[192,1024]{1,0:T(8,128)(2,1)S(1)} %maximum_select_fusion.1.refs_12_) | copy-start | bytes 1179652
  121.9 10.9 %collective-permute-start.13 = (bf16[192,1024]{1,0:T(8,128)(2,1)S(1)}, bf16[192,1024]{1,0:T(8,128)(2,1)}, u32[]{:S(2)}, u32[]{:S(2)}) collective-permute-start(bf16[192,1024]{1,0:T(8,128)(2,1)S(1)} %maximum_select_fusion.1.refs_12_), channel_id=1, source_target_pairs={{0,4},{2,6},{4,0},{6,2},{8,12},{10,14},{12,8},{14,10},{16,20},{18,... | collective-permute-start | bytes 1179656 | tf_op jit(solution)/shard_map/ppermute | solution.py:127
  123.5 2.3 collective-permute-start.3
  123.5 12.4 %collective-permute-start.8 = (bf16[192,1664]{1,0:T(8,128)(2,1)S(1)}, bf16[192,1664]{1,0:T(8,128)(2,1)}, u32[]{:S(2)}, u32[]{:S(2)}) collective-permute-start(bf16[192,1664]{1,0:T(8,128)(2,1)S(1)} %maximum_select_fusion.refs_8_), channel_id=1, source_target_pairs={{0,2},{2,0},{4,6},{6,4},{8,10},{10,8},{12,14},{14,12},{16,18},{18,... | collective-permute-start | bytes 1916936 | tf_op jit(solution)/shard_map/ppermute | solution.py:127
  124.0 8.8 %copy-start.10 = (bf16[64,2688]{1,0:T(8,128)(2,1)}, bf16[64,2688]{1,0:T(8,128)(2,1)S(1)}, u32[]{:S(2)}) copy-start(bf16[64,2688]{1,0:T(8,128)(2,1)S(1)} %collective-permute-done.2.refs_6_) | copy-start | bytes 1032196
  124.0 14.0 %collective-permute-start.9 = (bf16[192,1664]{1,0:T(8,128)(2,1)}, bf16[192,1664]{1,0:T(8,128)(2,1)}, u32[]{:S(2)}, u32[]{:S(2)}) collective-permute-start(bf16[192,1664]{1,0:T(8,128)(2,1)} %collective-permute-done.7.refs_9_), channel_id=1, source_target_pairs={{0,2},{2,0},{4,6},{6,4},{8,10},{10,8},{12,14},{14,12},{16,18},{18,... | collective-permute-start | bytes 1916936 | tf_op jit(solution)/shard_map/ppermute | solution.py:127
  125.8 7.0 %copy-start.11 = (bf16[64,2688]{1,0:T(8,128)(2,1)}, bf16[64,2688]{1,0:T(8,128)(2,1)S(1)}, u32[]{:S(2)}) copy-start(bf16[64,2688]{1,0:T(8,128)(2,1)S(1)} %collective-permute-done.3.refs_7_) | copy-start | bytes 1032196
  125.8 10.7 %collective-permute-start.14 = (bf16[192,1024]{1,0:T(8,128)(2,1)S(1)}, bf16[192,1024]{1,0:T(8,128)(2,1)}, u32[]{:S(2)}, u32[]{:S(2)}) collective-permute-start(bf16[192,1024]{1,0:T(8,128)(2,1)S(1)} %maximum_select_fusion.1.refs_12_), channel_id=1, source_target_pairs={{0,2},{2,0},{4,6},{6,4},{8,10},{10,8},{12,14},{14,12},{16,18},{18,... | collective-permute-start | bytes 1179656 | tf_op jit(solution)/shard_map/ppermute | solution.py:127
  132.8 5.2 %collective-permute-start.15 = (bf16[192,1024]{1,0:T(8,128)(2,1)}, bf16[192,1024]{1,0:T(8,128)(2,1)}, u32[]{:S(2)}, u32[]{:S(2)}) collective-permute-start(bf16[192,1024]{1,0:T(8,128)(2,1)} %collective-permute-done.13.refs_13_), channel_id=1, source_target_pairs={{0,2},{2,0},{4,6},{6,4},{8,10},{10,8},{12,14},{14,12},{16,18},{18,... | collective-permute-start | bytes 1179656 | tf_op jit(solution)/shard_map/ppermute | solution.py:127
  135.9 32.3 %collective-permute-start.16 = (bf16[1024,512]{1,0:T(8,128)(2,1)S(1)}, bf16[1024,512]{1,0:T(8,128)(2,1)S(1)}, u32[]{:S(2)}, u32[]{:S(2)}) collective-permute-start(bf16[1024,512]{1,0:T(8,128)(2,1)S(1)} %pad_maximum_fusion), channel_id=1, source_target_pairs={{0,1},{1,0},{2,3},{3,2},{4,5},{5,4},{6,7},{7,6},{8,9},{9,8},{10,11... | collective-permute-start | bytes 3145736 | tf_op jit(solution)/shard_map/ppermute | solution.py:453
  136.5 49.7 %collective-permute-start = (bf16[1024,512]{1,0:T(8,128)(2,1)S(1)}, bf16[1024,512]{1,0:T(8,128)(2,1)S(1)}, u32[]{:S(2)}, u32[]{:S(2)}) collective-permute-start(bf16[1024,512]{1,0:T(8,128)(2,1)S(1)} %pad_maximum_fusion.1), channel_id=1, source_target_pairs={{0,1},{1,0},{2,3},{3,2},{4,5},{5,4},{6,7},{7,6},{8,9},{9,8},{10,11... | collective-permute-start | bytes 3145736 | tf_op jit(solution)/shard_map/ppermute | solution.py:453
  168.2 1.0 copy-start.8
  186.2 1.0 copy-start.7
  205.0 16.9 %copy-start = (bf16[512,2560]{1,0:T(8,128)(2,1)S(1)}, bf16[512,2560]{1,0:T(8,128)(2,1)}, u32[]{:S(2)}) copy-start(bf16[512,2560]{1,0:T(8,128)(2,1)} %get-tuple-element.36.refs_0_) | copy-start | bytes 7864324
  205.0 5.2 %collective-permute-start.19 = (bf16[512,2560]{1,0:T(8,128)(2,1)}, bf16[512,2560]{1,0:T(8,128)(2,1)S(1)}, u32[]{:S(2)}, u32[]{:S(2)}) collective-permute-start(bf16[512,2560]{1,0:T(8,128)(2,1)} %get-tuple-element.37), channel_id=1, source_target_pairs={{0,2},{2,0},{4,6},{6,4},{8,10},{10,8},{12,14},{14,12},{16,18},{18,... | collective-permute-start | bytes 7864328 | tf_op jit(solution)/shard_map/ppermute | solution.py:387
  205.1 48.3 %collective-permute-start.18 = (bf16[2048,512]{1,0:T(8,128)(2,1)}, bf16[2048,512]{1,0:T(8,128)(2,1)S(1)}, u32[]{:S(2)}, u32[]{:S(2)}) collective-permute-start(bf16[2048,512]{1,0:T(8,128)(2,1)} %get-tuple-element.35), channel_id=1, source_target_pairs={{0,1},{1,0},{2,3},{3,2},{4,5},{5,4},{6,7},{7,6},{8,9},{9,8},{10,11... | collective-permute-start | bytes 6291464 | tf_op jit(solution)/shard_map/ppermute | solution.py:461
  211.2 10.6 %collective-permute-start.21 = (bf16[64,2560]{1,0:T(8,128)(2,1)S(1)}, bf16[64,2560]{1,0:T(8,128)(2,1)S(1)}, u32[]{:S(2)}, u32[]{:S(2)}) collective-permute-start(bf16[64,2560]{1,0:T(8,128)(2,1)S(1)} %add_convert_fusion.3), channel_id=1, source_target_pairs={{0,4},{2,6},{4,0},{6,2},{8,12},{10,14},{12,8},{14,10},{16,20},{18,... | collective-permute-start | bytes 983048 | tf_op jit(solution)/shard_map/ppermute | solution.py:387
  213.9 22.0 %collective-permute-start.23 = (bf16[128,2560]{1,0:T(8,128)(2,1)S(1)}, bf16[128,2560]{1,0:T(8,128)(2,1)S(1)}, u32[]{:S(2)}, u32[]{:S(2)}) collective-permute-start(bf16[128,2560]{1,0:T(8,128)(2,1)S(1)} %add_convert_fusion.1), channel_id=1, source_target_pairs={{0,4},{2,6},{4,0},{6,2},{8,12},{10,14},{12,8},{14,10},{16,20},{18,... | collective-permute-start | bytes 1966088 | tf_op jit(solution)/shard_map/ppermute | solution.py:387
  222.0 31.3 %copy-start.1 = (bf16[2048,512]{1,0:T(8,128)(2,1)S(1)}, bf16[2048,512]{1,0:T(8,128)(2,1)}, u32[]{:S(2)}) copy-start(bf16[2048,512]{1,0:T(8,128)(2,1)} %get-tuple-element.34.kept_ref) | copy-start | bytes 6291460
  222.0 31.3 %collective-permute-start.22 = (bf16[64,2560]{1,0:T(8,128)(2,1)S(1)}, bf16[64,2560]{1,0:T(8,128)(2,1)S(1)}, u32[]{:S(2)}, u32[]{:S(2)}) collective-permute-start(bf16[64,2560]{1,0:T(8,128)(2,1)S(1)} %get-tuple-element.41), channel_id=1, source_target_pairs={{0,16},{2,18},{4,20},{6,22},{8,24},{10,26},{12,28},{14,30},{16,0},... | collective-permute-start | bytes 983048 | tf_op jit(solution)/shard_map/ppermute | solution.py:403
  222.1 31.2 %collective-permute-start.20 = (bf16[64,2560]{1,0:T(8,128)(2,1)S(1)}, bf16[64,2560]{1,0:T(8,128)(2,1)S(1)}, u32[]{:S(2)}, u32[]{:S(2)}) collective-permute-start(bf16[64,2560]{1,0:T(8,128)(2,1)S(1)} %get-tuple-element.42), channel_id=1, source_target_pairs={{0,4},{2,6},{4,0},{6,2},{8,12},{10,14},{12,8},{14,10},{16,20},{18,... | collective-permute-start | bytes 983048 | tf_op jit(solution)/shard_map/ppermute | solution.py:387
  236.2 17.2 %collective-permute-start.25 = (bf16[64,2560]{1,0:T(8,128)(2,1)S(1)}, bf16[64,2560]{1,0:T(8,128)(2,1)S(1)}, u32[]{:S(2)}, u32[]{:S(2)}) collective-permute-start(bf16[64,2560]{1,0:T(8,128)(2,1)S(1)} %get-tuple-element.43), channel_id=1, source_target_pairs={{0,8},{2,10},{4,12},{6,14},{8,16},{10,18},{12,20},{14,22},{16,24},... | collective-permute-start | bytes 983048 | tf_op jit(solution)/shard_map/ppermute | solution.py:403
  236.2 17.1 %collective-permute-start.24 = (bf16[64,2560]{1,0:T(8,128)(2,1)S(1)}, bf16[64,2560]{1,0:T(8,128)(2,1)S(1)}, u32[]{:S(2)}, u32[]{:S(2)}) collective-permute-start(bf16[64,2560]{1,0:T(8,128)(2,1)S(1)} %get-tuple-element.44), channel_id=1, source_target_pairs={{0,24},{2,26},{4,28},{6,30},{8,0},{10,2},{12,4},{14,6},{16,8},{18,... | collective-permute-start | bytes 983048 | tf_op jit(solution)/shard_map/ppermute | solution.py:403

commit v6 on v3

--- a/solution.py
+++ b/solution.py
@@ -202,10 +202,6 @@
         nt_s[:own, here] = bo.T
         nt_s[own:, here] = br.T
     only(0, loaded)
-    for h in range(heads):
-        c = slice(h * 4 * HEAD_DIM, (h + 1) * 4 * HEAD_DIM)
-        silu, slope_s[:, c] = gates(dot_nn(nb_s[...], w_s[:, c]))
-        g_s[:, c] = silu.astype(bf16)
     table = w_s[:, cols:].astype(f32)
     lengths = pltpu.roll(table, SLOTS // 2, 1)
     lane = lax.broadcasted_iota(jnp.int32, (1, SLOTS), 1)
@@ -269,15 +265,21 @@
         ship(lo, wide)
 
     block = 4 * HEAD_DIM
-    stride = max(1, 8 // histories)
-    for lo in range(0, heads, stride):
-        hi = min(lo + stride, heads)
-        units = [(h, n) for h in range(lo, hi) for n in range(histories)]
+
+    def project(h):
+        c = slice(h * block, (h + 1) * block)
+        silu, slope_s[:, c] = gates(dot_nn(nb_s[...], w_s[:, c]))
+        g_s[:, c] = silu.astype(bf16)
+
+    project(0)
+    for h in range(heads):
+        if h + 1 < heads:
+            project(h + 1)
+        units = [(h, n) for n in range(histories)]
         attention(units, causal, g_s, dh_s, slope_s, hb_s, dz_s)
-        for h in range(max(0, lo - stride), lo):
-            add(nt_s, dz_s.at[:, h * block : (h + 1) * block], h * block, block)
-    for h in range((heads - 1) // stride * stride, heads):
-        add(nt_s, dz_s.at[:, h * block : (h + 1) * block], h * block, block)
+        if h > 0:
+            add(nt_s, dz_s.at[:, (h - 1) * block : h * block], (h - 1) * block, block)
+    add(nt_s, dz_s.at[:, (heads - 1) * block : cols_in], (heads - 1) * block, block)
     add(dt_s, hb_s, cols_in, heads * HEAD_DIM)
     dn_all = dot_nt(dz_s[...], w_s[:, :cols_in])
     for here, rstd in zip(halves, rstds):

time: 186 us -> 195 us (1.048)
  Pallas kernels: 67.4 us -> 77.2 us
    pallas_call x3, Pallas kernels: 65 us -> 74.8 us  [group_call(): pl.pallas_call(functools.partial(group_kernel, start, steps, first, last,...]
  transfers between devices with their start and end apart: 26 -> 26, of which waited for: 9 -> 9; matrix products, arithmetic and copies ran while one was open for 9% -> 9% of each run, Pallas kernels for 26% -> 28%
where the time goes in v6:
time: 195 us; the launch traced here: 192 us
  Pallas kernels  77.2 us (40%)
  waiting for transfers between devices  54.2 us (28%)
  starting transfers between devices  37.4 us (19%)
  local copies, waits for them, and re-layouts  10.8 us (6%)
  other arithmetic  9.68 us (5%)
  between operations  2.96 us (2%)
    pallas_call x3, Pallas kernels, group_call(): pl.pallas_call(functools.partial(group_kernel, start, steps, first, last,...  74.8 us
    ppermute x13, waiting for transfers between devices, swap(): return lax.ppermute(block, 'user', [(i, i ^ bit) for i in range(users)])  33 us
    ppermute x6, starting transfers between devices, gather_parts(): moved.append(lax.ppermute(part, 'user', pairs))  13.2 us
    ppermute x1, waiting for transfers between devices, give_back(): return lax.ppermute(block, 'tensor', [(0, 1), (1, 0)])  11.6 us
    ppermute x3, starting transfers between devices, scatter_parts(): moved.append(lax.ppermute(block, 'user', pairs))  10.3 us
    ppermute x13, starting transfers between devices, swap(): return lax.ppermute(block, 'user', [(i, i ^ bit) for i in range(users)])  8.65 us
    ppermute x6, waiting for transfers between devices, gather_parts(): moved.append(lax.ppermute(part, 'user', pairs))  6.54 us
  transfers between devices with their start and end apart: 26, of which 9 were waited for; matrix products, arithmetic and copies ran while one was open for 9% of the time, Pallas kernels for 28%

profile of v6, /device:TPU:0, one launch (start us, length us, event | category | flops | bytes accessed | tf_op | source)
XLA Modules:
  0.0 192.3 jit_solution(11155817521671258296)
XLA Ops:
  0.6 1.1 slice.106
  1.7 4.1 %collective-permute-start.4 = (bf16[64,1280]{1,0:T(8,128)(2,1)S(1)}, bf16[64,1280]{1,0:T(8,128)(2,1)S(1)}, u32[]{:S(2)}, u32[]{:S(2)}) collective-permute-start(bf16[64,1280]{1,0:T(8,128)(2,1)S(1)} %slice.106), channel_id=1, source_target_pairs={{0,16},{2,18},{4,20},{6,22},{8,24},{10,26},{12,28},{14,30},{16,0},... | collective-permute-start | bytes 491528 | tf_op jit(solution)/shard_map/ppermute | solution.py:112
  5.8 1.3 collective-permute-start.5
  7.2 0.7 collective-permute-start.6
  7.9 0.7 convert_bitcast_fusion
  8.6 1.0 fusion.1.refs_4_
  9.7 1.6 collective-permute-start.1
  11.2 1.3 fusion.5
  12.6 1.5 pad_maximum_fusion
  14.0 1.5 collective-permute-start.17
  15.6 0.5 slice.126
  18.3 0.5 slice.128
  19.5 0.6 slice.124
  20.1 1.5 maximum_select_fusion.1.refs_8_
  21.6 1.5 collective-permute-start.7
  23.1 5.0 %collective-permute-start.10 = (bf16[64,1408]{1,0:T(8,128)(2,1)S(1)}, bf16[64,1408]{1,0:T(8,128)(2,1)S(1)}, u32[]{:S(2)}, u32[]{:S(2)}) collective-permute-start(bf16[64,1408]{1,0:T(8,128)(2,1)S(1)} %slice_select_fusion), channel_id=1, source_target_pairs={{0,16},{2,18},{4,20},{6,22},{8,24},{10,26},{12,28},{14,30},{16,0},... | collective-permute-start | bytes 540680 | tf_op jit(solution)/shard_map/ppermute | solution.py:112
  28.2 2.0 %collective-permute-start.11 = (bf16[64,1408]{1,0:T(8,128)(2,1)S(1)}, bf16[64,1408]{1,0:T(8,128)(2,1)S(1)}, u32[]{:S(2)}, u32[]{:S(2)}) collective-permute-start(bf16[64,1408]{1,0:T(8,128)(2,1)S(1)} %slice_select_fusion), channel_id=1, source_target_pairs={{0,24},{2,26},{4,28},{6,30},{8,0},{10,2},{12,4},{14,6},{16,8},{18,... | collective-permute-start | bytes 540680 | tf_op jit(solution)/shard_map/ppermute | solution.py:112
  30.2 3.8 %collective-permute-done.7.refs_9_ = bf16[192,1280]{1,0:T(8,128)(2,1)} collective-permute-done((bf16[192,1280]{1,0:T(8,128)(2,1)}, bf16[192,1280]{1,0:T(8,128)(2,1)}, u32[]{:S(2)}, u32[]{:S(2)}) %collective-permute-start.7) | collective-permute-done | bytes 491552 | tf_op jit(solution)/shard_map/ppermute | solution.py:99
  34.0 1.2 slice.125
  35.2 6.1 %collective-permute-done.10 = bf16[64,1408]{1,0:T(8,128)(2,1)S(1)} collective-permute-done((bf16[64,1408]{1,0:T(8,128)(2,1)S(1)}, bf16[64,1408]{1,0:T(8,128)(2,1)S(1)}, u32[]{:S(2)}, u32[]{:S(2)}) %collective-permute-start.10) | collective-permute-done | bytes 180256 | tf_op jit(solution)/shard_map/ppermute | solution.py:112
  41.3 1.5 maximum_select_fusion.refs_12_
  42.8 0.8 collective-permute-start.13
  44.1 10.8 %collective-permute-done.13.refs_13_ = bf16[192,1408]{1,0:T(8,128)(2,1)} collective-permute-done((bf16[192,1408]{1,0:T(8,128)(2,1)}, bf16[192,1408]{1,0:T(8,128)(2,1)}, u32[]{:S(2)}, u32[]{:S(2)}) %collective-permute-start.13) | collective-permute-done | bytes 540704 | tf_op jit(solution)/shard_map/ppermute | solution.py:99
  55.4 0.8 copy-done.9
  56.3 1.1 slice.102
  57.5 1.1 slice.104
  58.6 0.6 pad_add_fusion.refs_0_
  59.3 1.6 collective-permute-start.16
  61.4 33.4 %shard_map.85 = (bf16[2048,512]{1,0:T(8,128)(2,1)}, bf16[2048,512]{1,0:T(8,128)(2,1)}, f32[1024,2560]{1,0:T(8,128)}) custom-call(s32[2]{0:T(128)} %pad_add_fusion.refs_0_, bf16[2048,512]{1,0:T(8,128)(2,1)} %bitcast.16, bf16[2048,512]{1,0:T(8,128)(2,1)} %bitcast.23, bf16[2048,512]{1,0:T(8,128)(2,1)} %collective-permute-done.17.refs_3_, ...), custom_call_target="tpu_custom_call" | custom-call | flops 15032385536 | bytes 16777216 | tf_op jit(solution)/shard_map/pallas_call | solution.py:317
  94.8 1.0 copy-done.6
  95.8 20.3 %shard_map.86 = (bf16[2048,512]{1,0:T(8,128)(2,1)}, bf16[2048,512]{1,0:T(8,128)(2,1)}, f32[1024,2560]{1,0:T(8,128)}) custom-call(s32[2]{0:T(128)} %pad_add_fusion.refs_0_, bf16[2048,512]{1,0:T(8,128)(2,1)} %bitcast.17, bf16[2048,512]{1,0:T(8,128)(2,1)} %bitcast.24, bf16[1024,512]{1,0:T(8,128)(2,1)} %copy-done.6, ...), custom_call_target="tpu_custom_call", output_to_operand_aliasing={{0}: (17, {}), {1}: (18, {})} | custom-call | flops 7516192768 | bytes 16777216 | tf_op jit(solution)/shard_map/pallas_call | solution.py:317
  116.1 1.0 copy-done.5
  117.1 21.1 %shard_map.87 = (bf16[2048,512]{1,0:T(8,128)(2,1)}, bf16[2048,512]{1,0:T(8,128)(2,1)}, bf16[512,2560]{1,0:T(8,128)(2,1)}, bf16[512,2560]{1,0:T(8,128)(2,1)}) custom-call(s32[2]{0:T(128)} %pad_add_fusion.refs_0_, bf16[2048,512]{1,0:T(8,128)(2,1)} %bitcast.18, bf16[2048,512]{1,0:T(8,128)(2,1)} %bitcast.25, ...), custom_call_target="tpu_custom_call", output_to_operand_aliasing={{0}: (17, {}), {1}: (18, {})} | custom-call | flops 7516192768 | bytes 16777216 | tf_op jit(solution)/shard_map/pallas_call | solution.py:317
  138.3 1.6 collective-permute-start.18
  139.9 3.5 %collective-permute-done.19.refs_1_ = bf16[512,2560]{1,0:T(8,128)(2,1)S(1)} collective-permute-done((bf16[512,2560]{1,0:T(8,128)(2,1)}, bf16[512,2560]{1,0:T(8,128)(2,1)S(1)}, u32[]{:S(2)}, u32[]{:S(2)}) %collective-permute-start.19) | collective-permute-done | bytes 2621472 | tf_op jit(solution)/shard_map/ppermute | solution.py:361
  143.4 1.0 add_convert_fusion.3
  144.5 1.4 collective-permute-start.21
  145.9 1.2 add_convert_fusion.1
  147.1 0.7 collective-permute-start.23
  147.9 7.2 %collective-permute-done.21 = bf16[64,2560]{1,0:T(8,128)(2,1)S(1)} collective-permute-done((bf16[64,2560]{1,0:T(8,128)(2,1)S(1)}, bf16[64,2560]{1,0:T(8,128)(2,1)S(1)}, u32[]{:S(2)}, u32[]{:S(2)}) %collective-permute-start.21) | collective-permute-done | bytes 327712 | tf_op jit(solution)/shard_map/ppermute | solution.py:361
  155.3 1.4 collective-permute-start.20
  156.7 4.8 %collective-permute-start.22 = (bf16[64,2560]{1,0:T(8,128)(2,1)S(1)}, bf16[64,2560]{1,0:T(8,128)(2,1)S(1)}, u32[]{:S(2)}, u32[]{:S(2)}) collective-permute-start(bf16[64,2560]{1,0:T(8,128)(2,1)S(1)} %get-tuple-element.37), channel_id=1, source_target_pairs={{0,16},{2,18},{4,20},{6,22},{8,24},{10,26},{12,28},{14,30},{16,0},... | collective-permute-start | bytes 983048 | tf_op jit(solution)/shard_map/ppermute | solution.py:377
  161.5 7.6 %collective-permute-done.23 = bf16[128,2560]{1,0:T(8,128)(2,1)S(1)} collective-permute-done((bf16[128,2560]{1,0:T(8,128)(2,1)S(1)}, bf16[128,2560]{1,0:T(8,128)(2,1)S(1)}, u32[]{:S(2)}, u32[]{:S(2)}) %collective-permute-start.23) | collective-permute-done | bytes 655392 | tf_op jit(solution)/shard_map/ppermute | solution.py:361
  169.4 2.6 %collective-permute-start.24 = (bf16[64,2560]{1,0:T(8,128)(2,1)S(1)}, bf16[64,2560]{1,0:T(8,128)(2,1)S(1)}, u32[]{:S(2)}, u32[]{:S(2)}) collective-permute-start(bf16[64,2560]{1,0:T(8,128)(2,1)S(1)} %get-tuple-element.44), channel_id=1, source_target_pairs={{0,24},{2,26},{4,28},{6,30},{8,0},{10,2},{12,4},{14,6},{16,8},{18,... | collective-permute-start | bytes 983048 | tf_op jit(solution)/shard_map/ppermute | solution.py:377
  172.0 3.0 %collective-permute-start.25 = (bf16[64,2560]{1,0:T(8,128)(2,1)S(1)}, bf16[64,2560]{1,0:T(8,128)(2,1)S(1)}, u32[]{:S(2)}, u32[]{:S(2)}) collective-permute-start(bf16[64,2560]{1,0:T(8,128)(2,1)S(1)} %get-tuple-element.43), channel_id=1, source_target_pairs={{0,8},{2,10},{4,12},{6,14},{8,16},{10,18},{12,20},{14,22},{16,24},... | collective-permute-start | bytes 983048 | tf_op jit(solution)/shard_map/ppermute | solution.py:377
  175.0 11.6 %collective-permute-done.18.sent_ref = bf16[2048,512]{1,0:T(8,128)(2,1)S(1)} collective-permute-done((bf16[2048,512]{1,0:T(8,128)(2,1)}, bf16[2048,512]{1,0:T(8,128)(2,1)S(1)}, u32[]{:S(2)}, u32[]{:S(2)}) %collective-permute-start.18) | collective-permute-done | bytes 2097184 | tf_op jit(solution)/shard_map/ppermute | solution.py:435
  186.6 3.1 %collective-permute-done.25.refs_5_ = bf16[64,2560]{1,0:T(8,128)(2,1)S(1)} collective-permute-done((bf16[64,2560]{1,0:T(8,128)(2,1)S(1)}, bf16[64,2560]{1,0:T(8,128)(2,1)S(1)}, u32[]{:S(2)}, u32[]{:S(2)}) %collective-permute-start.25) | collective-permute-done | bytes 327712 | tf_op jit(solution)/shard_map/ppermute | solution.py:377
  189.6 2.4 %shard_map.88 = (bf16[2048,512]{1,0:T(8,128)(2,1)}, f32[64,2048]{1,0:T(8,128)}, f32[64,512]{1,0:T(8,128)}) custom-call(bf16[2048,512]{1,0:T(8,128)(2,1)S(1)} %copy-done.1, bf16[2048,512]{1,0:T(8,128)(2,1)S(1)} %collective-permute-done.18.sent_ref, bf16[512,2560]{1,0:T(8,128)(2,1)S(1)} %copy-done, bf16[512,2560]{1,0:T(8,128)(2,1)S(1)} %collective-permute-done.19.refs_1_, ...), custom_call_target="tpu_custom_call" | custom-call | flops 1048576 | bytes 12582912 | tf_op jit(solution)/shard_map/pallas_call | solution.py:404
  (56 shorter events, 3.6 us)
Async XLA Ops:
  0.6 11.9 %copy-start.3 = (bf16[16,128,512]{2,1,0:T(8,128)(2,1)S(1)}, bf16[16,128,512]{2,1,0:T(8,128)(2,1)}, u32[]{:S(2)}) copy-start(bf16[16,128,512]{2,1,0:T(8,128)(2,1)} %param.7) | copy-start | bytes 6291460
  1.7 13.8 %collective-permute-start.4 = (bf16[64,1280]{1,0:T(8,128)(2,1)S(1)}, bf16[64,1280]{1,0:T(8,128)(2,1)S(1)}, u32[]{:S(2)}, u32[]{:S(2)}) collective-permute-start(bf16[64,1280]{1,0:T(8,128)(2,1)S(1)} %slice.106), channel_id=1, source_target_pairs={{0,16},{2,18},{4,20},{6,22},{8,24},{10,26},{12,28},{14,30},{16,0},... | collective-permute-start | bytes 491528 | tf_op jit(solution)/shard_map/ppermute | solution.py:112
  5.8 10.2 %collective-permute-start.5 = (bf16[64,1280]{1,0:T(8,128)(2,1)S(1)}, bf16[64,1280]{1,0:T(8,128)(2,1)S(1)}, u32[]{:S(2)}, u32[]{:S(2)}) collective-permute-start(bf16[64,1280]{1,0:T(8,128)(2,1)S(1)} %slice.106), channel_id=1, source_target_pairs={{0,24},{2,26},{4,28},{6,30},{8,0},{10,2},{12,4},{14,6},{16,8},{18,... | collective-permute-start | bytes 491528 | tf_op jit(solution)/shard_map/ppermute | solution.py:112
  7.2 11.1 %collective-permute-start.6 = (bf16[64,1280]{1,0:T(8,128)(2,1)S(1)}, bf16[64,1280]{1,0:T(8,128)(2,1)S(1)}, u32[]{:S(2)}, u32[]{:S(2)}) collective-permute-start(bf16[64,1280]{1,0:T(8,128)(2,1)S(1)} %slice.106), channel_id=1, source_target_pairs={{0,8},{2,10},{4,12},{6,14},{8,16},{10,18},{12,20},{14,22},{16,24},... | collective-permute-start | bytes 491528 | tf_op jit(solution)/shard_map/ppermute | solution.py:112
  9.6 33.9 %copy-start.4 = (bf16[64,2688]{1,0:T(8,128)(2,1)}, bf16[64,2688]{1,0:T(8,128)(2,1)S(1)}, u32[]{:S(2)}) copy-start(bf16[64,2688]{1,0:T(8,128)(2,1)S(1)} %fusion.1.refs_4_) | copy-start | bytes 1032196
  9.7 9.8 %collective-permute-start.1 = (bf16[64,2688]{1,0:T(8,128)(2,1)S(1)}, bf16[64,2688]{1,0:T(8,128)(2,1)S(1)}, u32[]{:S(2)}, u32[]{:S(2)}) collective-permute-start(bf16[64,2688]{1,0:T(8,128)(2,1)S(1)} %fusion.1.refs_4_), channel_id=1, source_target_pairs={{0,4},{2,6},{4,0},{6,2},{8,12},{10,14},{12,8},{14,10},{16,20},{18,... | collective-permute-start | bytes 1032200 | tf_op jit(solution)/shard_map/ppermute | solution.py:99
  14.0 42.2 %copy-start.2 = (bf16[16,128,512]{2,1,0:T(8,128)(2,1)S(1)}, bf16[16,128,512]{2,1,0:T(8,128)(2,1)}, u32[]{:S(2)}) copy-start(bf16[16,128,512]{2,1,0:T(8,128)(2,1)} %param.6) | copy-start | bytes 6291460
  14.0 47.4 %collective-permute-start.17 = (bf16[2048,512]{1,0:T(8,128)(2,1)}, bf16[2048,512]{1,0:T(8,128)(2,1)}, u32[]{:S(2)}, u32[]{:S(2)}) collective-permute-start(bf16[2048,512]{1,0:T(8,128)(2,1)} %pad_maximum_fusion), channel_id=1, source_target_pairs={{0,1},{1,0},{2,3},{3,2},{4,5},{5,4},{6,7},{7,6},{8,9},{9,8},{10,11... | collective-permute-start | bytes 6291464 | tf_op jit(solution)/shard_map/ppermute | solution.py:427
  19.4 36.8 %copy-start.7 = (bf16[64,2688]{1,0:T(8,128)(2,1)}, bf16[64,2688]{1,0:T(8,128)(2,1)S(1)}, u32[]{:S(2)}) copy-start(bf16[64,2688]{1,0:T(8,128)(2,1)S(1)} %collective-permute-done.1.refs_5_) | copy-start | bytes 1032196
  21.6 12.4 %collective-permute-start.7 = (bf16[192,1280]{1,0:T(8,128)(2,1)}, bf16[192,1280]{1,0:T(8,128)(2,1)}, u32[]{:S(2)}, u32[]{:S(2)}) collective-permute-start(bf16[192,1280]{1,0:T(8,128)(2,1)} %maximum_select_fusion.1.refs_8_), channel_id=1, source_target_pairs={{0,4},{2,6},{4,0},{6,2},{8,12},{10,14},{12,8},{14,10},{16,20},{18,... | collective-permute-start | bytes 1474568 | tf_op jit(solution)/shard_map/ppermute | solution.py:99
  23.1 18.1 %collective-permute-start.10 = (bf16[64,1408]{1,0:T(8,128)(2,1)S(1)}, bf16[64,1408]{1,0:T(8,128)(2,1)S(1)}, u32[]{:S(2)}, u32[]{:S(2)}) collective-permute-start(bf16[64,1408]{1,0:T(8,128)(2,1)S(1)} %slice_select_fusion), channel_id=1, source_target_pairs={{0,16},{2,18},{4,20},{6,22},{8,24},{10,26},{12,28},{14,30},{16,0},... | collective-permute-start | bytes 540680 | tf_op jit(solution)/shard_map/ppermute | solution.py:112
  28.2 13.1 %collective-permute-start.11 = (bf16[64,1408]{1,0:T(8,128)(2,1)S(1)}, bf16[64,1408]{1,0:T(8,128)(2,1)S(1)}, u32[]{:S(2)}, u32[]{:S(2)}) collective-permute-start(bf16[64,1408]{1,0:T(8,128)(2,1)S(1)} %slice_select_fusion), channel_id=1, source_target_pairs={{0,24},{2,26},{4,28},{6,30},{8,0},{10,2},{12,4},{14,6},{16,8},{18,... | collective-permute-start | bytes 540680 | tf_op jit(solution)/shard_map/ppermute | solution.py:112
  30.2 11.0 %collective-permute-start.12 = (bf16[64,1408]{1,0:T(8,128)(2,1)S(1)}, bf16[64,1408]{1,0:T(8,128)(2,1)S(1)}, u32[]{:S(2)}, u32[]{:S(2)}) collective-permute-start(bf16[64,1408]{1,0:T(8,128)(2,1)S(1)} %slice_select_fusion), channel_id=1, source_target_pairs={{0,8},{2,10},{4,12},{6,14},{8,16},{10,18},{12,20},{14,22},{16,24},... | collective-permute-start | bytes 540680 | tf_op jit(solution)/shard_map/ppermute | solution.py:112
  42.8 12.1 %collective-permute-start.13 = (bf16[192,1408]{1,0:T(8,128)(2,1)}, bf16[192,1408]{1,0:T(8,128)(2,1)}, u32[]{:S(2)}, u32[]{:S(2)}) collective-permute-start(bf16[192,1408]{1,0:T(8,128)(2,1)} %maximum_select_fusion.refs_12_), channel_id=1, source_target_pairs={{0,4},{2,6},{4,0},{6,2},{8,12},{10,14},{12,8},{14,10},{16,20},{18,... | collective-permute-start | bytes 1622024 | tf_op jit(solution)/shard_map/ppermute | solution.py:99
  43.6 11.3 %collective-permute-start.2 = (bf16[64,2688]{1,0:T(8,128)(2,1)S(1)}, bf16[64,2688]{1,0:T(8,128)(2,1)S(1)}, u32[]{:S(2)}, u32[]{:S(2)}) collective-permute-start(bf16[64,2688]{1,0:T(8,128)(2,1)S(1)} %fusion.1.refs_4_), channel_id=1, source_target_pairs={{0,2},{2,0},{4,6},{6,4},{8,10},{10,8},{12,14},{14,12},{16,18},{18,... | collective-permute-start | bytes 1032200 | tf_op jit(solution)/shard_map/ppermute | solution.py:99
  43.6 11.8 %collective-permute-start.3 = (bf16[64,2688]{1,0:T(8,128)(2,1)S(1)}, bf16[64,2688]{1,0:T(8,128)(2,1)S(1)}, u32[]{:S(2)}, u32[]{:S(2)}) collective-permute-start(bf16[64,2688]{1,0:T(8,128)(2,1)S(1)} %collective-permute-done.1.refs_5_), channel_id=1, source_target_pairs={{0,2},{2,0},{4,6},{6,4},{8,10},{10,8},{12,14},{14,12},{16,18},{18,... | collective-permute-start | bytes 1032200 | tf_op jit(solution)/shard_map/ppermute | solution.py:99
  44.1 17.3 %collective-permute-start.14 = (bf16[192,1408]{1,0:T(8,128)(2,1)}, bf16[192,1408]{1,0:T(8,128)(2,1)}, u32[]{:S(2)}, u32[]{:S(2)}) collective-permute-start(bf16[192,1408]{1,0:T(8,128)(2,1)} %maximum_select_fusion.refs_12_), channel_id=1, source_target_pairs={{0,2},{2,0},{4,6},{6,4},{8,10},{10,8},{12,14},{14,12},{16,18},{18,... | collective-permute-start | bytes 1622024 | tf_op jit(solution)/shard_map/ppermute | solution.py:99
  54.9 6.6 %collective-permute-start.15 = (bf16[192,1408]{1,0:T(8,128)(2,1)}, bf16[192,1408]{1,0:T(8,128)(2,1)}, u32[]{:S(2)}, u32[]{:S(2)}) collective-permute-start(bf16[192,1408]{1,0:T(8,128)(2,1)} %collective-permute-done.13.refs_13_), channel_id=1, source_target_pairs={{0,2},{2,0},{4,6},{6,4},{8,10},{10,8},{12,14},{14,12},{16,18},{18,... | collective-permute-start | bytes 1622024 | tf_op jit(solution)/shard_map/ppermute | solution.py:99
  54.9 1.4 copy-start.8
  54.9 4.4 %collective-permute-start.8 = (bf16[192,1280]{1,0:T(8,128)(2,1)}, bf16[192,1280]{1,0:T(8,128)(2,1)}, u32[]{:S(2)}, u32[]{:S(2)}) collective-permute-start(bf16[192,1280]{1,0:T(8,128)(2,1)} %maximum_select_fusion.1.refs_8_), channel_id=1, source_target_pairs={{0,2},{2,0},{4,6},{6,4},{8,10},{10,8},{12,14},{14,12},{16,18},{18,... | collective-permute-start | bytes 1474568 | tf_op jit(solution)/shard_map/ppermute | solution.py:99
  55.4 0.8 copy-start.9
  56.1 4.8 %collective-permute-start.9 = (bf16[192,1280]{1,0:T(8,128)(2,1)}, bf16[192,1280]{1,0:T(8,128)(2,1)}, u32[]{:S(2)}, u32[]{:S(2)}) collective-permute-start(bf16[192,1280]{1,0:T(8,128)(2,1)} %collective-permute-done.7.refs_9_), channel_id=1, source_target_pairs={{0,2},{2,0},{4,6},{6,4},{8,10},{10,8},{12,14},{14,12},{16,18},{18,... | collective-permute-start | bytes 1474568 | tf_op jit(solution)/shard_map/ppermute | solution.py:99
  59.3 35.5 %collective-permute-start.16 = (bf16[1024,512]{1,0:T(8,128)(2,1)S(1)}, bf16[1024,512]{1,0:T(8,128)(2,1)S(1)}, u32[]{:S(2)}, u32[]{:S(2)}) collective-permute-start(bf16[1024,512]{1,0:T(8,128)(2,1)S(1)} %pad_maximum_fusion.1), channel_id=1, source_target_pairs={{0,1},{1,0},{2,3},{3,2},{4,5},{5,4},{6,7},{7,6},{8,9},{9,8},{10,11... | collective-permute-start | bytes 3145736 | tf_op jit(solution)/shard_map/ppermute | solution.py:427
  60.9 55.2 %collective-permute-start = (bf16[1024,512]{1,0:T(8,128)(2,1)S(1)}, bf16[1024,512]{1,0:T(8,128)(2,1)S(1)}, u32[]{:S(2)}, u32[]{:S(2)}) collective-permute-start(bf16[1024,512]{1,0:T(8,128)(2,1)S(1)} %pad_maximum_fusion.2), channel_id=1, source_target_pairs={{0,1},{1,0},{2,3},{3,2},{4,5},{5,4},{6,7},{7,6},{8,9},{9,8},{10,11... | collective-permute-start | bytes 3145736 | tf_op jit(solution)/shard_map/ppermute | solution.py:427
  94.8 1.0 copy-start.6
  116.1 1.0 copy-start.5
  138.2 16.9 %copy-start = (bf16[512,2560]{1,0:T(8,128)(2,1)S(1)}, bf16[512,2560]{1,0:T(8,128)(2,1)}, u32[]{:S(2)}) copy-start(bf16[512,2560]{1,0:T(8,128)(2,1)} %get-tuple-element.32.refs_0_) | copy-start | bytes 7864324
  138.2 5.2 %collective-permute-start.19 = (bf16[512,2560]{1,0:T(8,128)(2,1)}, bf16[512,2560]{1,0:T(8,128)(2,1)S(1)}, u32[]{:S(2)}, u32[]{:S(2)}) collective-permute-start(bf16[512,2560]{1,0:T(8,128)(2,1)} %get-tuple-element.33), channel_id=1, source_target_pairs={{0,2},{2,0},{4,6},{6,4},{8,10},{10,8},{12,14},{14,12},{16,18},{18,... | collective-permute-start | bytes 7864328 | tf_op jit(solution)/shard_map/ppermute | solution.py:361
  138.3 48.3 %collective-permute-start.18 = (bf16[2048,512]{1,0:T(8,128)(2,1)}, bf16[2048,512]{1,0:T(8,128)(2,1)S(1)}, u32[]{:S(2)}, u32[]{:S(2)}) collective-permute-start(bf16[2048,512]{1,0:T(8,128)(2,1)} %get-tuple-element.31), channel_id=1, source_target_pairs={{0,1},{1,0},{2,3},{3,2},{4,5},{5,4},{6,7},{7,6},{8,9},{9,8},{10,11... | collective-permute-start | bytes 6291464 | tf_op jit(solution)/shard_map/ppermute | solution.py:435
  144.5 10.6 %collective-permute-start.21 = (bf16[64,2560]{1,0:T(8,128)(2,1)S(1)}, bf16[64,2560]{1,0:T(8,128)(2,1)S(1)}, u32[]{:S(2)}, u32[]{:S(2)}) collective-permute-start(bf16[64,2560]{1,0:T(8,128)(2,1)S(1)} %add_convert_fusion.3), channel_id=1, source_target_pairs={{0,4},{2,6},{4,0},{6,2},{8,12},{10,14},{12,8},{14,10},{16,20},{18,... | collective-permute-start | bytes 983048 | tf_op jit(solution)/shard_map/ppermute | solution.py:361
  147.1 22.0 %collective-permute-start.23 = (bf16[128,2560]{1,0:T(8,128)(2,1)S(1)}, bf16[128,2560]{1,0:T(8,128)(2,1)S(1)}, u32[]{:S(2)}, u32[]{:S(2)}) collective-permute-start(bf16[128,2560]{1,0:T(8,128)(2,1)S(1)} %add_convert_fusion.1), channel_id=1, source_target_pairs={{0,4},{2,6},{4,0},{6,2},{8,12},{10,14},{12,8},{14,10},{16,20},{18,... | collective-permute-start | bytes 1966088 | tf_op jit(solution)/shard_map/ppermute | solution.py:361
  155.3 34.4 %copy-start.1 = (bf16[2048,512]{1,0:T(8,128)(2,1)S(1)}, bf16[2048,512]{1,0:T(8,128)(2,1)}, u32[]{:S(2)}) copy-start(bf16[2048,512]{1,0:T(8,128)(2,1)} %get-tuple-element.30.kept_ref) | copy-start | bytes 6291460
  155.3 31.3 %collective-permute-start.20 = (bf16[64,2560]{1,0:T(8,128)(2,1)S(1)}, bf16[64,2560]{1,0:T(8,128)(2,1)S(1)}, u32[]{:S(2)}, u32[]{:S(2)}) collective-permute-start(bf16[64,2560]{1,0:T(8,128)(2,1)S(1)} %get-tuple-element.38), channel_id=1, source_target_pairs={{0,4},{2,6},{4,0},{6,2},{8,12},{10,14},{12,8},{14,10},{16,20},{18,... | collective-permute-start | bytes 983048 | tf_op jit(solution)/shard_map/ppermute | solution.py:361
  156.7 29.8 %collective-permute-start.22 = (bf16[64,2560]{1,0:T(8,128)(2,1)S(1)}, bf16[64,2560]{1,0:T(8,128)(2,1)S(1)}, u32[]{:S(2)}, u32[]{:S(2)}) collective-permute-start(bf16[64,2560]{1,0:T(8,128)(2,1)S(1)} %get-tuple-element.37), channel_id=1, source_target_pairs={{0,16},{2,18},{4,20},{6,22},{8,24},{10,26},{12,28},{14,30},{16,0},... | collective-permute-start | bytes 983048 | tf_op jit(solution)/shard_map/ppermute | solution.py:377
  169.4 17.2 %collective-permute-start.24 = (bf16[64,2560]{1,0:T(8,128)(2,1)S(1)}, bf16[64,2560]{1,0:T(8,128)(2,1)S(1)}, u32[]{:S(2)}, u32[]{:S(2)}) collective-permute-start(bf16[64,2560]{1,0:T(8,128)(2,1)S(1)} %get-tuple-element.44), channel_id=1, source_target_pairs={{0,24},{2,26},{4,28},{6,30},{8,0},{10,2},{12,4},{14,6},{16,8},{18,... | collective-permute-start | bytes 983048 | tf_op jit(solution)/shard_map/ppermute | solution.py:377
  172.0 17.7 %collective-permute-start.25 = (bf16[64,2560]{1,0:T(8,128)(2,1)S(1)}, bf16[64,2560]{1,0:T(8,128)(2,1)S(1)}, u32[]{:S(2)}, u32[]{:S(2)}) collective-permute-start(bf16[64,2560]{1,0:T(8,128)(2,1)S(1)} %get-tuple-element.43), channel_id=1, source_target_pairs={{0,8},{2,10},{4,12},{6,14},{8,16},{10,18},{12,20},{14,22},{16,24},... | collective-permute-start | bytes 983048 | tf_op jit(solution)/shard_map/ppermute | solution.py:377

commit v7 on v3

--- a/solution.py
+++ b/solution.py
@@ -269,7 +269,7 @@
         ship(lo, wide)
 
     block = 4 * HEAD_DIM
-    stride = max(1, 8 // histories)
+    stride = max(1, 16 // histories)
     for lo in range(0, heads, stride):
         hi = min(lo + stride, heads)
         units = [(h, n) for h in range(lo, hi) for n in range(histories)]

time: 186 us -> 186 us (level)
  no operation moved by 1% of the time
where the time goes in v7:
time: 186 us; the launch traced here: 183 us
  Pallas kernels  67.9 us (37%)
  waiting for transfers between devices  54.2 us (29%)
  starting transfers between devices  37.4 us (20%)
  local copies, waits for them, and re-layouts  10.8 us (6%)
  other arithmetic  9.68 us (5%)
  between operations  3.21 us (2%)
    pallas_call x3, Pallas kernels, group_call(): pl.pallas_call(functools.partial(group_kernel, start, steps, first, last,...  65.5 us
    ppermute x13, waiting for transfers between devices, swap(): return lax.ppermute(block, 'user', [(i, i ^ bit) for i in range(users)])  33 us
    ppermute x6, starting transfers between devices, gather_parts(): moved.append(lax.ppermute(part, 'user', pairs))  13.2 us
    ppermute x1, waiting for transfers between devices, give_back(): return lax.ppermute(block, 'tensor', [(0, 1), (1, 0)])  11.6 us
    ppermute x3, starting transfers between devices, scatter_parts(): moved.append(lax.ppermute(block, 'user', pairs))  10.3 us
    ppermute x13, starting transfers between devices, swap(): return lax.ppermute(block, 'user', [(i, i ^ bit) for i in range(users)])  8.65 us
    ppermute x6, waiting for transfers between devices, gather_parts(): moved.append(lax.ppermute(part, 'user', pairs))  6.54 us
  transfers between devices with their start and end apart: 26, of which 9 were waited for; matrix products, arithmetic and copies ran while one was open for 9% of the time, Pallas kernels for 26%

profile of v7, /device:TPU:0, one launch (start us, length us, event | category | flops | bytes accessed | tf_op | source)
XLA Modules:
  0.0 183.2 jit_solution(7194557014100989117)
XLA Ops:
  0.6 1.1 slice.106
  1.7 4.1 %collective-permute-start.4 = (bf16[64,1280]{1,0:T(8,128)(2,1)S(1)}, bf16[64,1280]{1,0:T(8,128)(2,1)S(1)}, u32[]{:S(2)}, u32[]{:S(2)}) collective-permute-start(bf16[64,1280]{1,0:T(8,128)(2,1)S(1)} %slice.106), channel_id=1, source_target_pairs={{0,16},{2,18},{4,20},{6,22},{8,24},{10,26},{12,28},{14,30},{16,0},... | collective-permute-start | bytes 491528 | tf_op jit(solution)/shard_map/ppermute | solution.py:112
  5.8 1.3 collective-permute-start.5
  7.2 0.7 collective-permute-start.6
  7.9 0.7 convert_bitcast_fusion
  8.6 1.0 fusion.1.refs_4_
  9.7 1.6 collective-permute-start.1
  11.2 1.3 fusion.5
  12.6 1.5 pad_maximum_fusion
  14.0 1.5 collective-permute-start.17
  15.6 0.5 slice.126
  18.3 0.5 slice.128
  19.5 0.6 slice.124
  20.1 1.5 maximum_select_fusion.1.refs_8_
  21.6 1.5 collective-permute-start.7
  23.1 5.0 %collective-permute-start.10 = (bf16[64,1408]{1,0:T(8,128)(2,1)S(1)}, bf16[64,1408]{1,0:T(8,128)(2,1)S(1)}, u32[]{:S(2)}, u32[]{:S(2)}) collective-permute-start(bf16[64,1408]{1,0:T(8,128)(2,1)S(1)} %slice_select_fusion), channel_id=1, source_target_pairs={{0,16},{2,18},{4,20},{6,22},{8,24},{10,26},{12,28},{14,30},{16,0},... | collective-permute-start | bytes 540680 | tf_op jit(solution)/shard_map/ppermute | solution.py:112
  28.2 2.0 %collective-permute-start.11 = (bf16[64,1408]{1,0:T(8,128)(2,1)S(1)}, bf16[64,1408]{1,0:T(8,128)(2,1)S(1)}, u32[]{:S(2)}, u32[]{:S(2)}) collective-permute-start(bf16[64,1408]{1,0:T(8,128)(2,1)S(1)} %slice_select_fusion), channel_id=1, source_target_pairs={{0,24},{2,26},{4,28},{6,30},{8,0},{10,2},{12,4},{14,6},{16,8},{18,... | collective-permute-start | bytes 540680 | tf_op jit(solution)/shard_map/ppermute | solution.py:112
  30.2 3.8 %collective-permute-done.7.refs_9_ = bf16[192,1280]{1,0:T(8,128)(2,1)} collective-permute-done((bf16[192,1280]{1,0:T(8,128)(2,1)}, bf16[192,1280]{1,0:T(8,128)(2,1)}, u32[]{:S(2)}, u32[]{:S(2)}) %collective-permute-start.7) | collective-permute-done | bytes 491552 | tf_op jit(solution)/shard_map/ppermute | solution.py:99
  34.0 1.2 slice.125
  35.2 6.1 %collective-permute-done.10 = bf16[64,1408]{1,0:T(8,128)(2,1)S(1)} collective-permute-done((bf16[64,1408]{1,0:T(8,128)(2,1)S(1)}, bf16[64,1408]{1,0:T(8,128)(2,1)S(1)}, u32[]{:S(2)}, u32[]{:S(2)}) %collective-permute-start.10) | collective-permute-done | bytes 180256 | tf_op jit(solution)/shard_map/ppermute | solution.py:112
  41.3 1.5 maximum_select_fusion.refs_12_
  42.8 0.8 collective-permute-start.13
  44.1 10.8 %collective-permute-done.13.refs_13_ = bf16[192,1408]{1,0:T(8,128)(2,1)} collective-permute-done((bf16[192,1408]{1,0:T(8,128)(2,1)}, bf16[192,1408]{1,0:T(8,128)(2,1)}, u32[]{:S(2)}, u32[]{:S(2)}) %collective-permute-start.13) | collective-permute-done | bytes 540704 | tf_op jit(solution)/shard_map/ppermute | solution.py:99
  55.4 0.8 copy-done.9
  56.3 1.1 slice.102
  57.5 1.1 slice.104
  58.6 0.6 pad_add_fusion.refs_0_
  59.3 1.6 collective-permute-start.16
  61.4 30.4 %shard_map.85 = (bf16[2048,512]{1,0:T(8,128)(2,1)}, bf16[2048,512]{1,0:T(8,128)(2,1)}, f32[1024,2560]{1,0:T(8,128)}) custom-call(s32[2]{0:T(128)} %pad_add_fusion.refs_0_, bf16[2048,512]{1,0:T(8,128)(2,1)} %bitcast.16, bf16[2048,512]{1,0:T(8,128)(2,1)} %bitcast.23, bf16[2048,512]{1,0:T(8,128)(2,1)} %collective-permute-done.17.refs_3_, ...), custom_call_target="tpu_custom_call" | custom-call | flops 15032385536 | bytes 16777216 | tf_op jit(solution)/shard_map/pallas_call | solution.py:315
  91.8 1.0 copy-done.6
  92.8 17.0 %shard_map.86 = (bf16[2048,512]{1,0:T(8,128)(2,1)}, bf16[2048,512]{1,0:T(8,128)(2,1)}, f32[1024,2560]{1,0:T(8,128)}) custom-call(s32[2]{0:T(128)} %pad_add_fusion.refs_0_, bf16[2048,512]{1,0:T(8,128)(2,1)} %bitcast.17, bf16[2048,512]{1,0:T(8,128)(2,1)} %bitcast.24, bf16[1024,512]{1,0:T(8,128)(2,1)} %copy-done.6, ...), custom_call_target="tpu_custom_call", output_to_operand_aliasing={{0}: (17, {}), {1}: (18, {})} | custom-call | flops 7516192768 | bytes 16777216 | tf_op jit(solution)/shard_map/pallas_call | solution.py:315
  109.8 1.0 copy-done.5
  110.8 18.1 %shard_map.87 = (bf16[2048,512]{1,0:T(8,128)(2,1)}, bf16[2048,512]{1,0:T(8,128)(2,1)}, bf16[512,2560]{1,0:T(8,128)(2,1)}, bf16[512,2560]{1,0:T(8,128)(2,1)}) custom-call(s32[2]{0:T(128)} %pad_add_fusion.refs_0_, bf16[2048,512]{1,0:T(8,128)(2,1)} %bitcast.18, bf16[2048,512]{1,0:T(8,128)(2,1)} %bitcast.25, ...), custom_call_target="tpu_custom_call", output_to_operand_aliasing={{0}: (17, {}), {1}: (18, {})} | custom-call | flops 7516192768 | bytes 16777216 | tf_op jit(solution)/shard_map/pallas_call | solution.py:315
  129.0 1.6 collective-permute-start.18
  130.6 3.5 %collective-permute-done.19.refs_1_ = bf16[512,2560]{1,0:T(8,128)(2,1)S(1)} collective-permute-done((bf16[512,2560]{1,0:T(8,128)(2,1)}, bf16[512,2560]{1,0:T(8,128)(2,1)S(1)}, u32[]{:S(2)}, u32[]{:S(2)}) %collective-permute-start.19) | collective-permute-done | bytes 2621472 | tf_op jit(solution)/shard_map/ppermute | solution.py:359
  134.1 1.0 add_convert_fusion.3
  135.1 1.4 collective-permute-start.21
  136.6 1.2 add_convert_fusion.1
  137.8 0.7 collective-permute-start.23
  138.5 7.2 %collective-permute-done.21 = bf16[64,2560]{1,0:T(8,128)(2,1)S(1)} collective-permute-done((bf16[64,2560]{1,0:T(8,128)(2,1)S(1)}, bf16[64,2560]{1,0:T(8,128)(2,1)S(1)}, u32[]{:S(2)}, u32[]{:S(2)}) %collective-permute-start.21) | collective-permute-done | bytes 327712 | tf_op jit(solution)/shard_map/ppermute | solution.py:359
  146.0 1.4 collective-permute-start.20
  147.4 4.8 %collective-permute-start.22 = (bf16[64,2560]{1,0:T(8,128)(2,1)S(1)}, bf16[64,2560]{1,0:T(8,128)(2,1)S(1)}, u32[]{:S(2)}, u32[]{:S(2)}) collective-permute-start(bf16[64,2560]{1,0:T(8,128)(2,1)S(1)} %get-tuple-element.37), channel_id=1, source_target_pairs={{0,16},{2,18},{4,20},{6,22},{8,24},{10,26},{12,28},{14,30},{16,0},... | collective-permute-start | bytes 983048 | tf_op jit(solution)/shard_map/ppermute | solution.py:375
  152.2 7.6 %collective-permute-done.23 = bf16[128,2560]{1,0:T(8,128)(2,1)S(1)} collective-permute-done((bf16[128,2560]{1,0:T(8,128)(2,1)S(1)}, bf16[128,2560]{1,0:T(8,128)(2,1)S(1)}, u32[]{:S(2)}, u32[]{:S(2)}) %collective-permute-start.23) | collective-permute-done | bytes 655392 | tf_op jit(solution)/shard_map/ppermute | solution.py:359
  160.1 2.6 %collective-permute-start.24 = (bf16[64,2560]{1,0:T(8,128)(2,1)S(1)}, bf16[64,2560]{1,0:T(8,128)(2,1)S(1)}, u32[]{:S(2)}, u32[]{:S(2)}) collective-permute-start(bf16[64,2560]{1,0:T(8,128)(2,1)S(1)} %get-tuple-element.44), channel_id=1, source_target_pairs={{0,24},{2,26},{4,28},{6,30},{8,0},{10,2},{12,4},{14,6},{16,8},{18,... | collective-permute-start | bytes 983048 | tf_op jit(solution)/shard_map/ppermute | solution.py:375
  162.6 3.0 %collective-permute-start.25 = (bf16[64,2560]{1,0:T(8,128)(2,1)S(1)}, bf16[64,2560]{1,0:T(8,128)(2,1)S(1)}, u32[]{:S(2)}, u32[]{:S(2)}) collective-permute-start(bf16[64,2560]{1,0:T(8,128)(2,1)S(1)} %get-tuple-element.43), channel_id=1, source_target_pairs={{0,8},{2,10},{4,12},{6,14},{8,16},{10,18},{12,20},{14,22},{16,24},... | collective-permute-start | bytes 983048 | tf_op jit(solution)/shard_map/ppermute | solution.py:375
  165.6 11.6 %collective-permute-done.18.sent_ref = bf16[2048,512]{1,0:T(8,128)(2,1)S(1)} collective-permute-done((bf16[2048,512]{1,0:T(8,128)(2,1)}, bf16[2048,512]{1,0:T(8,128)(2,1)S(1)}, u32[]{:S(2)}, u32[]{:S(2)}) %collective-permute-start.18) | collective-permute-done | bytes 2097184 | tf_op jit(solution)/shard_map/ppermute | solution.py:433
  177.2 3.1 %collective-permute-done.25.refs_5_ = bf16[64,2560]{1,0:T(8,128)(2,1)S(1)} collective-permute-done((bf16[64,2560]{1,0:T(8,128)(2,1)S(1)}, bf16[64,2560]{1,0:T(8,128)(2,1)S(1)}, u32[]{:S(2)}, u32[]{:S(2)}) %collective-permute-start.25) | collective-permute-done | bytes 327712 | tf_op jit(solution)/shard_map/ppermute | solution.py:375
  180.3 2.4 %shard_map.88 = (bf16[2048,512]{1,0:T(8,128)(2,1)}, f32[64,2048]{1,0:T(8,128)}, f32[64,512]{1,0:T(8,128)}) custom-call(bf16[2048,512]{1,0:T(8,128)(2,1)S(1)} %copy-done.1, bf16[2048,512]{1,0:T(8,128)(2,1)S(1)} %collective-permute-done.18.sent_ref, bf16[512,2560]{1,0:T(8,128)(2,1)S(1)} %copy-done, bf16[512,2560]{1,0:T(8,128)(2,1)S(1)} %collective-permute-done.19.refs_1_, ...), custom_call_target="tpu_custom_call" | custom-call | flops 1048576 | bytes 12582912 | tf_op jit(solution)/shard_map/pallas_call | solution.py:402
  (56 shorter events, 3.6 us)
Async XLA Ops:
  0.6 11.9 %copy-start.3 = (bf16[16,128,512]{2,1,0:T(8,128)(2,1)S(1)}, bf16[16,128,512]{2,1,0:T(8,128)(2,1)}, u32[]{:S(2)}) copy-start(bf16[16,128,512]{2,1,0:T(8,128)(2,1)} %param.7) | copy-start | bytes 6291460
  1.7 13.8 %collective-permute-start.4 = (bf16[64,1280]{1,0:T(8,128)(2,1)S(1)}, bf16[64,1280]{1,0:T(8,128)(2,1)S(1)}, u32[]{:S(2)}, u32[]{:S(2)}) collective-permute-start(bf16[64,1280]{1,0:T(8,128)(2,1)S(1)} %slice.106), channel_id=1, source_target_pairs={{0,16},{2,18},{4,20},{6,22},{8,24},{10,26},{12,28},{14,30},{16,0},... | collective-permute-start | bytes 491528 | tf_op jit(solution)/shard_map/ppermute | solution.py:112
  5.8 10.2 %collective-permute-start.5 = (bf16[64,1280]{1,0:T(8,128)(2,1)S(1)}, bf16[64,1280]{1,0:T(8,128)(2,1)S(1)}, u32[]{:S(2)}, u32[]{:S(2)}) collective-permute-start(bf16[64,1280]{1,0:T(8,128)(2,1)S(1)} %slice.106), channel_id=1, source_target_pairs={{0,24},{2,26},{4,28},{6,30},{8,0},{10,2},{12,4},{14,6},{16,8},{18,... | collective-permute-start | bytes 491528 | tf_op jit(solution)/shard_map/ppermute | solution.py:112
  7.2 11.1 %collective-permute-start.6 = (bf16[64,1280]{1,0:T(8,128)(2,1)S(1)}, bf16[64,1280]{1,0:T(8,128)(2,1)S(1)}, u32[]{:S(2)}, u32[]{:S(2)}) collective-permute-start(bf16[64,1280]{1,0:T(8,128)(2,1)S(1)} %slice.106), channel_id=1, source_target_pairs={{0,8},{2,10},{4,12},{6,14},{8,16},{10,18},{12,20},{14,22},{16,24},... | collective-permute-start | bytes 491528 | tf_op jit(solution)/shard_map/ppermute | solution.py:112
  9.6 33.9 %copy-start.4 = (bf16[64,2688]{1,0:T(8,128)(2,1)}, bf16[64,2688]{1,0:T(8,128)(2,1)S(1)}, u32[]{:S(2)}) copy-start(bf16[64,2688]{1,0:T(8,128)(2,1)S(1)} %fusion.1.refs_4_) | copy-start | bytes 1032196
  9.7 9.8 %collective-permute-start.1 = (bf16[64,2688]{1,0:T(8,128)(2,1)S(1)}, bf16[64,2688]{1,0:T(8,128)(2,1)S(1)}, u32[]{:S(2)}, u32[]{:S(2)}) collective-permute-start(bf16[64,2688]{1,0:T(8,128)(2,1)S(1)} %fusion.1.refs_4_), channel_id=1, source_target_pairs={{0,4},{2,6},{4,0},{6,2},{8,12},{10,14},{12,8},{14,10},{16,20},{18,... | collective-permute-start | bytes 1032200 | tf_op jit(solution)/shard_map/ppermute | solution.py:99
  14.0 42.2 %copy-start.2 = (bf16[16,128,512]{2,1,0:T(8,128)(2,1)S(1)}, bf16[16,128,512]{2,1,0:T(8,128)(2,1)}, u32[]{:S(2)}) copy-start(bf16[16,128,512]{2,1,0:T(8,128)(2,1)} %param.6) | copy-start | bytes 6291460
  14.0 47.4 %collective-permute-start.17 = (bf16[2048,512]{1,0:T(8,128)(2,1)}, bf16[2048,512]{1,0:T(8,128)(2,1)}, u32[]{:S(2)}, u32[]{:S(2)}) collective-permute-start(bf16[2048,512]{1,0:T(8,128)(2,1)} %pad_maximum_fusion), channel_id=1, source_target_pairs={{0,1},{1,0},{2,3},{3,2},{4,5},{5,4},{6,7},{7,6},{8,9},{9,8},{10,11... | collective-permute-start | bytes 6291464 | tf_op jit(solution)/shard_map/ppermute | solution.py:425
  19.4 36.8 %copy-start.7 = (bf16[64,2688]{1,0:T(8,128)(2,1)}, bf16[64,2688]{1,0:T(8,128)(2,1)S(1)}, u32[]{:S(2)}) copy-start(bf16[64,2688]{1,0:T(8,128)(2,1)S(1)} %collective-permute-done.1.refs_5_) | copy-start | bytes 1032196
  21.6 12.4 %collective-permute-start.7 = (bf16[192,1280]{1,0:T(8,128)(2,1)}, bf16[192,1280]{1,0:T(8,128)(2,1)}, u32[]{:S(2)}, u32[]{:S(2)}) collective-permute-start(bf16[192,1280]{1,0:T(8,128)(2,1)} %maximum_select_fusion.1.refs_8_), channel_id=1, source_target_pairs={{0,4},{2,6},{4,0},{6,2},{8,12},{10,14},{12,8},{14,10},{16,20},{18,... | collective-permute-start | bytes 1474568 | tf_op jit(solution)/shard_map/ppermute | solution.py:99
  23.1 18.1 %collective-permute-start.10 = (bf16[64,1408]{1,0:T(8,128)(2,1)S(1)}, bf16[64,1408]{1,0:T(8,128)(2,1)S(1)}, u32[]{:S(2)}, u32[]{:S(2)}) collective-permute-start(bf16[64,1408]{1,0:T(8,128)(2,1)S(1)} %slice_select_fusion), channel_id=1, source_target_pairs={{0,16},{2,18},{4,20},{6,22},{8,24},{10,26},{12,28},{14,30},{16,0},... | collective-permute-start | bytes 540680 | tf_op jit(solution)/shard_map/ppermute | solution.py:112
  28.2 13.1 %collective-permute-start.11 = (bf16[64,1408]{1,0:T(8,128)(2,1)S(1)}, bf16[64,1408]{1,0:T(8,128)(2,1)S(1)}, u32[]{:S(2)}, u32[]{:S(2)}) collective-permute-start(bf16[64,1408]{1,0:T(8,128)(2,1)S(1)} %slice_select_fusion), channel_id=1, source_target_pairs={{0,24},{2,26},{4,28},{6,30},{8,0},{10,2},{12,4},{14,6},{16,8},{18,... | collective-permute-start | bytes 540680 | tf_op jit(solution)/shard_map/ppermute | solution.py:112
  30.2 11.0 %collective-permute-start.12 = (bf16[64,1408]{1,0:T(8,128)(2,1)S(1)}, bf16[64,1408]{1,0:T(8,128)(2,1)S(1)}, u32[]{:S(2)}, u32[]{:S(2)}) collective-permute-start(bf16[64,1408]{1,0:T(8,128)(2,1)S(1)} %slice_select_fusion), channel_id=1, source_target_pairs={{0,8},{2,10},{4,12},{6,14},{8,16},{10,18},{12,20},{14,22},{16,24},... | collective-permute-start | bytes 540680 | tf_op jit(solution)/shard_map/ppermute | solution.py:112
  42.8 12.1 %collective-permute-start.13 = (bf16[192,1408]{1,0:T(8,128)(2,1)}, bf16[192,1408]{1,0:T(8,128)(2,1)}, u32[]{:S(2)}, u32[]{:S(2)}) collective-permute-start(bf16[192,1408]{1,0:T(8,128)(2,1)} %maximum_select_fusion.refs_12_), channel_id=1, source_target_pairs={{0,4},{2,6},{4,0},{6,2},{8,12},{10,14},{12,8},{14,10},{16,20},{18,... | collective-permute-start | bytes 1622024 | tf_op jit(solution)/shard_map/ppermute | solution.py:99
  43.6 11.3 %collective-permute-start.2 = (bf16[64,2688]{1,0:T(8,128)(2,1)S(1)}, bf16[64,2688]{1,0:T(8,128)(2,1)S(1)}, u32[]{:S(2)}, u32[]{:S(2)}) collective-permute-start(bf16[64,2688]{1,0:T(8,128)(2,1)S(1)} %fusion.1.refs_4_), channel_id=1, source_target_pairs={{0,2},{2,0},{4,6},{6,4},{8,10},{10,8},{12,14},{14,12},{16,18},{18,... | collective-permute-start | bytes 1032200 | tf_op jit(solution)/shard_map/ppermute | solution.py:99
  43.6 11.8 %collective-permute-start.3 = (bf16[64,2688]{1,0:T(8,128)(2,1)S(1)}, bf16[64,2688]{1,0:T(8,128)(2,1)S(1)}, u32[]{:S(2)}, u32[]{:S(2)}) collective-permute-start(bf16[64,2688]{1,0:T(8,128)(2,1)S(1)} %collective-permute-done.1.refs_5_), channel_id=1, source_target_pairs={{0,2},{2,0},{4,6},{6,4},{8,10},{10,8},{12,14},{14,12},{16,18},{18,... | collective-permute-start | bytes 1032200 | tf_op jit(solution)/shard_map/ppermute | solution.py:99
  44.1 17.3 %collective-permute-start.14 = (bf16[192,1408]{1,0:T(8,128)(2,1)}, bf16[192,1408]{1,0:T(8,128)(2,1)}, u32[]{:S(2)}, u32[]{:S(2)}) collective-permute-start(bf16[192,1408]{1,0:T(8,128)(2,1)} %maximum_select_fusion.refs_12_), channel_id=1, source_target_pairs={{0,2},{2,0},{4,6},{6,4},{8,10},{10,8},{12,14},{14,12},{16,18},{18,... | collective-permute-start | bytes 1622024 | tf_op jit(solution)/shard_map/ppermute | solution.py:99
  54.9 6.6 %collective-permute-start.15 = (bf16[192,1408]{1,0:T(8,128)(2,1)}, bf16[192,1408]{1,0:T(8,128)(2,1)}, u32[]{:S(2)}, u32[]{:S(2)}) collective-permute-start(bf16[192,1408]{1,0:T(8,128)(2,1)} %collective-permute-done.13.refs_13_), channel_id=1, source_target_pairs={{0,2},{2,0},{4,6},{6,4},{8,10},{10,8},{12,14},{14,12},{16,18},{18,... | collective-permute-start | bytes 1622024 | tf_op jit(solution)/shard_map/ppermute | solution.py:99
  54.9 1.4 copy-start.8
  54.9 4.4 %collective-permute-start.8 = (bf16[192,1280]{1,0:T(8,128)(2,1)}, bf16[192,1280]{1,0:T(8,128)(2,1)}, u32[]{:S(2)}, u32[]{:S(2)}) collective-permute-start(bf16[192,1280]{1,0:T(8,128)(2,1)} %maximum_select_fusion.1.refs_8_), channel_id=1, source_target_pairs={{0,2},{2,0},{4,6},{6,4},{8,10},{10,8},{12,14},{14,12},{16,18},{18,... | collective-permute-start | bytes 1474568 | tf_op jit(solution)/shard_map/ppermute | solution.py:99
  55.4 0.8 copy-start.9
  56.1 4.8 %collective-permute-start.9 = (bf16[192,1280]{1,0:T(8,128)(2,1)}, bf16[192,1280]{1,0:T(8,128)(2,1)}, u32[]{:S(2)}, u32[]{:S(2)}) collective-permute-start(bf16[192,1280]{1,0:T(8,128)(2,1)} %collective-permute-done.7.refs_9_), channel_id=1, source_target_pairs={{0,2},{2,0},{4,6},{6,4},{8,10},{10,8},{12,14},{14,12},{16,18},{18,... | collective-permute-start | bytes 1474568 | tf_op jit(solution)/shard_map/ppermute | solution.py:99
  59.3 32.5 %collective-permute-start.16 = (bf16[1024,512]{1,0:T(8,128)(2,1)S(1)}, bf16[1024,512]{1,0:T(8,128)(2,1)S(1)}, u32[]{:S(2)}, u32[]{:S(2)}) collective-permute-start(bf16[1024,512]{1,0:T(8,128)(2,1)S(1)} %pad_maximum_fusion.1), channel_id=1, source_target_pairs={{0,1},{1,0},{2,3},{3,2},{4,5},{5,4},{6,7},{7,6},{8,9},{9,8},{10,11... | collective-permute-start | bytes 3145736 | tf_op jit(solution)/shard_map/ppermute | solution.py:425
  60.9 48.9 %collective-permute-start = (bf16[1024,512]{1,0:T(8,128)(2,1)S(1)}, bf16[1024,512]{1,0:T(8,128)(2,1)S(1)}, u32[]{:S(2)}, u32[]{:S(2)}) collective-permute-start(bf16[1024,512]{1,0:T(8,128)(2,1)S(1)} %pad_maximum_fusion.2), channel_id=1, source_target_pairs={{0,1},{1,0},{2,3},{3,2},{4,5},{5,4},{6,7},{7,6},{8,9},{9,8},{10,11... | collective-permute-start | bytes 3145736 | tf_op jit(solution)/shard_map/ppermute | solution.py:425
  91.8 1.0 copy-start.6
  109.8 1.0 copy-start.5
  128.9 16.9 %copy-start = (bf16[512,2560]{1,0:T(8,128)(2,1)S(1)}, bf16[512,2560]{1,0:T(8,128)(2,1)}, u32[]{:S(2)}) copy-start(bf16[512,2560]{1,0:T(8,128)(2,1)} %get-tuple-element.32.refs_0_) | copy-start | bytes 7864324
  128.9 5.2 %collective-permute-start.19 = (bf16[512,2560]{1,0:T(8,128)(2,1)}, bf16[512,2560]{1,0:T(8,128)(2,1)S(1)}, u32[]{:S(2)}, u32[]{:S(2)}) collective-permute-start(bf16[512,2560]{1,0:T(8,128)(2,1)} %get-tuple-element.33), channel_id=1, source_target_pairs={{0,2},{2,0},{4,6},{6,4},{8,10},{10,8},{12,14},{14,12},{16,18},{18,... | collective-permute-start | bytes 7864328 | tf_op jit(solution)/shard_map/ppermute | solution.py:359
  129.0 48.3 %collective-permute-start.18 = (bf16[2048,512]{1,0:T(8,128)(2,1)}, bf16[2048,512]{1,0:T(8,128)(2,1)S(1)}, u32[]{:S(2)}, u32[]{:S(2)}) collective-permute-start(bf16[2048,512]{1,0:T(8,128)(2,1)} %get-tuple-element.31), channel_id=1, source_target_pairs={{0,1},{1,0},{2,3},{3,2},{4,5},{5,4},{6,7},{7,6},{8,9},{9,8},{10,11... | collective-permute-start | bytes 6291464 | tf_op jit(solution)/shard_map/ppermute | solution.py:433
  135.1 10.6 %collective-permute-start.21 = (bf16[64,2560]{1,0:T(8,128)(2,1)S(1)}, bf16[64,2560]{1,0:T(8,128)(2,1)S(1)}, u32[]{:S(2)}, u32[]{:S(2)}) collective-permute-start(bf16[64,2560]{1,0:T(8,128)(2,1)S(1)} %add_convert_fusion.3), channel_id=1, source_target_pairs={{0,4},{2,6},{4,0},{6,2},{8,12},{10,14},{12,8},{14,10},{16,20},{18,... | collective-permute-start | bytes 983048 | tf_op jit(solution)/shard_map/ppermute | solution.py:359
  137.8 22.0 %collective-permute-start.23 = (bf16[128,2560]{1,0:T(8,128)(2,1)S(1)}, bf16[128,2560]{1,0:T(8,128)(2,1)S(1)}, u32[]{:S(2)}, u32[]{:S(2)}) collective-permute-start(bf16[128,2560]{1,0:T(8,128)(2,1)S(1)} %add_convert_fusion.1), channel_id=1, source_target_pairs={{0,4},{2,6},{4,0},{6,2},{8,12},{10,14},{12,8},{14,10},{16,20},{18,... | collective-permute-start | bytes 1966088 | tf_op jit(solution)/shard_map/ppermute | solution.py:359
  145.9 34.4 %copy-start.1 = (bf16[2048,512]{1,0:T(8,128)(2,1)S(1)}, bf16[2048,512]{1,0:T(8,128)(2,1)}, u32[]{:S(2)}) copy-start(bf16[2048,512]{1,0:T(8,128)(2,1)} %get-tuple-element.30.kept_ref) | copy-start | bytes 6291460
  146.0 31.3 %collective-permute-start.20 = (bf16[64,2560]{1,0:T(8,128)(2,1)S(1)}, bf16[64,2560]{1,0:T(8,128)(2,1)S(1)}, u32[]{:S(2)}, u32[]{:S(2)}) collective-permute-start(bf16[64,2560]{1,0:T(8,128)(2,1)S(1)} %get-tuple-element.38), channel_id=1, source_target_pairs={{0,4},{2,6},{4,0},{6,2},{8,12},{10,14},{12,8},{14,10},{16,20},{18,... | collective-permute-start | bytes 983048 | tf_op jit(solution)/shard_map/ppermute | solution.py:359
  147.4 29.8 %collective-permute-start.22 = (bf16[64,2560]{1,0:T(8,128)(2,1)S(1)}, bf16[64,2560]{1,0:T(8,128)(2,1)S(1)}, u32[]{:S(2)}, u32[]{:S(2)}) collective-permute-start(bf16[64,2560]{1,0:T(8,128)(2,1)S(1)} %get-tuple-element.37), channel_id=1, source_target_pairs={{0,16},{2,18},{4,20},{6,22},{8,24},{10,26},{12,28},{14,30},{16,0},... | collective-permute-start | bytes 983048 | tf_op jit(solution)/shard_map/ppermute | solution.py:375
  160.1 17.2 %collective-permute-start.24 = (bf16[64,2560]{1,0:T(8,128)(2,1)S(1)}, bf16[64,2560]{1,0:T(8,128)(2,1)S(1)}, u32[]{:S(2)}, u32[]{:S(2)}) collective-permute-start(bf16[64,2560]{1,0:T(8,128)(2,1)S(1)} %get-tuple-element.44), channel_id=1, source_target_pairs={{0,24},{2,26},{4,28},{6,30},{8,0},{10,2},{12,4},{14,6},{16,8},{18,... | collective-permute-start | bytes 983048 | tf_op jit(solution)/shard_map/ppermute | solution.py:375
  162.6 17.7 %collective-permute-start.25 = (bf16[64,2560]{1,0:T(8,128)(2,1)S(1)}, bf16[64,2560]{1,0:T(8,128)(2,1)S(1)}, u32[]{:S(2)}, u32[]{:S(2)}) collective-permute-start(bf16[64,2560]{1,0:T(8,128)(2,1)S(1)} %get-tuple-element.43), channel_id=1, source_target_pairs={{0,8},{2,10},{4,12},{6,14},{8,16},{10,18},{12,20},{14,22},{16,24},... | collective-permute-start | bytes 983048 | tf_op jit(solution)/shard_map/ppermute | solution.py:375
